TPU v7x, 512 devices: a whole 4x4x16 slice. The times are simulated.
512 devices in a mesh: gy: 32 (over z_lo, y), gx: 4 (over x), gz: 4 (over z_hi, core).
Axes of the slice: x: 4, y: 4, z: 16 (z_hi: 2, z_lo: 8; z = z_hi * 8 + z_lo), core: 2. Of those that a mesh axis runs over, the one named last changes fastest.
Arguments:
- wall: bfloat16 [3, 1024, 768], P(None, ('gy', 'gx'), 'gz'), may hold values from -6 to 6
- kernel: bfloat16 [2, 3, 3, 32, 768, 1024], P(None, None, None, 'gy', 'gz', 'gx'), may hold values from -3 to 3
Outputs:
- estimate: bfloat16 [3, 32, 768, 1024], P(None, 'gy', 'gz', 'gx')
All inputs are finite; a program needn't handle non-finite values.
Results may differ from a plain program's by a relative error of at most 0.025.
Values may be sent and summed in bfloat16 or wider, within the bound.
No kernel may reach another device: no remote copies, remote signals or barrier semaphores. Data moves between devices by JAX's collectives and lax.ppermute only.
A program may use at most 64 MiB of HBM per device.

v0:
```python
import math

import jax
import jax.numpy as jnp
from jax import lax
from jax.sharding import PartitionSpec as P

NX = 1024
NZ = 768


def split_pair(values):
    upper_part = values.astype(jnp.bfloat16)
    lower_part = (values - upper_part.astype(jnp.float32)).astype(jnp.bfloat16)
    return (upper_part, lower_part)


def twiddle(left_index, right_index, length):
    phase_index = left_index[:, None] * right_index[None, :] % length
    angles = phase_index.astype(jnp.float32) * (2.0 * math.pi / length)
    factor = 1.0 / math.sqrt(length)
    return (split_pair(jnp.cos(angles) * factor), split_pair(jnp.sin(angles) * factor))


def apply_right(values, pair):
    flattened = values.reshape(-1, values.shape[-1])
    result = jnp.dot(flattened, pair[0], preferred_element_type=jnp.float32)
    result = result + jnp.dot(flattened, pair[1], preferred_element_type=jnp.float32)
    return result.reshape(values.shape[:-1] + (pair[0].shape[1],))


def apply_left(pair, values):
    result = jnp.dot(pair[0], values, preferred_element_type=jnp.float32)
    return result + jnp.dot(pair[1], values, preferred_element_type=jnp.float32)


def apply_middle(values, pair):
    result = jnp.einsum("abkw,kx->abxw", values, pair[0], preferred_element_type=jnp.float32)
    return result + jnp.einsum("abkw,kx->abxw", values, pair[1], preferred_element_type=jnp.float32)


def per_device(wall, kernel):
    components, rows_local, cols_local = wall.shape
    modes_z = kernel.shape[4]
    modes_x = kernel.shape[5]
    span_z = lax.axis_index("gz") * modes_z + jnp.arange(modes_z, dtype=jnp.int32)
    span_x = lax.axis_index("gx") * modes_x + jnp.arange(modes_x, dtype=jnp.int32)
    zero_block = jnp.zeros((components * rows_local, modes_z), jnp.float32)
    block_piece = lax.all_gather(wall, "gz", axis=2, tiled=True)
    amount = block_piece.shape[2]
    places = jnp.arange(amount, dtype=jnp.int32)
    cos_pair, sin_pair = twiddle(places, span_z, NZ)
    flattened = block_piece.reshape(-1, amount)
    z_real = apply_right(flattened, cos_pair)
    z_imag = (zero_block, zero_block)[1] - apply_right(flattened, sin_pair)

    def to_rows(values):
        shaped = values.astype(jnp.bfloat16).reshape(components, rows_local, modes_z)
        return jnp.transpose(shaped, (1, 0, 2)).reshape(rows_local, components * modes_z)

    row_real = to_rows(z_real)
    row_imag = to_rows(z_imag)
    pieces = (
        lax.all_gather(row_real, ("gy", "gx"), axis=0, tiled=True),
        lax.all_gather(row_imag, ("gy", "gx"), axis=0, tiled=True),
    )
    amount = pieces[0].shape[0]
    places = jnp.arange(amount, dtype=jnp.int32)
    cos_pair, sin_pair = twiddle(span_x, places, NX)
    real_sum = apply_left(cos_pair, pieces[0]) + apply_left(sin_pair, pieces[1])
    imag_sum = apply_left(cos_pair, pieces[1]) - apply_left(sin_pair, pieces[0])

    def to_modes(values):
        shaped = lax.optimization_barrier(values.astype(jnp.bfloat16)).astype(jnp.float32)
        return jnp.transpose(shaped.reshape(modes_x, components, modes_z), (1, 2, 0))

    wall_real = to_modes(real_sum)[None, :, None]
    wall_imag = to_modes(imag_sum)[None, :, None]
    kernel_real = kernel[0].astype(jnp.float32)
    kernel_imag = kernel[1].astype(jnp.float32)
    mode_real = jnp.sum(kernel_real * wall_real - kernel_imag * wall_imag, axis=1).astype(
        jnp.bfloat16
    )
    mode_imag = jnp.sum(kernel_real * wall_imag + kernel_imag * wall_real, axis=1).astype(
        jnp.bfloat16
    )
    pieces = (
        lax.all_to_all(mode_real, "gz", split_axis=3, concat_axis=2, tiled=True),
        lax.all_to_all(mode_imag, "gz", split_axis=3, concat_axis=2, tiled=True),
    )
    full_z = jnp.arange(NZ, dtype=jnp.int32)
    cos_pair, sin_pair = twiddle(full_z, full_z, NZ)
    inner_real = (apply_middle(pieces[0], cos_pair) - apply_middle(pieces[1], sin_pair)).astype(
        jnp.bfloat16
    )
    inner_imag = (apply_middle(pieces[0], sin_pair) + apply_middle(pieces[1], cos_pair)).astype(
        jnp.bfloat16
    )
    column_real = lax.all_to_all(inner_real, "gz", split_axis=2, concat_axis=3, tiled=True)
    column_imag = lax.all_to_all(inner_imag, "gz", split_axis=2, concat_axis=3, tiled=True)
    pieces = (
        lax.all_to_all(column_real, "gx", split_axis=2, concat_axis=3, tiled=True),
        lax.all_to_all(column_imag, "gx", split_axis=2, concat_axis=3, tiled=True),
    )
    full_x = jnp.arange(NX, dtype=jnp.int32)
    cos_pair, sin_pair = twiddle(full_x, full_x, NX)
    plane_values = (apply_right(pieces[0], cos_pair) - apply_right(pieces[1], sin_pair)).astype(
        jnp.bfloat16
    )
    return lax.all_to_all(plane_values, "gx", split_axis=3, concat_axis=2, tiled=True)


def solution(mesh):
    return jax.shard_map(
        per_device,
        mesh=mesh,
        in_specs=(P(None, ("gy", "gx"), "gz"), P(None, None, None, "gy", "gz", "gx")),
        out_specs=P(None, "gy", "gz", "gx"),
        check_vma=False,
    )
```

profile of v0, /device:TPU:1, one launch (start us, length us, event | category | flops | bytes accessed | tf_op | source)
XLA Modules:
  0.0 2249.7 jit_solution(1259711877255137506)
XLA Ops:
  6.5 0.9 copy.50
  7.4 22.9 %all_gather.9 = bf16[3,8,768]{1,0,2:T(4,128)(2,1)S(1)} all-gather(bf16[3,8,192]{1,0,2:T(4,128)(2,1)S(1)} %copy.50), channel_id=1, replica_groups=mesh['gy'=32,'gx'=4,'gz'=4] {'gz'}, dimensions={2}, use_global_device_ids=true | all-gather | bytes 46080 | tf_op jit(solution)/shard_map/all_gather | solution.py:49
  30.7 3.3 fusion.79
  34.0 3.3 fusion.53
  38.1 3.3 fusion.77
  41.4 3.5 fusion.52
  45.6 874.6 %all-gather.3.cloned.1.call-done = bf16[1024,576]{1,0:T(8,128)(2,1)} async-done(((bf16[8,576]{1,0:T(8,128)(2,1)}), bf16[1024,576]{1,0:T(8,128)(2,1)}) %all-gather.3.cloned.1.call-update) | async-done | bytes 1179664 | tf_op jit(solution)/shard_map/all_gather | solution.py:64
  920.2 5.8 fusion.75
  926.0 4.4 convolution_add_fusion.3
  930.5 944.0 %all-gather.5.cloned.1.call-done = bf16[1024,576]{1,0:T(8,128)(2,1)} async-done(((bf16[8,576]{1,0:T(8,128)(2,1)}), bf16[1024,576]{1,0:T(8,128)(2,1)}) %all-gather.5.cloned.1.call-update) | async-done | bytes 1179664 | tf_op jit(solution)/shard_map/all_gather | solution.py:65
  1874.4 6.2 fusion.71
  1880.7 5.1 fusion.35
  1885.8 4.4 fusion.73
  1890.2 4.4 fusion.69
  1894.6 4.6 convolution_add_fusion.1
  1899.2 5.1 fusion.36
  1904.4 1.4 copy-done
  1906.3 1.1 copy.54
  1907.4 97.1 %all-to-all-start = ((bf16[3,1,192,256]{2,0,1,3:T(4,128)(2,1)}), bf16[3,1,192,256]{2,0,1,3:T(4,128)(2,1)S(1)}, u32[]{:S(2)}, u32[]{:S(2)}) async-start(bf16[3,1,192,256]{2,0,1,3:T(4,128)(2,1)} %copy.54), calls=%async_computation | async-start | bytes 1048576 | tf_op jit(solution)/shard_map/all_to_all | solution.py:88
  2004.5 1.1 copy.57
  2005.5 15.7 all-to-all-done
  2021.2 4.5 all-to-all-start.1
  2026.4 9.6 fusion.39
  2036.0 10.9 fusion.48
  2047.6 9.5 fusion.43
  2057.1 9.8 fusion.46
  2066.9 9.5 fusion.41
  2076.4 9.6 fusion.45
  2086.8 1.2 reshape.234
  2088.0 12.4 all-to-all-start.4
  2100.4 9.6 fusion.37
  2110.0 9.7 fusion.47
  2120.4 1.2 reshape.232
  2121.6 12.0 all-to-all-start.2
  2134.7 1.0 copy.67
  2135.7 12.2 all-to-all-done.2
  2147.9 3.5 all-to-all-start.5
  2152.4 1.0 copy.62
  2153.4 4.9 all-to-all-done.5
  2158.3 3.6 all-to-all-start.3
  2162.2 16.2 fusion.8
  2178.6 16.1 fusion.10
  2194.8 16.4 fusion.33
  2211.2 17.1 fusion.34
  2229.1 1.2 reshape.236
  2230.3 9.7 all_to_all.114
  2240.0 1.4 reshape.237
  2241.4 1.2 copy.71
  (44 shorter events, 8.6 us)
Async XLA Ops:
  6.5 913.7 %all-gather.3.cloned.1.call-start = ((), (), s32[]{:S(2)}) async-start(), calls=%async_computation.7 | async-start | bytes 1320960 | tf_op jit(solution)/shard_map/all_gather | solution.py:64
  38.0 1836.4 %all-gather.5.cloned.1.call-start = ((), (), s32[]{:S(2)}) async-start(), calls=%async_computation.8 | async-start | bytes 1320960 | tf_op jit(solution)/shard_map/all_gather | solution.py:65
  920.2 5.8 copy-start.2
  1874.4 6.3 copy-start.3
  1904.2 1.5 copy-start
  1907.4 113.8 %all-to-all-start = ((bf16[3,1,192,256]{2,0,1,3:T(4,128)(2,1)}), bf16[3,1,192,256]{2,0,1,3:T(4,128)(2,1)S(1)}, u32[]{:S(2)}, u32[]{:S(2)}) async-start(bf16[3,1,192,256]{2,0,1,3:T(4,128)(2,1)} %copy.54), calls=%async_computation | async-start | bytes 1048576 | tf_op jit(solution)/shard_map/all_to_all | solution.py:88
  2021.2 25.7 %all-to-all-start.1 = ((bf16[3,1,192,256]{2,0,1,3:T(4,128)(2,1)}), bf16[3,1,192,256]{2,0,1,3:T(4,128)(2,1)S(1)}, u32[]{:S(2)}, u32[]{:S(2)}) async-start(bf16[3,1,192,256]{2,0,1,3:T(4,128)(2,1)} %copy.57), calls=%async_computation.1 | async-start | bytes 1048576 | tf_op jit(solution)/shard_map/all_to_all | solution.py:89
  2076.4 9.6 copy-start.1
  2088.0 33.6 %all-to-all-start.4 = ((bf16[4,2,18432]{2,1,0:T(2,128)(2,1)}), bf16[4,2,18432]{2,1,0:T(2,128)(2,1)S(1)}, u32[]{:S(2)}, u32[]{:S(2)}) async-start(bf16[4,2,18432]{2,1,0:T(2,128)(2,1)} %reshape.234), calls=%async_computation.4 | async-start | bytes 589824 | tf_op jit(solution)/shard_map/all_to_all | solution.py:100
  2121.6 26.2 %all-to-all-start.2 = ((bf16[4,2,18432]{2,1,0:T(2,128)(2,1)}), bf16[4,2,18432]{2,1,0:T(2,128)(2,1)S(1)}, u32[]{:S(2)}, u32[]{:S(2)}) async-start(bf16[4,2,18432]{2,1,0:T(2,128)(2,1)} %reshape.232), calls=%async_computation.2 | async-start | bytes 589824 | tf_op jit(solution)/shard_map/all_to_all | solution.py:99
  2147.9 10.4 all-to-all-start.5
  2158.3 20.1 all-to-all-start.3
Sparse Core Ops, SparseCore 0:
  38.1 882.0 all-gather.2
  922.3 952.0 all-gather.4
where the time goes:
time: 2260 us; the launch traced here: 2250 us
  waiting for transfers between devices  1850 us (82%)
  matrix products  197 us (9%)
  starting transfers between devices  133 us (6%)
  blocking collectives  32.6 us (1%)
    all_gather x1, waiting for transfers between devices, per_device(): lax.all_gather(row_imag, ('gy', 'gx'), axis=0, tiled=True)  944 us
    all_gather x1, waiting for transfers between devices, per_device(): lax.all_gather(row_real, ('gy', 'gx'), axis=0, tiled=True)  875 us
    all_to_all x1, starting transfers between devices, per_device(): lax.all_to_all(mode_real, 'gz', split_axis=3, concat_axis=2, tiled=True)  97.1 us
    unnamed x8, matrix products  78.1 us
  transfers between devices with their start and end apart: 8, of which 5 were waited for; matrix products, arithmetic and copies ran while one was open for 4% of the time, Pallas kernels for 0%

commit v1 on v0

v1 whole, which is shorter than its diff:
```python
import functools
import math

import jax
import jax.numpy as jnp
import numpy as np
from jax import lax
from jax.experimental import pallas as pl
from jax.experimental.pallas import tpu as pltpu
from jax.sharding import Mesh, PartitionSpec as P

NX = 1024
NZ = 768
NQ = 192
NP = 256
VMEM = 40 * 1024 * 1024


def angle(left, right, length):
    phase = (left[:, None].astype(np.int64) * right[None, :].astype(np.int64)) % length
    return phase * (2.0 * math.pi / length)


def forward_z_table():
    q = np.arange(NQ)
    theta = angle(q, q, NZ)
    both = np.stack([np.cos(theta), np.sin(theta)])
    main, tail = both[..., :128], both[..., 128:]
    zero = np.zeros_like(tail)
    return np.concatenate([tail, zero, main, zero, tail], axis=-1).astype(jnp.bfloat16)


def forward_x_table():
    y, source, low, r = np.meshgrid(
        np.arange(4), np.arange(4), np.arange(8), np.arange(8), indexing="ij"
    )
    x = (8 * (4 * (low * 4 + y) + source) + r).reshape(-1)
    theta = angle(x, np.arange(NP), NX).reshape(16, 64, NP)
    cos, sin = np.cos(theta), np.sin(theta)
    from_real = np.concatenate([cos, -sin], axis=2)
    from_imag = np.concatenate([sin, cos], axis=2)
    both = np.concatenate([from_real, from_imag], axis=1)
    return both.reshape(8, 256, 512).astype(jnp.bfloat16)


def inverse_x_table():
    theta = angle(np.arange(NX), np.arange(NX), NX).reshape(NX, 8, 128)
    both = np.concatenate([np.cos(theta), np.sin(theta)], axis=2)
    return np.transpose(both, (1, 0, 2)).astype(jnp.bfloat16)


def inverse_z_table():
    q = (
        48 * np.arange(4)[:, None, None]
        + 192 * np.arange(2)[None, :, None]
        + np.arange(48)[None, None, :]
    ).reshape(-1)
    theta = angle(np.arange(NZ), q, NZ).reshape(NZ, 8, 48)
    both = np.stack([np.cos(theta), -np.sin(theta)], axis=2)
    return both.reshape(4, NQ, NZ).astype(jnp.bfloat16)


def pack_body(wall_ref, table_ref, out_ref, kept_ref):
    kept_ref[...] = table_ref[...]
    rows = [wall_ref[c].astype(jnp.float32) for c in range(3)]
    tails = [row[:, 128:] for row in rows] + [jnp.zeros((8, 64), jnp.float32)]
    pieces = [row[:, :128] for row in rows]
    for c in range(0, 4, 2):
        pieces.append(jnp.concatenate(tails[c : c + 2], axis=1))
    packed = jnp.concatenate(pieces, axis=0).astype(jnp.bfloat16)
    for k in range(16):
        out_ref[k] = packed


def pack_call(wall, table):
    return pl.pallas_call(
        pack_body,
        out_shape=[
            jax.ShapeDtypeStruct((16, 40, 128), jnp.bfloat16),
            jax.ShapeDtypeStruct((2, NQ, 384), jnp.bfloat16),
        ],
        compiler_params=pltpu.CompilerParams(vmem_limit_bytes=VMEM),
        cost_estimate=pl.CostEstimate(flops=10000, bytes_accessed=180000, transcendentals=0),
        name="pack",
    )(wall, table)


def turned_lanes(values, turn):
    lane = lax.broadcasted_iota(jnp.int32, values.shape, 1)
    keep = jnp.where(turn == 0, 1.0, jnp.where(turn == 2, -1.0, 0.0))
    swap = jnp.where(turn == 1, 1.0, jnp.where(turn == 3, -1.0, 0.0))
    swap = jnp.where(lane < 64, swap, -swap)
    return values * keep + pltpu.roll(values, 64, axis=1) * swap


def partial_z(me, rows_ref, table_ref, step, c):
    turn = (me * lax.broadcasted_iota(jnp.int32, (64, 256), 1)) % 4
    to_real = jnp.where(turn == 0, 1.0, jnp.where(turn == 2, -1.0, 0.0))
    to_imag = jnp.where(turn == 3, 1.0, jnp.where(turn == 1, -1.0, 0.0))
    row = lax.broadcasted_iota(jnp.int32, (NQ, 128), 0)
    core = me % 2
    result = None
    for high in range(2):
        position = high * 2 + (core if step == 0 else 1 - core)
        blocks = [rows_ref[low * 2 + high].astype(jnp.float32) for low in range(8)]
        main = jnp.concatenate([block[c * 8 : c * 8 + 8] for block in blocks], axis=0)
        start = 24 + (c // 2) * 8
        tail = jnp.concatenate([block[start : start + 8] for block in blocks], axis=0)
        both = [main, tail] if c == 1 else [tail, main]
        rows = jnp.concatenate(both, axis=1)
        real = rows * to_real
        imag = rows * to_imag
        by_cos = jnp.concatenate([real, imag], axis=0).astype(jnp.bfloat16)
        by_sin = jnp.concatenate([imag, -real], axis=0).astype(jnp.bfloat16)
        lanes = slice(128, 384) if c == 1 else slice(0, 256)
        total = jnp.zeros((NQ, 128), jnp.float32)
        for part, values in enumerate((by_cos, by_sin)):
            total = total + lax.dot_general(
                table_ref[part, :, lanes],
                values,
                (((1,), (1,)), ((), ())),
                preferred_element_type=jnp.float32,
            )
        total = turned_lanes(total, (position * row) % 4)
        result = total if result is None else result + total
    return result


def forward_z_own_body(me_ref, rows_ref, table_ref, out_ref):
    for c in range(3):
        out_ref[c] = partial_z(me_ref[0], rows_ref, table_ref, 0, c)


def forward_z_body(me_ref, rows_ref, table_ref, own_ref, out_ref):
    lane = lax.broadcasted_iota(jnp.int32, (NQ, 128), 1)
    for c in range(3):
        total = own_ref[c] + partial_z(me_ref[0], rows_ref, table_ref, 1, c)
        total = total * (1.0 / math.sqrt(NZ))
        for x in range(4):
            turned = turned_lanes(total, (x * lane) % 4).astype(jnp.bfloat16)
            for y in range(4):
                out_ref[y * 4 + x, c * 48 : c * 48 + 48, :] = turned[y * 48 : y * 48 + 48]


def forward_z_call(me, rows, table, own):
    rows_spec = pl.BlockSpec((16, 40, 128), lambda j, s: (0, 0, 0))
    table_spec = pl.BlockSpec((2, NQ, 384), lambda j, s: (0, 0, 0))
    own_spec = pl.BlockSpec((3, NQ, 128), lambda j, s: (0, 0, 0))
    out_spec = pl.BlockSpec((16, 144, 128), lambda j, s: (0, 0, 0))
    first = own is None
    return pl.pallas_call(
        forward_z_own_body if first else forward_z_body,
        grid_spec=pltpu.PrefetchScalarGridSpec(
            num_scalar_prefetch=1,
            grid=(1,),
            in_specs=[rows_spec, table_spec] + ([] if first else [own_spec]),
            out_specs=own_spec if first else out_spec,
        ),
        out_shape=jax.ShapeDtypeStruct((3, NQ, 128), jnp.float32)
        if first
        else jax.ShapeDtypeStruct((16, 144, 128), jnp.bfloat16),
        compiler_params=pltpu.CompilerParams(vmem_limit_bytes=VMEM),
        cost_estimate=pl.CostEstimate(flops=151000000, bytes_accessed=1700000, transcendentals=0),
        name="forward_z_own" if first else "forward_z",
    )(me, rows, table, *([] if first else [own]))


def forward_x_body(values_ref, table_ref, out_ref):
    total = jnp.zeros((144, 512), jnp.float32)
    for k in range(8):
        pair = jnp.concatenate([values_ref[2 * k], values_ref[2 * k + 1]], axis=1)
        total = total + jnp.dot(pair, table_ref[k], preferred_element_type=jnp.float32)
    total = (total * (1.0 / 32.0)).astype(jnp.bfloat16)
    for y in range(4):
        out_ref[y] = total


def forward_x_call(values, table):
    return pl.pallas_call(
        forward_x_body,
        out_shape=jax.ShapeDtypeStruct((4, 144, 512), jnp.bfloat16),
        compiler_params=pltpu.CompilerParams(vmem_limit_bytes=VMEM),
        cost_estimate=pl.CostEstimate(flops=302000000, bytes_accessed=3300000, transcendentals=0),
        name="forward_x",
    )(values, table)


def modes_body(kernel_ref, spec_ref, out_ref):
    spec = [spec_ref[0, c * 48 : c * 48 + 48, :].astype(jnp.float32) for c in range(3)]
    for o in range(3):
        real = None
        imag = None
        for c in range(3):
            kr = kernel_ref[0, o, c, 0].astype(jnp.float32)
            ki = kernel_ref[1, o, c, 0].astype(jnp.float32)
            sr = spec[c][:, :NP]
            si = spec[c][:, NP:]
            r = kr * sr - ki * si
            i = kr * si + ki * sr
            real = r if real is None else real + r
            imag = i if imag is None else imag + i
        out_ref[0, o * 48 : o * 48 + 48, :] = real.astype(jnp.bfloat16)
        out_ref[0, 144 + o * 48 : 192 + o * 48, :] = imag.astype(jnp.bfloat16)


def modes_call(kernel, spec):
    return pl.pallas_call(
        modes_body,
        grid=(4,),
        in_specs=[
            pl.BlockSpec((2, 3, 3, 1, 48, NP), lambda j: (0, 0, 0, 0, j, 0)),
            pl.BlockSpec((1, 144, 512), lambda j: (j, 0, 0)),
        ],
        out_specs=pl.BlockSpec((1, 288, NP), lambda j: (j, 0, 0)),
        out_shape=jax.ShapeDtypeStruct((4, 288, NP), jnp.bfloat16),
        compiler_params=pltpu.CompilerParams(vmem_limit_bytes=VMEM),
        cost_estimate=pl.CostEstimate(flops=3600000, bytes_accessed=2950000, transcendentals=0),
        name="modes",
    )(kernel, spec)


def inverse_x_body(values_ref, table_ref, out_ref):
    values = jnp.concatenate([values_ref[s] for s in range(4)], axis=1)

    def block(j, carry):
        total = jnp.dot(values, table_ref[j], preferred_element_type=jnp.float32)
        total = total * (1.0 / 32.0)
        real = (total[:144, :128] - total[144:, 128:]).astype(jnp.bfloat16)
        imag = (total[:144, 128:] + total[144:, :128]).astype(jnp.bfloat16)
        for o in range(3):
            out_ref[j, 0:48, o * 128 : (o + 1) * 128] = real[o * 48 : (o + 1) * 48]
            out_ref[j, 48:96, o * 128 : (o + 1) * 128] = imag[o * 48 : (o + 1) * 48]
        return carry

    lax.fori_loop(0, 8, block, 0, unroll=True)


def inverse_x_call(values, table):
    return pl.pallas_call(
        inverse_x_body,
        out_shape=jax.ShapeDtypeStruct((8, 96, 384), jnp.bfloat16),
        compiler_params=pltpu.CompilerParams(vmem_limit_bytes=VMEM),
        cost_estimate=pl.CostEstimate(flops=1208000000, bytes_accessed=5400000, transcendentals=0),
        name="inverse_x",
    )(values, table)


def inverse_z_body(steps, me_ref, values_ref, table_ref, *out_refs):
    me = me_ref[0]
    values = values_ref[...]
    odd = (lax.broadcasted_iota(jnp.int32, (NQ, 384), 0) * (me // 2)) % 2
    scale = jnp.where(odd == 1, -1.0, 1.0) * (1.0 / math.sqrt(NZ))
    for k, out_ref in zip(steps, out_refs):
        total = jnp.dot(table_ref[me ^ k], values, preferred_element_type=jnp.float32)
        out_ref[...] = (total * scale).astype(out_ref.dtype)


def inverse_z_call(me, values, table, steps):
    block = pl.BlockSpec((NQ, 384), lambda j, s: (0, 0))
    return pl.pallas_call(
        functools.partial(inverse_z_body, steps),
        grid_spec=pltpu.PrefetchScalarGridSpec(
            num_scalar_prefetch=1,
            grid=(1,),
            in_specs=[
                pl.BlockSpec((NZ, 384), lambda j, s: (0, 0)),
                pl.BlockSpec((4, NQ, NZ), lambda j, s: (0, 0, 0)),
            ],
            out_specs=[block] * 2,
        ),
        out_shape=[jax.ShapeDtypeStruct((NQ, 384), jnp.bfloat16) for _ in range(2)],
        compiler_params=pltpu.CompilerParams(vmem_limit_bytes=VMEM),
        cost_estimate=pl.CostEstimate(flops=227000000, bytes_accessed=2000000, transcendentals=0),
        name="inverse_z_far" if steps[0] else "inverse_z_near",
    )(me, values, table)


def finish_body(core_ref, own_ref, far_own_ref, near_ref, far_near_ref, out_ref):
    own = own_ref[...].astype(jnp.float32) + far_own_ref[...].astype(jnp.float32)
    near = near_ref[...].astype(jnp.float32) + far_near_ref[...].astype(jnp.float32)
    first = core_ref[0] == 0
    left = jnp.where(first, own, near).astype(jnp.bfloat16)
    right = jnp.where(first, near, own).astype(jnp.bfloat16)
    for o in range(3):
        out_ref[o, 0, :, 0:128] = left[:, o * 128 : (o + 1) * 128]
        out_ref[o, 0, :, 128:256] = right[:, o * 128 : (o + 1) * 128]


def finish_call(core, own, far_own, near, far_near):
    block = pl.BlockSpec((NQ, 384), lambda j, s: (0, 0))
    return pl.pallas_call(
        finish_body,
        grid_spec=pltpu.PrefetchScalarGridSpec(
            num_scalar_prefetch=1,
            grid=(1,),
            in_specs=[block] * 4,
            out_specs=pl.BlockSpec((3, 1, NQ, NP), lambda j, s: (0, 0, 0, 0)),
        ),
        out_shape=jax.ShapeDtypeStruct((3, 1, NQ, NP), jnp.bfloat16),
        compiler_params=pltpu.CompilerParams(vmem_limit_bytes=VMEM),
        cost_estimate=pl.CostEstimate(flops=150000, bytes_accessed=900000, transcendentals=0),
        name="finish",
    )(core, own, far_own, near, far_near)


def exchange(values, axis):
    return lax.all_to_all(values, axis, split_axis=0, concat_axis=0, tiled=True)


def swap_cores(values):
    return lax.ppermute(values, "core", [(0, 1), (1, 0)])


def move_z(values, step, flip):
    def position(z, core):
        return (z % 8) * 4 + (z // 8) * 2 + core

    perm = []
    for z in range(16):
        for core in range(2):
            target = (z + (step if core == 0 else -step)) % 16
            perm.append((position(z, core), position(target, core ^ flip)))
    return lax.ppermute(values, ("z_lo", "z_hi", "core"), perm)


def per_device(wall, kernel):
    core = lax.axis_index("core")
    gz = (lax.axis_index("z_hi") * 2 + core).reshape(1).astype(jnp.int32)

    rows, z_table = pack_call(wall, jnp.asarray(forward_z_table()))
    rows = exchange(rows, ("z_lo", "z_hi"))
    other = swap_cores(rows)
    z_spectra = forward_z_call(gz, other, z_table, forward_z_call(gz, rows, z_table, None))
    z_spectra = exchange(z_spectra, ("y", "gx"))
    spec = exchange(forward_x_call(z_spectra, jnp.asarray(forward_x_table())), "y")

    modes = exchange(modes_call(kernel, spec), "gx")
    planes = exchange(inverse_x_call(modes, jnp.asarray(inverse_x_table())), ("gx", "core"))
    planes = planes.reshape(NZ, 384)
    z_table = jnp.asarray(inverse_z_table())
    to_far, to_far_near = inverse_z_call(gz, planes, z_table, (2, 3))
    own, to_near = inverse_z_call(gz, planes, z_table, (0, 1))
    far_own = move_z(move_z(to_far, 4, 0), 4, 0)
    far_near = move_z(move_z(to_far_near, 4, 0), 4, 1)
    near = swap_cores(to_near)
    return finish_call(core.reshape(1).astype(jnp.int32), own, far_own, near, far_near)


def solution(mesh):
    fine = Mesh(mesh.devices.reshape(8, 4, 4, 2, 2), ("z_lo", "y", "gx", "z_hi", "core"))
    return jax.shard_map(
        per_device,
        mesh=fine,
        in_specs=(
            P(None, ("z_lo", "y", "gx"), ("z_hi", "core")),
            P(None, None, None, ("z_lo", "y"), ("z_hi", "core"), "gx"),
        ),
        out_specs=P(None, ("z_lo", "y"), ("z_hi", "core"), "gx"),
        check_vma=False,
    )
```

time: 2260 us -> 133 us (0.06)
  waiting for transfers between devices: 1850 us -> 19.4 us
  matrix products: 197 us -> 0 us
  starting transfers between devices: 133 us -> 18.4 us
  blocking collectives: 32.6 us -> 85.2 us
    all_gather x2 -> x0, waiting for transfers between devices: 1820 us -> none  [the longest x1 944 us: per_device(): lax.all_gather(row_imag, ('gy', 'gx'), axis=0, tiled=True)]
    all_to_all x6 -> x0, starting transfers between devices: 133 us -> none  [the longest x1 97.1 us: per_device(): lax.all_to_all(mode_real, 'gz', split_axis=3, concat_axis=2, tiled=True)]
    dot_general x16 -> x0, matrix products: 119 us -> none  [the longest x4 40.4 us: apply_right(): jnp.dot(flattened, pair[1], preferred_element_type=jnp.float32)]
    unnamed x8 -> x0, matrix products: 78.1 us -> none
    all_to_all x1 -> x5, blocking collectives: 9.72 us -> 85.2 us  [exchange(): return lax.all_to_all(values, axis, split_axis=0, concat_axis=0, tiled=True)]
    all_to_all x6 -> x0, waiting for transfers between devices: 32.8 us -> none  [the longest x1 15.7 us: per_device(): lax.all_to_all(mode_real, 'gz', split_axis=3, concat_axis=2, tiled=True)]
    all_gather x1 -> x0, blocking collectives: 22.9 us -> none  [per_device(): block_piece = lax.all_gather(wall, 'gz', axis=2, tiled=True)]
  transfers between devices with their start and end apart: 8 -> 6, of which waited for: 5 -> 5; matrix products, arithmetic and copies ran while one was open for 4% -> 0% of each run, Pallas kernels for 0% -> 1%
where the time goes in v1:
time: 133 us; the launch traced here: 131 us
  blocking collectives  85.2 us (64%)
  waiting for transfers between devices  19.4 us (15%)
  starting transfers between devices  18.4 us (14%)
  Pallas kernels  5.9 us (4%)
  local copies, waits for them, and re-layouts  1.83 us (1%)
    all_to_all x5, blocking collectives, exchange(): return lax.all_to_all(values, axis, split_axis=0, concat_axis=0, tiled=True)  85.2 us
    ppermute x4, waiting for transfers between devices, move_z(): return lax.ppermute(values, ('z_lo', 'z_hi', 'core'), perm)  19 us
    ppermute x4, starting transfers between devices, move_z(): return lax.ppermute(values, ('z_lo', 'z_hi', 'core'), perm)  10.2 us
    ppermute x2, starting transfers between devices, swap_cores(): return lax.ppermute(values, 'core', [(0, 1), (1, 0)])  8.18 us
  transfers between devices with their start and end apart: 6, of which 5 were waited for; matrix products, arithmetic and copies ran while one was open for 0% of the time, Pallas kernels for 1%

profile of v1, /device:TPU:1, one launch (start us, length us, event | category | flops | bytes accessed | tf_op | source)
XLA Modules:
  0.0 130.9 jit_solution(12608122993504204399)
XLA Ops:
  0.0 0.0 copy-start.2
  0.0 0.0 copy-start.4
  0.0 1.1 copy-done.4
  1.1 0.0 copy-start.5
  1.1 0.7 copy-done.5
  1.8 0.1 pack.1
  1.9 29.6 %all_to_all.25.rows_ref = bf16[16,40,128]{2,1,0:T(8,128)(2,1)S(1)} all-to-all(bf16[16,40,128]{2,1,0:T(8,128)(2,1)S(1)} %get-tuple-element.11), channel_id=1, replica_groups=mesh['z_lo'=8,'y'=4,'gx'=4,'z_hi'=2,'core'=2] {'z_lo','z_hi'}, dimensions={0} | all-to-all | bytes 327680 | tf_op jit(solution)/shard_map/all_to_all | solution.py:307
  31.6 5.3 %collective-permute-start = (bf16[16,40,128]{2,1,0:T(8,128)(2,1)S(1)}, bf16[16,40,128]{2,1,0:T(8,128)(2,1)S(1)}, u32[]{:S(2)}, u32[]{:S(2)}) collective-permute-start(bf16[16,40,128]{2,1,0:T(8,128)(2,1)S(1)} %all_to_all.25.rows_ref), channel_id=1, source_target_pairs={{0,1},{1,0},{2,3},{3,2},{4,5},{5,4},{6,7},{7,6},{8,9},{9,8},{10,11... | collective-permute-start | bytes 491528 | tf_op jit(solution)/shard_map/ppermute | solution.py:311
  36.9 0.6 forward_z_own.1.own_ref
  37.5 0.4 collective-permute-done.rows_ref
  37.9 0.7 forward_z.1
  38.6 18.0 %all_to_all.26.values_ref = bf16[16,144,128]{2,1,0:T(8,128)(2,1)S(1)} all-to-all(bf16[16,144,128]{2,1,0:T(8,128)(2,1)S(1)} %forward_z.1), channel_id=1, replica_groups=mesh['z_lo'=8,'y'=4,'gx'=4,'z_hi'=2,'core'=2] {'y','gx'}, dimensions={0} | all-to-all | bytes 1179648 | tf_op jit(solution)/shard_map/all_to_all | solution.py:307
  56.6 0.0 copy-done.2
  56.6 0.0 copy-start.3
  56.6 0.5 forward_x.1
  57.1 0.0 copy-start.1
  57.1 10.8 %all_to_all.27.spec_ref = bf16[4,144,512]{2,1,0:T(8,128)(2,1)S(1)} all-to-all(bf16[4,144,512]{2,1,0:T(8,128)(2,1)S(1)} %forward_x.1), channel_id=1, replica_groups=mesh['z_lo'=8,'y'=4,'gx'=4,'z_hi'=2,'core'=2] {'y'}, dimensions={0} | all-to-all | bytes 1179648 | tf_op jit(solution)/shard_map/all_to_all | solution.py:307
  67.9 0.0 copy-done.3
  67.9 0.9 modes.1
  68.8 9.8 %all_to_all.28.values_ref = bf16[4,288,256]{2,1,0:T(8,128)(2,1)S(1)} all-to-all(bf16[4,288,256]{2,1,0:T(8,128)(2,1)S(1)} %modes.1), channel_id=1, replica_groups=mesh['z_lo'=8,'y'=4,'gx'=4,'z_hi'=2,'core'=2] {'gx'}, dimensions={0} | all-to-all | bytes 1179648 | tf_op jit(solution)/shard_map/all_to_all | solution.py:307
  78.6 0.0 copy-done.1
  78.6 0.0 copy-start
  78.6 1.4 %inverse_x.1 = bf16[8,96,384]{2,1,0:T(8,128)(2,1)S(1)} custom-call(bf16[4,288,256]{2,1,0:T(8,128)(2,1)S(1)} %all_to_all.28.values_ref, bf16[8,1024,256]{2,1,0:T(8,128)(2,1)S(1)} %copy-done.1), custom_call_target="tpu_custom_call" | custom-call | flops 1208000000 | bytes 5400000 | tf_op jit(solution)/shard_map/inverse_x/pallas_call | solution.py:239
  80.0 17.0 %all_to_all.29 = bf16[8,96,384]{2,1,0:T(8,128)(2,1)S(1)} all-to-all(bf16[8,96,384]{2,1,0:T(8,128)(2,1)S(1)} %inverse_x.1), channel_id=1, replica_groups=mesh['z_lo'=8,'y'=4,'gx'=4,'z_hi'=2,'core'=2] {'gx','core'}, dimensions={0} | all-to-all | bytes 1179648 | tf_op jit(solution)/shard_map/all_to_all | solution.py:307
  97.0 0.0 copy-done
  97.0 0.5 inverse_z_far.1
  97.4 3.4 %collective-permute-start.1 = (bf16[192,384]{1,0:T(8,128)(2,1)S(1)}, bf16[192,384]{1,0:T(8,128)(2,1)S(1)}, u32[]{:S(2)}, u32[]{:S(2)}) collective-permute-start(bf16[192,384]{1,0:T(8,128)(2,1)S(1)} %get-tuple-element.14), channel_id=1, source_target_pairs={{0,256},{1,259},{64,320},{65,323},{128,384},{129,387},{192,448},{1... | collective-permute-start | bytes 442376 | tf_op jit(solution)/shard_map/ppermute | solution.py:323
  100.8 1.9 %collective-permute-start.4 = (bf16[192,384]{1,0:T(8,128)(2,1)S(1)}, bf16[192,384]{1,0:T(8,128)(2,1)S(1)}, u32[]{:S(2)}, u32[]{:S(2)}) collective-permute-start(bf16[192,384]{1,0:T(8,128)(2,1)S(1)} %get-tuple-element.16), channel_id=1, source_target_pairs={{0,256},{1,259},{64,320},{65,323},{128,384},{129,387},{192,448},{1... | collective-permute-start | bytes 442376 | tf_op jit(solution)/shard_map/ppermute | solution.py:323
  102.7 0.5 inverse_z_near.1
  103.2 2.8 %collective-permute-start.3 = (bf16[192,384]{1,0:T(8,128)(2,1)S(1)}, bf16[192,384]{1,0:T(8,128)(2,1)S(1)}, u32[]{:S(2)}, u32[]{:S(2)}) collective-permute-start(bf16[192,384]{1,0:T(8,128)(2,1)S(1)} %get-tuple-element.15), channel_id=1, source_target_pairs={{0,1},{1,0},{2,3},{3,2},{4,5},{5,4},{6,7},{7,6},{8,9},{9,8},{10,11... | collective-permute-start | bytes 442376 | tf_op jit(solution)/shard_map/ppermute | solution.py:311
  106.0 8.1 %collective-permute-done.1 = bf16[192,384]{1,0:T(8,128)(2,1)S(1)} collective-permute-done((bf16[192,384]{1,0:T(8,128)(2,1)S(1)}, bf16[192,384]{1,0:T(8,128)(2,1)S(1)}, u32[]{:S(2)}, u32[]{:S(2)}) %collective-permute-start.1) | collective-permute-done | bytes 147488 | tf_op jit(solution)/shard_map/ppermute | solution.py:323
  114.2 3.0 %collective-permute-start.2 = (bf16[192,384]{1,0:T(8,128)(2,1)S(1)}, bf16[192,384]{1,0:T(8,128)(2,1)S(1)}, u32[]{:S(2)}, u32[]{:S(2)}) collective-permute-start(bf16[192,384]{1,0:T(8,128)(2,1)S(1)} %collective-permute-done.1), channel_id=1, source_target_pairs={{0,256},{1,259},{64,320},{65,323},{128,384},{129,387},{192,448},{1... | collective-permute-start | bytes 442376 | tf_op jit(solution)/shard_map/ppermute | solution.py:323
  117.2 1.9 %collective-permute-done.4 = bf16[192,384]{1,0:T(8,128)(2,1)S(1)} collective-permute-done((bf16[192,384]{1,0:T(8,128)(2,1)S(1)}, bf16[192,384]{1,0:T(8,128)(2,1)S(1)}, u32[]{:S(2)}, u32[]{:S(2)}) %collective-permute-start.4) | collective-permute-done | bytes 147488 | tf_op jit(solution)/shard_map/ppermute | solution.py:323
  119.1 1.9 %collective-permute-start.5 = (bf16[192,384]{1,0:T(8,128)(2,1)S(1)}, bf16[192,384]{1,0:T(8,128)(2,1)S(1)}, u32[]{:S(2)}, u32[]{:S(2)}) collective-permute-start(bf16[192,384]{1,0:T(8,128)(2,1)S(1)} %collective-permute-done.4), channel_id=1, source_target_pairs={{0,257},{1,258},{64,321},{65,322},{128,385},{129,386},{192,449},{1... | collective-permute-start | bytes 442376 | tf_op jit(solution)/shard_map/ppermute | solution.py:323
  121.1 0.0 collective-permute-done.3.near_ref
  121.1 5.7 %collective-permute-done.2.far_own_ref = bf16[192,384]{1,0:T(8,128)(2,1)S(1)} collective-permute-done((bf16[192,384]{1,0:T(8,128)(2,1)S(1)}, bf16[192,384]{1,0:T(8,128)(2,1)S(1)}, u32[]{:S(2)}, u32[]{:S(2)}) %collective-permute-start.2) | collective-permute-done | bytes 147488 | tf_op jit(solution)/shard_map/ppermute | solution.py:323
  126.8 3.3 %collective-permute-done.5.far_near_ref = bf16[192,384]{1,0:T(8,128)(2,1)S(1)} collective-permute-done((bf16[192,384]{1,0:T(8,128)(2,1)S(1)}, bf16[192,384]{1,0:T(8,128)(2,1)S(1)}, u32[]{:S(2)}, u32[]{:S(2)}) %collective-permute-start.5) | collective-permute-done | bytes 147488 | tf_op jit(solution)/shard_map/ppermute | solution.py:323
  130.1 0.8 finish.1
Async XLA Ops:
  0.0 56.6 %copy-start.2 = (bf16[8,256,512]{2,1,0:T(8,128)(2,1)S(1)}, bf16[8,256,512]{2,1,0:T(8,128)(2,1)}, u32[]{:S(2)}) copy-start(bf16[8,256,512]{2,1,0:T(8,128)(2,1)} %constant.17.clone.table_ref) | copy-start | bytes 6291460
  0.0 1.1 copy-start.4
  1.1 0.7 copy-start.5
  31.6 6.3 %collective-permute-start = (bf16[16,40,128]{2,1,0:T(8,128)(2,1)S(1)}, bf16[16,40,128]{2,1,0:T(8,128)(2,1)S(1)}, u32[]{:S(2)}, u32[]{:S(2)}) collective-permute-start(bf16[16,40,128]{2,1,0:T(8,128)(2,1)S(1)} %all_to_all.25.rows_ref), channel_id=1, source_target_pairs={{0,1},{1,0},{2,3},{3,2},{4,5},{5,4},{6,7},{7,6},{8,9},{9,8},{10,11... | collective-permute-start | bytes 491528 | tf_op jit(solution)/shard_map/ppermute | solution.py:311
  56.6 11.3 %copy-start.3 = (bf16[2,3,3,1,192,256]{5,4,3,2,1,0:T(8,128)(2,1)S(1)}, bf16[2,3,3,1,192,256]{5,4,3,2,1,0:T(8,128)(2,1)}, u32[]{:S(2)}) copy-start(bf16[2,3,3,1,192,256]{5,4,3,2,1,0:T(8,128)(2,1)} %kernel_ref.1) | copy-start | bytes 5308420
  57.1 21.5 %copy-start.1 = (bf16[8,1024,256]{2,1,0:T(8,128)(2,1)S(1)}, bf16[8,1024,256]{2,1,0:T(8,128)(2,1)}, u32[]{:S(2)}) copy-start(bf16[8,1024,256]{2,1,0:T(8,128)(2,1)} %constant.18.clone.table_ref) | copy-start | bytes 12582916
  78.6 18.4 %copy-start = (bf16[4,192,768]{2,1,0:T(8,128)(2,1)S(1)}, bf16[4,192,768]{2,1,0:T(8,128)(2,1)}, u32[]{:S(2)}) copy-start(bf16[4,192,768]{2,1,0:T(8,128)(2,1)} %constant.19.clone.table_ref) | copy-start | bytes 3538948
  97.4 16.8 %collective-permute-start.1 = (bf16[192,384]{1,0:T(8,128)(2,1)S(1)}, bf16[192,384]{1,0:T(8,128)(2,1)S(1)}, u32[]{:S(2)}, u32[]{:S(2)}) collective-permute-start(bf16[192,384]{1,0:T(8,128)(2,1)S(1)} %get-tuple-element.14), channel_id=1, source_target_pairs={{0,256},{1,259},{64,320},{65,323},{128,384},{129,387},{192,448},{1... | collective-permute-start | bytes 442376 | tf_op jit(solution)/shard_map/ppermute | solution.py:323
  100.8 18.3 %collective-permute-start.4 = (bf16[192,384]{1,0:T(8,128)(2,1)S(1)}, bf16[192,384]{1,0:T(8,128)(2,1)S(1)}, u32[]{:S(2)}, u32[]{:S(2)}) collective-permute-start(bf16[192,384]{1,0:T(8,128)(2,1)S(1)} %get-tuple-element.16), channel_id=1, source_target_pairs={{0,256},{1,259},{64,320},{65,323},{128,384},{129,387},{192,448},{1... | collective-permute-start | bytes 442376 | tf_op jit(solution)/shard_map/ppermute | solution.py:323
  103.2 17.9 %collective-permute-start.3 = (bf16[192,384]{1,0:T(8,128)(2,1)S(1)}, bf16[192,384]{1,0:T(8,128)(2,1)S(1)}, u32[]{:S(2)}, u32[]{:S(2)}) collective-permute-start(bf16[192,384]{1,0:T(8,128)(2,1)S(1)} %get-tuple-element.15), channel_id=1, source_target_pairs={{0,1},{1,0},{2,3},{3,2},{4,5},{5,4},{6,7},{7,6},{8,9},{9,8},{10,11... | collective-permute-start | bytes 442376 | tf_op jit(solution)/shard_map/ppermute | solution.py:311
  114.2 12.6 %collective-permute-start.2 = (bf16[192,384]{1,0:T(8,128)(2,1)S(1)}, bf16[192,384]{1,0:T(8,128)(2,1)S(1)}, u32[]{:S(2)}, u32[]{:S(2)}) collective-permute-start(bf16[192,384]{1,0:T(8,128)(2,1)S(1)} %collective-permute-done.1), channel_id=1, source_target_pairs={{0,256},{1,259},{64,320},{65,323},{128,384},{129,387},{192,448},{1... | collective-permute-start | bytes 442376 | tf_op jit(solution)/shard_map/ppermute | solution.py:323
  119.1 11.0 %collective-permute-start.5 = (bf16[192,384]{1,0:T(8,128)(2,1)S(1)}, bf16[192,384]{1,0:T(8,128)(2,1)S(1)}, u32[]{:S(2)}, u32[]{:S(2)}) collective-permute-start(bf16[192,384]{1,0:T(8,128)(2,1)S(1)} %collective-permute-done.4), channel_id=1, source_target_pairs={{0,257},{1,258},{64,321},{65,322},{128,385},{129,386},{192,449},{1... | collective-permute-start | bytes 442376 | tf_op jit(solution)/shard_map/ppermute | solution.py:323

commit v2 on v1

--- a/solution.py
+++ b/solution.py
@@ -60,8 +60,12 @@
     return both.reshape(4, NQ, NZ).astype(jnp.bfloat16)
 
 
-def pack_body(wall_ref, table_ref, out_ref, kept_ref):
-    kept_ref[...] = table_ref[...]
+def pack_body(wall_hbm, table_hbm, out_ref, kept_ref, wall_ref, sems):
+    wall_copy = pltpu.make_async_copy(wall_hbm, wall_ref, sems.at[0])
+    table_copy = pltpu.make_async_copy(table_hbm, kept_ref, sems.at[1])
+    wall_copy.start()
+    table_copy.start()
+    wall_copy.wait()
     rows = [wall_ref[c].astype(jnp.float32) for c in range(3)]
     tails = [row[:, 128:] for row in rows] + [jnp.zeros((8, 64), jnp.float32)]
     pieces = [row[:, :128] for row in rows]
@@ -70,11 +74,14 @@
     packed = jnp.concatenate(pieces, axis=0).astype(jnp.bfloat16)
     for k in range(16):
         out_ref[k] = packed
+    table_copy.wait()
 
 
 def pack_call(wall, table):
     return pl.pallas_call(
         pack_body,
+        in_specs=[pl.BlockSpec(memory_space=pltpu.HBM)] * 2,
+        scratch_shapes=[pltpu.VMEM((3, 8, NQ), jnp.bfloat16), pltpu.SemaphoreType.DMA((2,))],
         out_shape=[
             jax.ShapeDtypeStruct((16, 40, 128), jnp.bfloat16),
             jax.ShapeDtypeStruct((2, NQ, 384), jnp.bfloat16),
@@ -82,7 +89,10 @@
         compiler_params=pltpu.CompilerParams(vmem_limit_bytes=VMEM),
         cost_estimate=pl.CostEstimate(flops=10000, bytes_accessed=180000, transcendentals=0),
         name="pack",
-    )(wall, table)
+    )(
+        pltpu.with_memory_space_constraint(wall, pltpu.HBM),
+        pltpu.with_memory_space_constraint(table, pltpu.HBM),
+    )
 
 
 def turned_lanes(values, turn):
@@ -133,20 +143,26 @@
 
 def forward_z_body(me_ref, rows_ref, table_ref, own_ref, out_ref):
     lane = lax.broadcasted_iota(jnp.int32, (NQ, 128), 1)
+    totals = []
     for c in range(3):
         total = own_ref[c] + partial_z(me_ref[0], rows_ref, table_ref, 1, c)
-        total = total * (1.0 / math.sqrt(NZ))
-        for x in range(4):
-            turned = turned_lanes(total, (x * lane) % 4).astype(jnp.bfloat16)
-            for y in range(4):
-                out_ref[y * 4 + x, c * 48 : c * 48 + 48, :] = turned[y * 48 : y * 48 + 48]
+        totals.append(total * (1.0 / math.sqrt(NZ)))
+    for pair in range(2):
+        if pair:
+            totals = [jnp.where(lane % 2 == 1, -total, total) for total in totals]
+        for y in range(4):
+            for half in range(2):
+                start = y * 48 + half * 24
+                pieces = [total[start : start + 24] for total in totals]
+                block = jnp.concatenate(pieces, axis=0).astype(jnp.bfloat16)
+                out_ref[y * 4 + pair * 2 + half] = block
 
 
 def forward_z_call(me, rows, table, own):
     rows_spec = pl.BlockSpec((16, 40, 128), lambda j, s: (0, 0, 0))
     table_spec = pl.BlockSpec((2, NQ, 384), lambda j, s: (0, 0, 0))
     own_spec = pl.BlockSpec((3, NQ, 128), lambda j, s: (0, 0, 0))
-    out_spec = pl.BlockSpec((16, 144, 128), lambda j, s: (0, 0, 0))
+    out_spec = pl.BlockSpec((16, 72, 128), lambda j, s: (0, 0, 0))
     first = own is None
     return pl.pallas_call(
         forward_z_own_body if first else forward_z_body,
@@ -158,7 +174,7 @@
         ),
         out_shape=jax.ShapeDtypeStruct((3, NQ, 128), jnp.float32)
         if first
-        else jax.ShapeDtypeStruct((16, 144, 128), jnp.bfloat16),
+        else jax.ShapeDtypeStruct((16, 72, 128), jnp.bfloat16),
         compiler_params=pltpu.CompilerParams(vmem_limit_bytes=VMEM),
         cost_estimate=pl.CostEstimate(flops=151000000, bytes_accessed=1700000, transcendentals=0),
         name="forward_z_own" if first else "forward_z",
@@ -166,27 +182,37 @@
 
 
 def forward_x_body(values_ref, table_ref, out_ref):
+    turn = lax.broadcasted_iota(jnp.int32, (72, 128), 1) % 4
     total = jnp.zeros((144, 512), jnp.float32)
     for k in range(8):
-        pair = jnp.concatenate([values_ref[2 * k], values_ref[2 * k + 1]], axis=1)
-        total = total + jnp.dot(pair, table_ref[k], preferred_element_type=jnp.float32)
-    total = (total * (1.0 / 32.0)).astype(jnp.bfloat16)
-    for y in range(4):
-        out_ref[y] = total
+        first = [values_ref[2 * k + i].astype(jnp.float32) for i in range(2)]
+        second = [turned_lanes(value, turn) for value in first]
+        both = [jnp.concatenate(pieces, axis=1) for pieces in (first, second)]
+        both = jnp.concatenate(both, axis=0).astype(jnp.bfloat16)
+        total = total + jnp.dot(both, table_ref[k], preferred_element_type=jnp.float32)
+    total = total * (1.0 / 32.0)
+    for half in range(2):
+        block = total[half * 72 : half * 72 + 72].astype(jnp.bfloat16)
+        for y in range(4):
+            out_ref[y * 2 + half] = block
 
 
 def forward_x_call(values, table):
     return pl.pallas_call(
         forward_x_body,
-        out_shape=jax.ShapeDtypeStruct((4, 144, 512), jnp.bfloat16),
-        compiler_params=pltpu.CompilerParams(vmem_limit_bytes=VMEM),
-        cost_estimate=pl.CostEstimate(flops=302000000, bytes_accessed=3300000, transcendentals=0),
+        out_shape=jax.ShapeDtypeStruct((8, 72, 512), jnp.bfloat16),
+        compiler_params=pltpu.CompilerParams(vmem_limit_bytes=VMEM),
+        cost_estimate=pl.CostEstimate(flops=302000000, bytes_accessed=3000000, transcendentals=0),
         name="forward_x",
     )(values, table)
 
 
 def modes_body(kernel_ref, spec_ref, out_ref):
-    spec = [spec_ref[0, c * 48 : c * 48 + 48, :].astype(jnp.float32) for c in range(3)]
+    halves = [spec_ref[half].astype(jnp.float32) for half in range(2)]
+    spec = []
+    for c in range(3):
+        pieces = [half[c * 24 : c * 24 + 24] for half in halves]
+        spec.append(jnp.concatenate(pieces, axis=0))
     for o in range(3):
         real = None
         imag = None
@@ -209,7 +235,7 @@
         grid=(4,),
         in_specs=[
             pl.BlockSpec((2, 3, 3, 1, 48, NP), lambda j: (0, 0, 0, 0, j, 0)),
-            pl.BlockSpec((1, 144, 512), lambda j: (j, 0, 0)),
+            pl.BlockSpec((2, 72, 512), lambda j: (j, 0, 0)),
         ],
         out_specs=pl.BlockSpec((1, 288, NP), lambda j: (j, 0, 0)),
         out_shape=jax.ShapeDtypeStruct((4, 288, NP), jnp.bfloat16),
@@ -331,11 +357,11 @@
     rows = exchange(rows, ("z_lo", "z_hi"))
     other = swap_cores(rows)
     z_spectra = forward_z_call(gz, other, z_table, forward_z_call(gz, rows, z_table, None))
-    z_spectra = exchange(z_spectra, ("y", "gx"))
-    spec = exchange(forward_x_call(z_spectra, jnp.asarray(forward_x_table())), "y")
-
-    modes = exchange(modes_call(kernel, spec), "gx")
-    planes = exchange(inverse_x_call(modes, jnp.asarray(inverse_x_table())), ("gx", "core"))
+    z_spectra = exchange(z_spectra, ("y", "gx_pair", "gx_in"))
+    spec = exchange(forward_x_call(z_spectra, jnp.asarray(forward_x_table())), ("y", "gx_in"))
+
+    modes = exchange(modes_call(kernel, spec), ("gx_pair", "gx_in"))
+    planes = exchange(inverse_x_call(modes, jnp.asarray(inverse_x_table())), ("gx_pair", "gx_in", "core"))
     planes = planes.reshape(NZ, 384)
     z_table = jnp.asarray(inverse_z_table())
     to_far, to_far_near = inverse_z_call(gz, planes, z_table, (2, 3))
@@ -347,14 +373,18 @@
 
 
 def solution(mesh):
-    fine = Mesh(mesh.devices.reshape(8, 4, 4, 2, 2), ("z_lo", "y", "gx", "z_hi", "core"))
+    fine = Mesh(
+        mesh.devices.reshape(8, 4, 2, 2, 2, 2),
+        ("z_lo", "y", "gx_pair", "gx_in", "z_hi", "core"),
+    )
+    gx, gz = ("gx_pair", "gx_in"), ("z_hi", "core")
     return jax.shard_map(
         per_device,
         mesh=fine,
         in_specs=(
-            P(None, ("z_lo", "y", "gx"), ("z_hi", "core")),
-            P(None, None, None, ("z_lo", "y"), ("z_hi", "core"), "gx"),
+            P(None, ("z_lo", "y") + gx, gz),
+            P(None, None, None, ("z_lo", "y"), gz, gx),
         ),
-        out_specs=P(None, ("z_lo", "y"), ("z_hi", "core"), "gx"),
+        out_specs=P(None, ("z_lo", "y"), gz, gx),
         check_vma=False,
     )

time: 133 us -> 130 us (0.977)
  blocking collectives: 85.2 us -> 82.9 us
  local copies, waits for them, and re-layouts: 1.83 us -> 0.02 us
    all_to_all x5, blocking collectives: 85.2 us -> 82.9 us  [exchange(): return lax.all_to_all(values, axis, split_axis=0, concat_axis=0, tiled=True)]
    unnamed x12 -> x8, local copies, waits for them, and re-layouts: 1.83 us -> 0.02 us
where the time goes in v2:
time: 130 us; the launch traced here: 128 us
  blocking collectives  82.9 us (64%)
  starting transfers between devices  19.3 us (15%)
  waiting for transfers between devices  18.7 us (14%)
  Pallas kernels  6.89 us (5%)
    all_to_all x5, blocking collectives, exchange(): return lax.all_to_all(values, axis, split_axis=0, concat_axis=0, tiled=True)  82.9 us
    ppermute x4, waiting for transfers between devices, move_z(): return lax.ppermute(values, ('z_lo', 'z_hi', 'core'), perm)  18.2 us
    ppermute x4, starting transfers between devices, move_z(): return lax.ppermute(values, ('z_lo', 'z_hi', 'core'), perm)  11.1 us
    ppermute x2, starting transfers between devices, swap_cores(): return lax.ppermute(values, 'core', [(0, 1), (1, 0)])  8.17 us
  transfers between devices with their start and end apart: 6, of which 5 were waited for; matrix products, arithmetic and copies ran while one was open for 0% of the time, Pallas kernels for 1%

profile of v2, /device:TPU:1, one launch (start us, length us, event | category | flops | bytes accessed | tf_op | source)
XLA Modules:
  0.0 127.9 jit_solution(5603494605387907066)
XLA Ops:
  0.0 0.0 copy-start.2
  0.0 1.1 pack.1
  1.2 29.7 %all_to_all.25.rows_ref = bf16[16,40,128]{2,1,0:T(8,128)(2,1)S(1)} all-to-all(bf16[16,40,128]{2,1,0:T(8,128)(2,1)S(1)} %get-tuple-element.11), channel_id=1, replica_groups=mesh['z_lo'=8,'y'=4,'gx_pair'=2,'gx_in'=2,'z_hi'=2,'core'=2] {'z_lo','z_..., dimensions={0} | all-to-all | bytes 327680 | tf_op jit(solution)/shard_map/all_to_all | solution.py:333
  30.8 5.3 %collective-permute-start = (bf16[16,40,128]{2,1,0:T(8,128)(2,1)S(1)}, bf16[16,40,128]{2,1,0:T(8,128)(2,1)S(1)}, u32[]{:S(2)}, u32[]{:S(2)}) collective-permute-start(bf16[16,40,128]{2,1,0:T(8,128)(2,1)S(1)} %all_to_all.25.rows_ref), channel_id=1, source_target_pairs={{0,1},{1,0},{2,3},{3,2},{4,5},{5,4},{6,7},{7,6},{8,9},{9,8},{10,11... | collective-permute-start | bytes 491528 | tf_op jit(solution)/shard_map/ppermute | solution.py:337
  36.2 0.6 forward_z_own.1.own_ref
  36.7 0.4 collective-permute-done.rows_ref
  37.2 0.6 forward_z.1
  37.7 15.0 %all_to_all.26.values_ref = bf16[16,72,128]{2,1,0:T(8,128)(2,1)S(1)} all-to-all(bf16[16,72,128]{2,1,0:T(8,128)(2,1)S(1)} %forward_z.1), channel_id=1, replica_groups=mesh['z_lo'=8,'y'=4,'gx_pair'=2,'gx_in'=2,'z_hi'=2,'core'=2] {'y','gx_pa..., dimensions={0} | all-to-all | bytes 589824 | tf_op jit(solution)/shard_map/all_to_all | solution.py:333
  52.8 0.0 copy-done.2
  52.8 0.0 copy-start.3
  52.8 0.5 forward_x.1
  53.3 0.0 copy-start.1
  53.3 12.0 %all_to_all.27.spec_ref = bf16[8,72,512]{2,1,0:T(8,128)(2,1)S(1)} all-to-all(bf16[8,72,512]{2,1,0:T(8,128)(2,1)S(1)} %forward_x.1), channel_id=1, replica_groups=mesh['z_lo'=8,'y'=4,'gx_pair'=2,'gx_in'=2,'z_hi'=2,'core'=2] {'y','gx_in'}, dimensions={0} | all-to-all | bytes 1179648 | tf_op jit(solution)/shard_map/all_to_all | solution.py:333
  65.3 0.0 copy-done.3
  65.3 0.9 modes.1
  66.2 9.7 %all_to_all.28.values_ref = bf16[4,288,256]{2,1,0:T(8,128)(2,1)S(1)} all-to-all(bf16[4,288,256]{2,1,0:T(8,128)(2,1)S(1)} %modes.1), channel_id=1, replica_groups=mesh['z_lo'=8,'y'=4,'gx_pair'=2,'gx_in'=2,'z_hi'=2,'core'=2] {'gx_pair',..., dimensions={0} | all-to-all | bytes 1179648 | tf_op jit(solution)/shard_map/all_to_all | solution.py:333
  75.9 0.0 copy-done.1
  75.9 0.0 copy-start
  75.9 1.4 %inverse_x.1 = bf16[8,96,384]{2,1,0:T(8,128)(2,1)S(1)} custom-call(bf16[4,288,256]{2,1,0:T(8,128)(2,1)S(1)} %all_to_all.28.values_ref, bf16[8,1024,256]{2,1,0:T(8,128)(2,1)S(1)} %copy-done.1), custom_call_target="tpu_custom_call" | custom-call | flops 1208000000 | bytes 5400000 | tf_op jit(solution)/shard_map/inverse_x/pallas_call | solution.py:265
  77.4 16.5 %all_to_all.29 = bf16[8,96,384]{2,1,0:T(8,128)(2,1)S(1)} all-to-all(bf16[8,96,384]{2,1,0:T(8,128)(2,1)S(1)} %inverse_x.1), channel_id=1, replica_groups=mesh['z_lo'=8,'y'=4,'gx_pair'=2,'gx_in'=2,'z_hi'=2,'core'=2] {'gx_pair',..., dimensions={0} | all-to-all | bytes 1179648 | tf_op jit(solution)/shard_map/all_to_all | solution.py:333
  93.9 0.0 copy-done
  93.9 0.5 inverse_z_far.1
  94.3 3.4 %collective-permute-start.1 = (bf16[192,384]{1,0:T(8,128)(2,1)S(1)}, bf16[192,384]{1,0:T(8,128)(2,1)S(1)}, u32[]{:S(2)}, u32[]{:S(2)}) collective-permute-start(bf16[192,384]{1,0:T(8,128)(2,1)S(1)} %get-tuple-element.14), channel_id=1, source_target_pairs={{0,256},{1,259},{64,320},{65,323},{128,384},{129,387},{192,448},{1... | collective-permute-start | bytes 442376 | tf_op jit(solution)/shard_map/ppermute | solution.py:349
  97.7 1.9 %collective-permute-start.4 = (bf16[192,384]{1,0:T(8,128)(2,1)S(1)}, bf16[192,384]{1,0:T(8,128)(2,1)S(1)}, u32[]{:S(2)}, u32[]{:S(2)}) collective-permute-start(bf16[192,384]{1,0:T(8,128)(2,1)S(1)} %get-tuple-element.16), channel_id=1, source_target_pairs={{0,256},{1,259},{64,320},{65,323},{128,384},{129,387},{192,448},{1... | collective-permute-start | bytes 442376 | tf_op jit(solution)/shard_map/ppermute | solution.py:349
  99.6 0.5 inverse_z_near.1
  100.1 2.8 %collective-permute-start.3 = (bf16[192,384]{1,0:T(8,128)(2,1)S(1)}, bf16[192,384]{1,0:T(8,128)(2,1)S(1)}, u32[]{:S(2)}, u32[]{:S(2)}) collective-permute-start(bf16[192,384]{1,0:T(8,128)(2,1)S(1)} %get-tuple-element.15), channel_id=1, source_target_pairs={{0,1},{1,0},{2,3},{3,2},{4,5},{5,4},{6,7},{7,6},{8,9},{9,8},{10,11... | collective-permute-start | bytes 442376 | tf_op jit(solution)/shard_map/ppermute | solution.py:337
  103.0 8.1 %collective-permute-done.1 = bf16[192,384]{1,0:T(8,128)(2,1)S(1)} collective-permute-done((bf16[192,384]{1,0:T(8,128)(2,1)S(1)}, bf16[192,384]{1,0:T(8,128)(2,1)S(1)}, u32[]{:S(2)}, u32[]{:S(2)}) %collective-permute-start.1) | collective-permute-done | bytes 147488 | tf_op jit(solution)/shard_map/ppermute | solution.py:349
  111.1 3.0 %collective-permute-start.2 = (bf16[192,384]{1,0:T(8,128)(2,1)S(1)}, bf16[192,384]{1,0:T(8,128)(2,1)S(1)}, u32[]{:S(2)}, u32[]{:S(2)}) collective-permute-start(bf16[192,384]{1,0:T(8,128)(2,1)S(1)} %collective-permute-done.1), channel_id=1, source_target_pairs={{0,256},{1,259},{64,320},{65,323},{128,384},{129,387},{192,448},{1... | collective-permute-start | bytes 442376 | tf_op jit(solution)/shard_map/ppermute | solution.py:349
  114.1 0.9 collective-permute-done.4
  115.0 2.9 %collective-permute-start.5 = (bf16[192,384]{1,0:T(8,128)(2,1)S(1)}, bf16[192,384]{1,0:T(8,128)(2,1)S(1)}, u32[]{:S(2)}, u32[]{:S(2)}) collective-permute-start(bf16[192,384]{1,0:T(8,128)(2,1)S(1)} %collective-permute-done.4), channel_id=1, source_target_pairs={{0,257},{1,258},{64,321},{65,322},{128,385},{129,386},{192,449},{1... | collective-permute-start | bytes 442376 | tf_op jit(solution)/shard_map/ppermute | solution.py:349
  117.9 0.0 collective-permute-done.3.near_ref
  117.9 6.0 %collective-permute-done.2.far_own_ref = bf16[192,384]{1,0:T(8,128)(2,1)S(1)} collective-permute-done((bf16[192,384]{1,0:T(8,128)(2,1)S(1)}, bf16[192,384]{1,0:T(8,128)(2,1)S(1)}, u32[]{:S(2)}, u32[]{:S(2)}) %collective-permute-start.2) | collective-permute-done | bytes 147488 | tf_op jit(solution)/shard_map/ppermute | solution.py:349
  123.9 3.2 %collective-permute-done.5.far_near_ref = bf16[192,384]{1,0:T(8,128)(2,1)S(1)} collective-permute-done((bf16[192,384]{1,0:T(8,128)(2,1)S(1)}, bf16[192,384]{1,0:T(8,128)(2,1)S(1)}, u32[]{:S(2)}, u32[]{:S(2)}) %collective-permute-start.5) | collective-permute-done | bytes 147488 | tf_op jit(solution)/shard_map/ppermute | solution.py:349
  127.1 0.8 finish.1
Async XLA Ops:
  0.0 52.8 %copy-start.2 = (bf16[8,256,512]{2,1,0:T(8,128)(2,1)S(1)}, bf16[8,256,512]{2,1,0:T(8,128)(2,1)}, u32[]{:S(2)}) copy-start(bf16[8,256,512]{2,1,0:T(8,128)(2,1)} %constant.17.clone.table_ref) | copy-start | bytes 6291460
  30.8 6.3 %collective-permute-start = (bf16[16,40,128]{2,1,0:T(8,128)(2,1)S(1)}, bf16[16,40,128]{2,1,0:T(8,128)(2,1)S(1)}, u32[]{:S(2)}, u32[]{:S(2)}) collective-permute-start(bf16[16,40,128]{2,1,0:T(8,128)(2,1)S(1)} %all_to_all.25.rows_ref), channel_id=1, source_target_pairs={{0,1},{1,0},{2,3},{3,2},{4,5},{5,4},{6,7},{7,6},{8,9},{9,8},{10,11... | collective-permute-start | bytes 491528 | tf_op jit(solution)/shard_map/ppermute | solution.py:337
  52.8 12.5 %copy-start.3 = (bf16[2,3,3,1,192,256]{5,4,3,2,1,0:T(8,128)(2,1)S(1)}, bf16[2,3,3,1,192,256]{5,4,3,2,1,0:T(8,128)(2,1)}, u32[]{:S(2)}) copy-start(bf16[2,3,3,1,192,256]{5,4,3,2,1,0:T(8,128)(2,1)} %kernel_ref.1) | copy-start | bytes 5308420
  53.3 22.6 %copy-start.1 = (bf16[8,1024,256]{2,1,0:T(8,128)(2,1)S(1)}, bf16[8,1024,256]{2,1,0:T(8,128)(2,1)}, u32[]{:S(2)}) copy-start(bf16[8,1024,256]{2,1,0:T(8,128)(2,1)} %constant.18.clone.table_ref) | copy-start | bytes 12582916
  75.9 17.9 %copy-start = (bf16[4,192,768]{2,1,0:T(8,128)(2,1)S(1)}, bf16[4,192,768]{2,1,0:T(8,128)(2,1)}, u32[]{:S(2)}) copy-start(bf16[4,192,768]{2,1,0:T(8,128)(2,1)} %constant.19.clone.table_ref) | copy-start | bytes 3538948
  94.3 16.8 %collective-permute-start.1 = (bf16[192,384]{1,0:T(8,128)(2,1)S(1)}, bf16[192,384]{1,0:T(8,128)(2,1)S(1)}, u32[]{:S(2)}, u32[]{:S(2)}) collective-permute-start(bf16[192,384]{1,0:T(8,128)(2,1)S(1)} %get-tuple-element.14), channel_id=1, source_target_pairs={{0,256},{1,259},{64,320},{65,323},{128,384},{129,387},{192,448},{1... | collective-permute-start | bytes 442376 | tf_op jit(solution)/shard_map/ppermute | solution.py:349
  97.7 17.3 %collective-permute-start.4 = (bf16[192,384]{1,0:T(8,128)(2,1)S(1)}, bf16[192,384]{1,0:T(8,128)(2,1)S(1)}, u32[]{:S(2)}, u32[]{:S(2)}) collective-permute-start(bf16[192,384]{1,0:T(8,128)(2,1)S(1)} %get-tuple-element.16), channel_id=1, source_target_pairs={{0,256},{1,259},{64,320},{65,323},{128,384},{129,387},{192,448},{1... | collective-permute-start | bytes 442376 | tf_op jit(solution)/shard_map/ppermute | solution.py:349
  100.1 17.8 %collective-permute-start.3 = (bf16[192,384]{1,0:T(8,128)(2,1)S(1)}, bf16[192,384]{1,0:T(8,128)(2,1)S(1)}, u32[]{:S(2)}, u32[]{:S(2)}) collective-permute-start(bf16[192,384]{1,0:T(8,128)(2,1)S(1)} %get-tuple-element.15), channel_id=1, source_target_pairs={{0,1},{1,0},{2,3},{3,2},{4,5},{5,4},{6,7},{7,6},{8,9},{9,8},{10,11... | collective-permute-start | bytes 442376 | tf_op jit(solution)/shard_map/ppermute | solution.py:337
  111.1 12.8 %collective-permute-start.2 = (bf16[192,384]{1,0:T(8,128)(2,1)S(1)}, bf16[192,384]{1,0:T(8,128)(2,1)S(1)}, u32[]{:S(2)}, u32[]{:S(2)}) collective-permute-start(bf16[192,384]{1,0:T(8,128)(2,1)S(1)} %collective-permute-done.1), channel_id=1, source_target_pairs={{0,256},{1,259},{64,320},{65,323},{128,384},{129,387},{192,448},{1... | collective-permute-start | bytes 442376 | tf_op jit(solution)/shard_map/ppermute | solution.py:349
  115.0 12.1 %collective-permute-start.5 = (bf16[192,384]{1,0:T(8,128)(2,1)S(1)}, bf16[192,384]{1,0:T(8,128)(2,1)S(1)}, u32[]{:S(2)}, u32[]{:S(2)}) collective-permute-start(bf16[192,384]{1,0:T(8,128)(2,1)S(1)} %collective-permute-done.4), channel_id=1, source_target_pairs={{0,257},{1,258},{64,321},{65,322},{128,385},{129,386},{192,449},{1... | collective-permute-start | bytes 442376 | tf_op jit(solution)/shard_map/ppermute | solution.py:349

commit v3 on v2

--- a/solution.py
+++ b/solution.py
@@ -366,8 +366,11 @@
     z_table = jnp.asarray(inverse_z_table())
     to_far, to_far_near = inverse_z_call(gz, planes, z_table, (2, 3))
     own, to_near = inverse_z_call(gz, planes, z_table, (0, 1))
-    far_own = move_z(move_z(to_far, 4, 0), 4, 0)
-    far_near = move_z(move_z(to_far_near, 4, 0), 4, 1)
+    half_own = move_z(to_far, 4, 0)
+    half_near = move_z(to_far_near, 4, 0)
+    half_own, to_near = lax.optimization_barrier((half_own, to_near))
+    far_own = move_z(half_own, 4, 0)
+    far_near = move_z(half_near, 4, 1)
     near = swap_cores(to_near)
     return finish_call(core.reshape(1).astype(jnp.int32), own, far_own, near, far_near)
 

time: 130 us -> 133 us (1.023); the launches traced: 128 us -> 133 us
  waiting for transfers between devices: 18.7 us -> 25.2 us
  starting transfers between devices: 19.3 us -> 17.4 us
    ppermute x4, waiting for transfers between devices: 18.2 us -> 24.8 us  [move_z(): return lax.ppermute(values, ('z_lo', 'z_hi', 'core'), perm)]
where the time goes in v3:
time: 133 us
  blocking collectives  82.9 us (62%)
  waiting for transfers between devices  25.2 us (19%)
  starting transfers between devices  17.4 us (13%)
  Pallas kernels  6.89 us (5%)
    all_to_all x5, blocking collectives, exchange(): return lax.all_to_all(values, axis, split_axis=0, concat_axis=0, tiled=True)  82.9 us
    ppermute x4, waiting for transfers between devices, move_z(): return lax.ppermute(values, ('z_lo', 'z_hi', 'core'), perm)  24.8 us
    ppermute x4, starting transfers between devices, move_z(): return lax.ppermute(values, ('z_lo', 'z_hi', 'core'), perm)  10.1 us
    ppermute x2, starting transfers between devices, swap_cores(): return lax.ppermute(values, 'core', [(0, 1), (1, 0)])  7.26 us
  transfers between devices with their start and end apart: 6, of which 5 were waited for; matrix products, arithmetic and copies ran while one was open for 0% of the time, Pallas kernels for 1%

profile of v3, /device:TPU:1, one launch (start us, length us, event | category | flops | bytes accessed | tf_op | source)
XLA Modules:
  0.0 132.5 jit_solution(4704712582546373492)
XLA Ops:
  0.0 0.0 copy-start.2
  0.0 1.1 pack.1
  1.2 29.7 %all_to_all.25.rows_ref = bf16[16,40,128]{2,1,0:T(8,128)(2,1)S(1)} all-to-all(bf16[16,40,128]{2,1,0:T(8,128)(2,1)S(1)} %get-tuple-element.13), channel_id=1, replica_groups=mesh['z_lo'=8,'y'=4,'gx_pair'=2,'gx_in'=2,'z_hi'=2,'core'=2] {'z_lo','z_..., dimensions={0} | all-to-all | bytes 327680 | tf_op jit(solution)/shard_map/all_to_all | solution.py:333
  30.8 5.3 %collective-permute-start = (bf16[16,40,128]{2,1,0:T(8,128)(2,1)S(1)}, bf16[16,40,128]{2,1,0:T(8,128)(2,1)S(1)}, u32[]{:S(2)}, u32[]{:S(2)}) collective-permute-start(bf16[16,40,128]{2,1,0:T(8,128)(2,1)S(1)} %all_to_all.25.rows_ref), channel_id=1, source_target_pairs={{0,1},{1,0},{2,3},{3,2},{4,5},{5,4},{6,7},{7,6},{8,9},{9,8},{10,11... | collective-permute-start | bytes 491528 | tf_op jit(solution)/shard_map/ppermute | solution.py:337
  36.2 0.6 forward_z_own.1.own_ref
  36.7 0.4 collective-permute-done.rows_ref
  37.2 0.6 forward_z.1
  37.7 15.0 %all_to_all.26.values_ref = bf16[16,72,128]{2,1,0:T(8,128)(2,1)S(1)} all-to-all(bf16[16,72,128]{2,1,0:T(8,128)(2,1)S(1)} %forward_z.1), channel_id=1, replica_groups=mesh['z_lo'=8,'y'=4,'gx_pair'=2,'gx_in'=2,'z_hi'=2,'core'=2] {'y','gx_pa..., dimensions={0} | all-to-all | bytes 589824 | tf_op jit(solution)/shard_map/all_to_all | solution.py:333
  52.8 0.0 copy-done.2
  52.8 0.0 copy-start.3
  52.8 0.5 forward_x.1
  53.3 0.0 copy-start.1
  53.3 12.0 %all_to_all.27.spec_ref = bf16[8,72,512]{2,1,0:T(8,128)(2,1)S(1)} all-to-all(bf16[8,72,512]{2,1,0:T(8,128)(2,1)S(1)} %forward_x.1), channel_id=1, replica_groups=mesh['z_lo'=8,'y'=4,'gx_pair'=2,'gx_in'=2,'z_hi'=2,'core'=2] {'y','gx_in'}, dimensions={0} | all-to-all | bytes 1179648 | tf_op jit(solution)/shard_map/all_to_all | solution.py:333
  65.3 0.0 copy-done.3
  65.3 0.9 modes.1
  66.2 9.7 %all_to_all.28.values_ref = bf16[4,288,256]{2,1,0:T(8,128)(2,1)S(1)} all-to-all(bf16[4,288,256]{2,1,0:T(8,128)(2,1)S(1)} %modes.1), channel_id=1, replica_groups=mesh['z_lo'=8,'y'=4,'gx_pair'=2,'gx_in'=2,'z_hi'=2,'core'=2] {'gx_pair',..., dimensions={0} | all-to-all | bytes 1179648 | tf_op jit(solution)/shard_map/all_to_all | solution.py:333
  75.9 0.0 copy-done.1
  75.9 0.0 copy-start
  75.9 1.4 %inverse_x.1 = bf16[8,96,384]{2,1,0:T(8,128)(2,1)S(1)} custom-call(bf16[4,288,256]{2,1,0:T(8,128)(2,1)S(1)} %all_to_all.28.values_ref, bf16[8,1024,256]{2,1,0:T(8,128)(2,1)S(1)} %copy-done.1), custom_call_target="tpu_custom_call" | custom-call | flops 1208000000 | bytes 5400000 | tf_op jit(solution)/shard_map/inverse_x/pallas_call | solution.py:265
  77.4 16.5 %all_to_all.29 = bf16[8,96,384]{2,1,0:T(8,128)(2,1)S(1)} all-to-all(bf16[8,96,384]{2,1,0:T(8,128)(2,1)S(1)} %inverse_x.1), channel_id=1, replica_groups=mesh['z_lo'=8,'y'=4,'gx_pair'=2,'gx_in'=2,'z_hi'=2,'core'=2] {'gx_pair',..., dimensions={0} | all-to-all | bytes 1179648 | tf_op jit(solution)/shard_map/all_to_all | solution.py:333
  93.9 0.0 copy-done
  93.9 0.5 inverse_z_far.1
  94.3 3.4 %collective-permute-start.1 = (bf16[192,384]{1,0:T(8,128)(2,1)S(1)}, bf16[192,384]{1,0:T(8,128)(2,1)S(1)}, u32[]{:S(2)}, u32[]{:S(2)}) collective-permute-start(bf16[192,384]{1,0:T(8,128)(2,1)S(1)} %get-tuple-element.16), channel_id=1, source_target_pairs={{0,256},{1,259},{64,320},{65,323},{128,384},{129,387},{192,448},{1... | collective-permute-start | bytes 442376 | tf_op jit(solution)/shard_map/ppermute | solution.py:349
  97.7 1.9 %collective-permute-start.4 = (bf16[192,384]{1,0:T(8,128)(2,1)S(1)}, bf16[192,384]{1,0:T(8,128)(2,1)S(1)}, u32[]{:S(2)}, u32[]{:S(2)}) collective-permute-start(bf16[192,384]{1,0:T(8,128)(2,1)S(1)} %get-tuple-element.20), channel_id=1, source_target_pairs={{0,256},{1,259},{64,320},{65,323},{128,384},{129,387},{192,448},{1... | collective-permute-start | bytes 442376 | tf_op jit(solution)/shard_map/ppermute | solution.py:349
  99.6 0.5 inverse_z_near.1
  100.1 11.0 %collective-permute-done.1 = bf16[192,384]{1,0:T(8,128)(2,1)S(1)} collective-permute-done((bf16[192,384]{1,0:T(8,128)(2,1)S(1)}, bf16[192,384]{1,0:T(8,128)(2,1)S(1)}, u32[]{:S(2)}, u32[]{:S(2)}) %collective-permute-start.1) | collective-permute-done | bytes 147488 | tf_op jit(solution)/shard_map/ppermute | solution.py:349
  111.1 3.0 %collective-permute-start.2 = (bf16[192,384]{1,0:T(8,128)(2,1)S(1)}, bf16[192,384]{1,0:T(8,128)(2,1)S(1)}, u32[]{:S(2)}, u32[]{:S(2)}) collective-permute-start(bf16[192,384]{1,0:T(8,128)(2,1)S(1)} %collective-permute-done.1), channel_id=1, source_target_pairs={{0,256},{1,259},{64,320},{65,323},{128,384},{129,387},{192,448},{1... | collective-permute-start | bytes 442376 | tf_op jit(solution)/shard_map/ppermute | solution.py:349
  114.1 1.9 %collective-permute-start.3 = (bf16[192,384]{1,0:T(8,128)(2,1)S(1)}, bf16[192,384]{1,0:T(8,128)(2,1)S(1)}, u32[]{:S(2)}, u32[]{:S(2)}) collective-permute-start(bf16[192,384]{1,0:T(8,128)(2,1)S(1)} %get-tuple-element.19), channel_id=1, source_target_pairs={{0,1},{1,0},{2,3},{3,2},{4,5},{5,4},{6,7},{7,6},{8,9},{9,8},{10,11... | collective-permute-start | bytes 442376 | tf_op jit(solution)/shard_map/ppermute | solution.py:337
  116.0 3.0 %collective-permute-done.4 = bf16[192,384]{1,0:T(8,128)(2,1)S(1)} collective-permute-done((bf16[192,384]{1,0:T(8,128)(2,1)S(1)}, bf16[192,384]{1,0:T(8,128)(2,1)S(1)}, u32[]{:S(2)}, u32[]{:S(2)}) %collective-permute-start.4) | collective-permute-done | bytes 147488 | tf_op jit(solution)/shard_map/ppermute | solution.py:349
  119.0 1.9 %collective-permute-start.5 = (bf16[192,384]{1,0:T(8,128)(2,1)S(1)}, bf16[192,384]{1,0:T(8,128)(2,1)S(1)}, u32[]{:S(2)}, u32[]{:S(2)}) collective-permute-start(bf16[192,384]{1,0:T(8,128)(2,1)S(1)} %collective-permute-done.4), channel_id=1, source_target_pairs={{0,257},{1,258},{64,321},{65,322},{128,385},{129,386},{192,449},{1... | collective-permute-start | bytes 442376 | tf_op jit(solution)/shard_map/ppermute | solution.py:349
  120.9 0.2 collective-permute-done.2.far_own_ref
  121.2 0.0 collective-permute-done.3.near_ref
  121.2 10.5 %collective-permute-done.5.far_near_ref = bf16[192,384]{1,0:T(8,128)(2,1)S(1)} collective-permute-done((bf16[192,384]{1,0:T(8,128)(2,1)S(1)}, bf16[192,384]{1,0:T(8,128)(2,1)S(1)}, u32[]{:S(2)}, u32[]{:S(2)}) %collective-permute-start.5) | collective-permute-done | bytes 147488 | tf_op jit(solution)/shard_map/ppermute | solution.py:349
  131.7 0.8 finish.1
Async XLA Ops:
  0.0 52.8 %copy-start.2 = (bf16[8,256,512]{2,1,0:T(8,128)(2,1)S(1)}, bf16[8,256,512]{2,1,0:T(8,128)(2,1)}, u32[]{:S(2)}) copy-start(bf16[8,256,512]{2,1,0:T(8,128)(2,1)} %constant.17.clone.table_ref) | copy-start | bytes 6291460
  30.8 6.3 %collective-permute-start = (bf16[16,40,128]{2,1,0:T(8,128)(2,1)S(1)}, bf16[16,40,128]{2,1,0:T(8,128)(2,1)S(1)}, u32[]{:S(2)}, u32[]{:S(2)}) collective-permute-start(bf16[16,40,128]{2,1,0:T(8,128)(2,1)S(1)} %all_to_all.25.rows_ref), channel_id=1, source_target_pairs={{0,1},{1,0},{2,3},{3,2},{4,5},{5,4},{6,7},{7,6},{8,9},{9,8},{10,11... | collective-permute-start | bytes 491528 | tf_op jit(solution)/shard_map/ppermute | solution.py:337
  52.8 12.5 %copy-start.3 = (bf16[2,3,3,1,192,256]{5,4,3,2,1,0:T(8,128)(2,1)S(1)}, bf16[2,3,3,1,192,256]{5,4,3,2,1,0:T(8,128)(2,1)}, u32[]{:S(2)}) copy-start(bf16[2,3,3,1,192,256]{5,4,3,2,1,0:T(8,128)(2,1)} %kernel_ref.1) | copy-start | bytes 5308420
  53.3 22.6 %copy-start.1 = (bf16[8,1024,256]{2,1,0:T(8,128)(2,1)S(1)}, bf16[8,1024,256]{2,1,0:T(8,128)(2,1)}, u32[]{:S(2)}) copy-start(bf16[8,1024,256]{2,1,0:T(8,128)(2,1)} %constant.18.clone.table_ref) | copy-start | bytes 12582916
  75.9 17.9 %copy-start = (bf16[4,192,768]{2,1,0:T(8,128)(2,1)S(1)}, bf16[4,192,768]{2,1,0:T(8,128)(2,1)}, u32[]{:S(2)}) copy-start(bf16[4,192,768]{2,1,0:T(8,128)(2,1)} %constant.19.clone.table_ref) | copy-start | bytes 3538948
  94.3 16.8 %collective-permute-start.1 = (bf16[192,384]{1,0:T(8,128)(2,1)S(1)}, bf16[192,384]{1,0:T(8,128)(2,1)S(1)}, u32[]{:S(2)}, u32[]{:S(2)}) collective-permute-start(bf16[192,384]{1,0:T(8,128)(2,1)S(1)} %get-tuple-element.16), channel_id=1, source_target_pairs={{0,256},{1,259},{64,320},{65,323},{128,384},{129,387},{192,448},{1... | collective-permute-start | bytes 442376 | tf_op jit(solution)/shard_map/ppermute | solution.py:349
  97.7 21.3 %collective-permute-start.4 = (bf16[192,384]{1,0:T(8,128)(2,1)S(1)}, bf16[192,384]{1,0:T(8,128)(2,1)S(1)}, u32[]{:S(2)}, u32[]{:S(2)}) collective-permute-start(bf16[192,384]{1,0:T(8,128)(2,1)S(1)} %get-tuple-element.20), channel_id=1, source_target_pairs={{0,256},{1,259},{64,320},{65,323},{128,384},{129,387},{192,448},{1... | collective-permute-start | bytes 442376 | tf_op jit(solution)/shard_map/ppermute | solution.py:349
  111.1 10.1 %collective-permute-start.2 = (bf16[192,384]{1,0:T(8,128)(2,1)S(1)}, bf16[192,384]{1,0:T(8,128)(2,1)S(1)}, u32[]{:S(2)}, u32[]{:S(2)}) collective-permute-start(bf16[192,384]{1,0:T(8,128)(2,1)S(1)} %collective-permute-done.1), channel_id=1, source_target_pairs={{0,256},{1,259},{64,320},{65,323},{128,384},{129,387},{192,448},{1... | collective-permute-start | bytes 442376 | tf_op jit(solution)/shard_map/ppermute | solution.py:349
  114.1 7.1 %collective-permute-start.3 = (bf16[192,384]{1,0:T(8,128)(2,1)S(1)}, bf16[192,384]{1,0:T(8,128)(2,1)S(1)}, u32[]{:S(2)}, u32[]{:S(2)}) collective-permute-start(bf16[192,384]{1,0:T(8,128)(2,1)S(1)} %get-tuple-element.19), channel_id=1, source_target_pairs={{0,1},{1,0},{2,3},{3,2},{4,5},{5,4},{6,7},{7,6},{8,9},{9,8},{10,11... | collective-permute-start | bytes 442376 | tf_op jit(solution)/shard_map/ppermute | solution.py:337
  119.0 12.7 %collective-permute-start.5 = (bf16[192,384]{1,0:T(8,128)(2,1)S(1)}, bf16[192,384]{1,0:T(8,128)(2,1)S(1)}, u32[]{:S(2)}, u32[]{:S(2)}) collective-permute-start(bf16[192,384]{1,0:T(8,128)(2,1)S(1)} %collective-permute-done.4), channel_id=1, source_target_pairs={{0,257},{1,258},{64,321},{65,322},{128,385},{129,386},{192,449},{1... | collective-permute-start | bytes 442376 | tf_op jit(solution)/shard_map/ppermute | solution.py:349

commit v4 on v2

--- a/solution.py
+++ b/solution.py
@@ -367,7 +367,7 @@
     to_far, to_far_near = inverse_z_call(gz, planes, z_table, (2, 3))
     own, to_near = inverse_z_call(gz, planes, z_table, (0, 1))
     far_own = move_z(move_z(to_far, 4, 0), 4, 0)
-    far_near = move_z(move_z(to_far_near, 4, 0), 4, 1)
+    far_near = move_z(move_z(to_far_near, 4, 1), -4, 0)
     near = swap_cores(to_near)
     return finish_call(core.reshape(1).astype(jnp.int32), own, far_own, near, far_near)
 

time: 130 us -> 130 us (level); the launches traced: 128 us -> 130 us
  starting transfers between devices: 19.3 us -> 26.5 us
  waiting for transfers between devices: 18.7 us -> 13.3 us
    ppermute x4, starting transfers between devices: 11.1 us -> 19.3 us  [move_z(): return lax.ppermute(values, ('z_lo', 'z_hi', 'core'), perm)]
    ppermute x4, waiting for transfers between devices: 18.2 us -> 12.9 us  [move_z(): return lax.ppermute(values, ('z_lo', 'z_hi', 'core'), perm)]
  transfers between devices with their start and end apart: 6 -> 6, of which waited for: 5 -> 4; matrix products, arithmetic and copies ran while one was open for 0% -> 0% of each run, Pallas kernels for 1% -> 1%
where the time goes in v4:
time: 130 us
  blocking collectives  82.9 us (64%)
  starting transfers between devices  26.5 us (20%)
  waiting for transfers between devices  13.3 us (10%)
  Pallas kernels  6.89 us (5%)
    all_to_all x5, blocking collectives, exchange(): return lax.all_to_all(values, axis, split_axis=0, concat_axis=0, tiled=True)  82.9 us
    ppermute x4, starting transfers between devices, move_z(): return lax.ppermute(values, ('z_lo', 'z_hi', 'core'), perm)  19.3 us
    ppermute x4, waiting for transfers between devices, move_z(): return lax.ppermute(values, ('z_lo', 'z_hi', 'core'), perm)  12.9 us
    ppermute x2, starting transfers between devices, swap_cores(): return lax.ppermute(values, 'core', [(0, 1), (1, 0)])  7.26 us
  transfers between devices with their start and end apart: 6, of which 4 were waited for; matrix products, arithmetic and copies ran while one was open for 0% of the time, Pallas kernels for 1%

profile of v4, /device:TPU:1, one launch (start us, length us, event | category | flops | bytes accessed | tf_op | source)
XLA Modules:
  0.0 129.8 jit_solution(2661967523937392991)
XLA Ops:
  0.0 0.0 copy-start.2
  0.0 1.1 pack.1
  1.2 29.7 %all_to_all.25.rows_ref = bf16[16,40,128]{2,1,0:T(8,128)(2,1)S(1)} all-to-all(bf16[16,40,128]{2,1,0:T(8,128)(2,1)S(1)} %get-tuple-element.11), channel_id=1, replica_groups=mesh['z_lo'=8,'y'=4,'gx_pair'=2,'gx_in'=2,'z_hi'=2,'core'=2] {'z_lo','z_..., dimensions={0} | all-to-all | bytes 327680 | tf_op jit(solution)/shard_map/all_to_all | solution.py:333
  30.8 5.3 %collective-permute-start = (bf16[16,40,128]{2,1,0:T(8,128)(2,1)S(1)}, bf16[16,40,128]{2,1,0:T(8,128)(2,1)S(1)}, u32[]{:S(2)}, u32[]{:S(2)}) collective-permute-start(bf16[16,40,128]{2,1,0:T(8,128)(2,1)S(1)} %all_to_all.25.rows_ref), channel_id=1, source_target_pairs={{0,1},{1,0},{2,3},{3,2},{4,5},{5,4},{6,7},{7,6},{8,9},{9,8},{10,11... | collective-permute-start | bytes 491528 | tf_op jit(solution)/shard_map/ppermute | solution.py:337
  36.2 0.6 forward_z_own.1.own_ref
  36.7 0.4 collective-permute-done.rows_ref
  37.2 0.6 forward_z.1
  37.7 15.0 %all_to_all.26.values_ref = bf16[16,72,128]{2,1,0:T(8,128)(2,1)S(1)} all-to-all(bf16[16,72,128]{2,1,0:T(8,128)(2,1)S(1)} %forward_z.1), channel_id=1, replica_groups=mesh['z_lo'=8,'y'=4,'gx_pair'=2,'gx_in'=2,'z_hi'=2,'core'=2] {'y','gx_pa..., dimensions={0} | all-to-all | bytes 589824 | tf_op jit(solution)/shard_map/all_to_all | solution.py:333
  52.8 0.0 copy-done.2
  52.8 0.0 copy-start.3
  52.8 0.5 forward_x.1
  53.3 0.0 copy-start.1
  53.3 12.0 %all_to_all.27.spec_ref = bf16[8,72,512]{2,1,0:T(8,128)(2,1)S(1)} all-to-all(bf16[8,72,512]{2,1,0:T(8,128)(2,1)S(1)} %forward_x.1), channel_id=1, replica_groups=mesh['z_lo'=8,'y'=4,'gx_pair'=2,'gx_in'=2,'z_hi'=2,'core'=2] {'y','gx_in'}, dimensions={0} | all-to-all | bytes 1179648 | tf_op jit(solution)/shard_map/all_to_all | solution.py:333
  65.3 0.0 copy-done.3
  65.3 0.9 modes.1
  66.2 9.7 %all_to_all.28.values_ref = bf16[4,288,256]{2,1,0:T(8,128)(2,1)S(1)} all-to-all(bf16[4,288,256]{2,1,0:T(8,128)(2,1)S(1)} %modes.1), channel_id=1, replica_groups=mesh['z_lo'=8,'y'=4,'gx_pair'=2,'gx_in'=2,'z_hi'=2,'core'=2] {'gx_pair',..., dimensions={0} | all-to-all | bytes 1179648 | tf_op jit(solution)/shard_map/all_to_all | solution.py:333
  75.9 0.0 copy-done.1
  75.9 0.0 copy-start
  75.9 1.4 %inverse_x.1 = bf16[8,96,384]{2,1,0:T(8,128)(2,1)S(1)} custom-call(bf16[4,288,256]{2,1,0:T(8,128)(2,1)S(1)} %all_to_all.28.values_ref, bf16[8,1024,256]{2,1,0:T(8,128)(2,1)S(1)} %copy-done.1), custom_call_target="tpu_custom_call" | custom-call | flops 1208000000 | bytes 5400000 | tf_op jit(solution)/shard_map/inverse_x/pallas_call | solution.py:265
  77.4 16.5 %all_to_all.29 = bf16[8,96,384]{2,1,0:T(8,128)(2,1)S(1)} all-to-all(bf16[8,96,384]{2,1,0:T(8,128)(2,1)S(1)} %inverse_x.1), channel_id=1, replica_groups=mesh['z_lo'=8,'y'=4,'gx_pair'=2,'gx_in'=2,'z_hi'=2,'core'=2] {'gx_pair',..., dimensions={0} | all-to-all | bytes 1179648 | tf_op jit(solution)/shard_map/all_to_all | solution.py:333
  93.9 0.0 copy-done
  93.9 0.5 inverse_z_far.1
  94.3 3.4 %collective-permute-start.1 = (bf16[192,384]{1,0:T(8,128)(2,1)S(1)}, bf16[192,384]{1,0:T(8,128)(2,1)S(1)}, u32[]{:S(2)}, u32[]{:S(2)}) collective-permute-start(bf16[192,384]{1,0:T(8,128)(2,1)S(1)} %get-tuple-element.14), channel_id=1, source_target_pairs={{0,256},{1,259},{64,320},{65,323},{128,384},{129,387},{192,448},{1... | collective-permute-start | bytes 442376 | tf_op jit(solution)/shard_map/ppermute | solution.py:349
  97.7 6.7 %collective-permute-start.4 = (bf16[192,384]{1,0:T(8,128)(2,1)S(1)}, bf16[192,384]{1,0:T(8,128)(2,1)S(1)}, u32[]{:S(2)}, u32[]{:S(2)}) collective-permute-start(bf16[192,384]{1,0:T(8,128)(2,1)S(1)} %get-tuple-element.16), channel_id=1, source_target_pairs={{0,257},{1,258},{64,321},{65,322},{128,385},{129,386},{192,449},{1... | collective-permute-start | bytes 442376 | tf_op jit(solution)/shard_map/ppermute | solution.py:349
  104.5 0.5 inverse_z_near.1
  104.9 1.9 %collective-permute-start.3 = (bf16[192,384]{1,0:T(8,128)(2,1)S(1)}, bf16[192,384]{1,0:T(8,128)(2,1)S(1)}, u32[]{:S(2)}, u32[]{:S(2)}) collective-permute-start(bf16[192,384]{1,0:T(8,128)(2,1)S(1)} %get-tuple-element.15), channel_id=1, source_target_pairs={{0,1},{1,0},{2,3},{3,2},{4,5},{5,4},{6,7},{7,6},{8,9},{9,8},{10,11... | collective-permute-start | bytes 442376 | tf_op jit(solution)/shard_map/ppermute | solution.py:337
  106.9 5.6 %collective-permute-done.1 = bf16[192,384]{1,0:T(8,128)(2,1)S(1)} collective-permute-done((bf16[192,384]{1,0:T(8,128)(2,1)S(1)}, bf16[192,384]{1,0:T(8,128)(2,1)S(1)}, u32[]{:S(2)}, u32[]{:S(2)}) %collective-permute-start.1) | collective-permute-done | bytes 147488 | tf_op jit(solution)/shard_map/ppermute | solution.py:349
  112.5 1.9 %collective-permute-start.2 = (bf16[192,384]{1,0:T(8,128)(2,1)S(1)}, bf16[192,384]{1,0:T(8,128)(2,1)S(1)}, u32[]{:S(2)}, u32[]{:S(2)}) collective-permute-start(bf16[192,384]{1,0:T(8,128)(2,1)S(1)} %collective-permute-done.1), channel_id=1, source_target_pairs={{0,256},{1,259},{64,320},{65,323},{128,384},{129,387},{192,448},{1... | collective-permute-start | bytes 442376 | tf_op jit(solution)/shard_map/ppermute | solution.py:349
  114.4 0.0 collective-permute-done.4
  114.4 7.3 %collective-permute-start.5 = (bf16[192,384]{1,0:T(8,128)(2,1)S(1)}, bf16[192,384]{1,0:T(8,128)(2,1)S(1)}, u32[]{:S(2)}, u32[]{:S(2)}) collective-permute-start(bf16[192,384]{1,0:T(8,128)(2,1)S(1)} %collective-permute-done.4), channel_id=1, source_target_pairs={{0,258},{1,257},{64,322},{65,321},{128,386},{129,385},{192,450},{1... | collective-permute-start | bytes 442376 | tf_op jit(solution)/shard_map/ppermute | solution.py:349
  121.7 0.0 collective-permute-done.3.near_ref
  121.7 3.4 %collective-permute-done.2.far_own_ref = bf16[192,384]{1,0:T(8,128)(2,1)S(1)} collective-permute-done((bf16[192,384]{1,0:T(8,128)(2,1)S(1)}, bf16[192,384]{1,0:T(8,128)(2,1)S(1)}, u32[]{:S(2)}, u32[]{:S(2)}) %collective-permute-start.2) | collective-permute-done | bytes 147488 | tf_op jit(solution)/shard_map/ppermute | solution.py:349
  125.1 3.9 %collective-permute-done.5.far_near_ref = bf16[192,384]{1,0:T(8,128)(2,1)S(1)} collective-permute-done((bf16[192,384]{1,0:T(8,128)(2,1)S(1)}, bf16[192,384]{1,0:T(8,128)(2,1)S(1)}, u32[]{:S(2)}, u32[]{:S(2)}) %collective-permute-start.5) | collective-permute-done | bytes 147488 | tf_op jit(solution)/shard_map/ppermute | solution.py:349
  129.0 0.8 finish.1
Async XLA Ops:
  0.0 52.8 %copy-start.2 = (bf16[8,256,512]{2,1,0:T(8,128)(2,1)S(1)}, bf16[8,256,512]{2,1,0:T(8,128)(2,1)}, u32[]{:S(2)}) copy-start(bf16[8,256,512]{2,1,0:T(8,128)(2,1)} %constant.17.clone.table_ref) | copy-start | bytes 6291460
  30.8 6.3 %collective-permute-start = (bf16[16,40,128]{2,1,0:T(8,128)(2,1)S(1)}, bf16[16,40,128]{2,1,0:T(8,128)(2,1)S(1)}, u32[]{:S(2)}, u32[]{:S(2)}) collective-permute-start(bf16[16,40,128]{2,1,0:T(8,128)(2,1)S(1)} %all_to_all.25.rows_ref), channel_id=1, source_target_pairs={{0,1},{1,0},{2,3},{3,2},{4,5},{5,4},{6,7},{7,6},{8,9},{9,8},{10,11... | collective-permute-start | bytes 491528 | tf_op jit(solution)/shard_map/ppermute | solution.py:337
  52.8 12.5 %copy-start.3 = (bf16[2,3,3,1,192,256]{5,4,3,2,1,0:T(8,128)(2,1)S(1)}, bf16[2,3,3,1,192,256]{5,4,3,2,1,0:T(8,128)(2,1)}, u32[]{:S(2)}) copy-start(bf16[2,3,3,1,192,256]{5,4,3,2,1,0:T(8,128)(2,1)} %kernel_ref.1) | copy-start | bytes 5308420
  53.3 22.6 %copy-start.1 = (bf16[8,1024,256]{2,1,0:T(8,128)(2,1)S(1)}, bf16[8,1024,256]{2,1,0:T(8,128)(2,1)}, u32[]{:S(2)}) copy-start(bf16[8,1024,256]{2,1,0:T(8,128)(2,1)} %constant.18.clone.table_ref) | copy-start | bytes 12582916
  75.9 17.9 %copy-start = (bf16[4,192,768]{2,1,0:T(8,128)(2,1)S(1)}, bf16[4,192,768]{2,1,0:T(8,128)(2,1)}, u32[]{:S(2)}) copy-start(bf16[4,192,768]{2,1,0:T(8,128)(2,1)} %constant.19.clone.table_ref) | copy-start | bytes 3538948
  94.3 18.1 %collective-permute-start.1 = (bf16[192,384]{1,0:T(8,128)(2,1)S(1)}, bf16[192,384]{1,0:T(8,128)(2,1)S(1)}, u32[]{:S(2)}, u32[]{:S(2)}) collective-permute-start(bf16[192,384]{1,0:T(8,128)(2,1)S(1)} %get-tuple-element.14), channel_id=1, source_target_pairs={{0,256},{1,259},{64,320},{65,323},{128,384},{129,387},{192,448},{1... | collective-permute-start | bytes 442376 | tf_op jit(solution)/shard_map/ppermute | solution.py:349
  97.7 16.7 %collective-permute-start.4 = (bf16[192,384]{1,0:T(8,128)(2,1)S(1)}, bf16[192,384]{1,0:T(8,128)(2,1)S(1)}, u32[]{:S(2)}, u32[]{:S(2)}) collective-permute-start(bf16[192,384]{1,0:T(8,128)(2,1)S(1)} %get-tuple-element.16), channel_id=1, source_target_pairs={{0,257},{1,258},{64,321},{65,322},{128,385},{129,386},{192,449},{1... | collective-permute-start | bytes 442376 | tf_op jit(solution)/shard_map/ppermute | solution.py:349
  104.9 16.7 %collective-permute-start.3 = (bf16[192,384]{1,0:T(8,128)(2,1)S(1)}, bf16[192,384]{1,0:T(8,128)(2,1)S(1)}, u32[]{:S(2)}, u32[]{:S(2)}) collective-permute-start(bf16[192,384]{1,0:T(8,128)(2,1)S(1)} %get-tuple-element.15), channel_id=1, source_target_pairs={{0,1},{1,0},{2,3},{3,2},{4,5},{5,4},{6,7},{7,6},{8,9},{9,8},{10,11... | collective-permute-start | bytes 442376 | tf_op jit(solution)/shard_map/ppermute | solution.py:337
  112.5 12.7 %collective-permute-start.2 = (bf16[192,384]{1,0:T(8,128)(2,1)S(1)}, bf16[192,384]{1,0:T(8,128)(2,1)S(1)}, u32[]{:S(2)}, u32[]{:S(2)}) collective-permute-start(bf16[192,384]{1,0:T(8,128)(2,1)S(1)} %collective-permute-done.1), channel_id=1, source_target_pairs={{0,256},{1,259},{64,320},{65,323},{128,384},{129,387},{192,448},{1... | collective-permute-start | bytes 442376 | tf_op jit(solution)/shard_map/ppermute | solution.py:349
  114.4 14.6 %collective-permute-start.5 = (bf16[192,384]{1,0:T(8,128)(2,1)S(1)}, bf16[192,384]{1,0:T(8,128)(2,1)S(1)}, u32[]{:S(2)}, u32[]{:S(2)}) collective-permute-start(bf16[192,384]{1,0:T(8,128)(2,1)S(1)} %collective-permute-done.4), channel_id=1, source_target_pairs={{0,258},{1,257},{64,322},{65,321},{128,386},{129,385},{192,450},{1... | collective-permute-start | bytes 442376 | tf_op jit(solution)/shard_map/ppermute | solution.py:349

commit v5 on v2

--- a/solution.py
+++ b/solution.py
@@ -31,7 +31,7 @@
 
 
 def forward_x_table():
-    y, source, low, r = np.meshgrid(
+    source, y, low, r = np.meshgrid(
         np.arange(4), np.arange(4), np.arange(8), np.arange(8), indexing="ij"
     )
     x = (8 * (4 * (low * 4 + y) + source) + r).reshape(-1)
@@ -51,8 +51,8 @@
 
 def inverse_z_table():
     q = (
-        48 * np.arange(4)[:, None, None]
-        + 192 * np.arange(2)[None, :, None]
+        192 * np.arange(2)[:, None, None]
+        + 48 * np.arange(4)[None, :, None]
         + np.arange(48)[None, None, :]
     ).reshape(-1)
     theta = angle(np.arange(NZ), q, NZ).reshape(NZ, 8, 48)
@@ -112,7 +112,7 @@
     result = None
     for high in range(2):
         position = high * 2 + (core if step == 0 else 1 - core)
-        blocks = [rows_ref[low * 2 + high].astype(jnp.float32) for low in range(8)]
+        blocks = [rows_ref[high * 8 + low].astype(jnp.float32) for low in range(8)]
         main = jnp.concatenate([block[c * 8 : c * 8 + 8] for block in blocks], axis=0)
         start = 24 + (c // 2) * 8
         tail = jnp.concatenate([block[start : start + 8] for block in blocks], axis=0)
@@ -155,7 +155,7 @@
                 start = y * 48 + half * 24
                 pieces = [total[start : start + 24] for total in totals]
                 block = jnp.concatenate(pieces, axis=0).astype(jnp.bfloat16)
-                out_ref[y * 4 + pair * 2 + half] = block
+                out_ref[pair * 8 + half * 4 + y] = block
 
 
 def forward_z_call(me, rows, table, own):
@@ -194,7 +194,7 @@
     for half in range(2):
         block = total[half * 72 : half * 72 + 72].astype(jnp.bfloat16)
         for y in range(4):
-            out_ref[y * 2 + half] = block
+            out_ref[half * 4 + y] = block
 
 
 def forward_x_call(values, table):
@@ -208,7 +208,7 @@
 
 
 def modes_body(kernel_ref, spec_ref, out_ref):
-    halves = [spec_ref[half].astype(jnp.float32) for half in range(2)]
+    halves = [spec_ref[half, 0].astype(jnp.float32) for half in range(2)]
     spec = []
     for c in range(3):
         pieces = [half[c * 24 : c * 24 + 24] for half in halves]
@@ -235,7 +235,7 @@
         grid=(4,),
         in_specs=[
             pl.BlockSpec((2, 3, 3, 1, 48, NP), lambda j: (0, 0, 0, 0, j, 0)),
-            pl.BlockSpec((2, 72, 512), lambda j: (j, 0, 0)),
+            pl.BlockSpec((2, 1, 72, 512), lambda j: (0, j, 0, 0)),
         ],
         out_specs=pl.BlockSpec((1, 288, NP), lambda j: (j, 0, 0)),
         out_shape=jax.ShapeDtypeStruct((4, 288, NP), jnp.bfloat16),
@@ -254,8 +254,8 @@
         real = (total[:144, :128] - total[144:, 128:]).astype(jnp.bfloat16)
         imag = (total[:144, 128:] + total[144:, :128]).astype(jnp.bfloat16)
         for o in range(3):
-            out_ref[j, 0:48, o * 128 : (o + 1) * 128] = real[o * 48 : (o + 1) * 48]
-            out_ref[j, 48:96, o * 128 : (o + 1) * 128] = imag[o * 48 : (o + 1) * 48]
+            out_ref[(j % 2) * 4 + j // 2, 0:48, o * 128 : (o + 1) * 128] = real[o * 48 : (o + 1) * 48]
+            out_ref[(j % 2) * 4 + j // 2, 48:96, o * 128 : (o + 1) * 128] = imag[o * 48 : (o + 1) * 48]
         return carry
 
     lax.fori_loop(0, 8, block, 0, unroll=True)
@@ -292,9 +292,9 @@
                 pl.BlockSpec((NZ, 384), lambda j, s: (0, 0)),
                 pl.BlockSpec((4, NQ, NZ), lambda j, s: (0, 0, 0)),
             ],
-            out_specs=[block] * 2,
+            out_specs=[block] * len(steps),
         ),
-        out_shape=[jax.ShapeDtypeStruct((NQ, 384), jnp.bfloat16) for _ in range(2)],
+        out_shape=[jax.ShapeDtypeStruct((NQ, 384), jnp.bfloat16) for _ in steps],
         compiler_params=pltpu.CompilerParams(vmem_limit_bytes=VMEM),
         cost_estimate=pl.CostEstimate(flops=227000000, bytes_accessed=2000000, transcendentals=0),
         name="inverse_z_far" if steps[0] else "inverse_z_near",
@@ -354,17 +354,18 @@
     gz = (lax.axis_index("z_hi") * 2 + core).reshape(1).astype(jnp.int32)
 
     rows, z_table = pack_call(wall, jnp.asarray(forward_z_table()))
-    rows = exchange(rows, ("z_lo", "z_hi"))
+    rows = exchange(rows, ("z_hi", "z_lo"))
     other = swap_cores(rows)
     z_spectra = forward_z_call(gz, other, z_table, forward_z_call(gz, rows, z_table, None))
-    z_spectra = exchange(z_spectra, ("y", "gx_pair", "gx_in"))
-    spec = exchange(forward_x_call(z_spectra, jnp.asarray(forward_x_table())), ("y", "gx_in"))
-
-    modes = exchange(modes_call(kernel, spec), ("gx_pair", "gx_in"))
-    planes = exchange(inverse_x_call(modes, jnp.asarray(inverse_x_table())), ("gx_pair", "gx_in", "core"))
+    z_spectra = exchange(z_spectra, ("gx_pair", "gx_in", "y"))
+    spec = exchange(forward_x_call(z_spectra, jnp.asarray(forward_x_table())), ("gx_in", "y"))
+
+    modes = exchange(modes_call(kernel, spec.reshape(2, 4, 72, 512)), ("gx_pair", "gx_in"))
+    planes = exchange(inverse_x_call(modes, jnp.asarray(inverse_x_table())), ("core", "gx_pair", "gx_in"))
     planes = planes.reshape(NZ, 384)
     z_table = jnp.asarray(inverse_z_table())
-    to_far, to_far_near = inverse_z_call(gz, planes, z_table, (2, 3))
+    (to_far,) = inverse_z_call(gz, planes, z_table, (2,))
+    (to_far_near,) = inverse_z_call(gz, planes, z_table, (3,))
     own, to_near = inverse_z_call(gz, planes, z_table, (0, 1))
     far_own = move_z(move_z(to_far, 4, 0), 4, 0)
     far_near = move_z(move_z(to_far_near, 4, 0), 4, 1)

time: 130 us -> 132 us (1.015)
  starting transfers between devices: 19.3 us -> 24.6 us
  blocking collectives: 82.9 us -> 80.7 us
    ppermute x4, starting transfers between devices: 11.1 us -> 15.4 us  [move_z(): return lax.ppermute(values, ('z_lo', 'z_hi', 'core'), perm)]
    all_to_all x5, blocking collectives: 82.9 us -> 80.7 us  [exchange(): return lax.all_to_all(values, axis, split_axis=0, concat_axis=0, tiled=True)]
where the time goes in v5:
time: 132 us; the launch traced here: 131 us
  blocking collectives  80.7 us (61%)
  starting transfers between devices  24.6 us (19%)
  waiting for transfers between devices  18.6 us (14%)
  Pallas kernels  7.11 us (5%)
    all_to_all x5, blocking collectives, exchange(): return lax.all_to_all(values, axis, split_axis=0, concat_axis=0, tiled=True)  80.7 us
    ppermute x4, waiting for transfers between devices, move_z(): return lax.ppermute(values, ('z_lo', 'z_hi', 'core'), perm)  18.2 us
    ppermute x4, starting transfers between devices, move_z(): return lax.ppermute(values, ('z_lo', 'z_hi', 'core'), perm)  15.4 us
    ppermute x2, starting transfers between devices, swap_cores(): return lax.ppermute(values, 'core', [(0, 1), (1, 0)])  9.12 us
  transfers between devices with their start and end apart: 6, of which 5 were waited for; matrix products, arithmetic and copies ran while one was open for 0% of the time, Pallas kernels for 1%

profile of v5, /device:TPU:1, one launch (start us, length us, event | category | flops | bytes accessed | tf_op | source)
XLA Modules:
  0.0 131.2 jit_solution(12651581284172121958)
XLA Ops:
  0.0 0.0 copy-start.2
  0.0 1.1 pack.1
  1.2 27.8 %all_to_all.25.rows_ref = bf16[16,40,128]{2,1,0:T(8,128)(2,1)S(1)} all-to-all(bf16[16,40,128]{2,1,0:T(8,128)(2,1)S(1)} %get-tuple-element.9), channel_id=1, replica_groups=mesh['z_lo'=8,'y'=4,'gx_pair'=2,'gx_in'=2,'z_hi'=2,'core'=2] {'z_hi','z_..., dimensions={0} | all-to-all | bytes 327680 | tf_op jit(solution)/shard_map/all_to_all | solution.py:333
  28.9 6.3 %collective-permute-start = (bf16[16,40,128]{2,1,0:T(8,128)(2,1)S(1)}, bf16[16,40,128]{2,1,0:T(8,128)(2,1)S(1)}, u32[]{:S(2)}, u32[]{:S(2)}) collective-permute-start(bf16[16,40,128]{2,1,0:T(8,128)(2,1)S(1)} %all_to_all.25.rows_ref), channel_id=1, source_target_pairs={{0,1},{1,0},{2,3},{3,2},{4,5},{5,4},{6,7},{7,6},{8,9},{9,8},{10,11... | collective-permute-start | bytes 491528 | tf_op jit(solution)/shard_map/ppermute | solution.py:337
  35.2 0.6 forward_z_own.1.own_ref
  35.8 0.4 collective-permute-done.rows_ref
  36.2 0.6 forward_z.1
  36.8 14.3 %all_to_all.26.values_ref = bf16[16,72,128]{2,1,0:T(8,128)(2,1)S(1)} all-to-all(bf16[16,72,128]{2,1,0:T(8,128)(2,1)S(1)} %forward_z.1), channel_id=1, replica_groups=mesh['z_lo'=8,'y'=4,'gx_pair'=2,'gx_in'=2,'z_hi'=2,'core'=2] {'gx_pair',..., dimensions={0} | all-to-all | bytes 589824 | tf_op jit(solution)/shard_map/all_to_all | solution.py:333
  51.1 0.0 copy-done.2
  51.1 0.0 copy-start.3
  51.1 0.5 forward_x.1
  51.6 0.0 copy-start.1
  51.6 11.6 %all_to_all.27 = bf16[8,72,512]{2,1,0:T(8,128)(2,1)S(1)} all-to-all(bf16[8,72,512]{2,1,0:T(8,128)(2,1)S(1)} %forward_x.1), channel_id=1, replica_groups=mesh['z_lo'=8,'y'=4,'gx_pair'=2,'gx_in'=2,'z_hi'=2,'core'=2] {'gx_in','y'}, dimensions={0} | all-to-all | bytes 1179648 | tf_op jit(solution)/shard_map/all_to_all | solution.py:333
  63.2 0.0 copy-done.3
  63.2 1.0 modes.1
  64.2 9.7 %all_to_all.28.values_ref = bf16[4,288,256]{2,1,0:T(8,128)(2,1)S(1)} all-to-all(bf16[4,288,256]{2,1,0:T(8,128)(2,1)S(1)} %modes.1), channel_id=1, replica_groups=mesh['z_lo'=8,'y'=4,'gx_pair'=2,'gx_in'=2,'z_hi'=2,'core'=2] {'gx_pair',..., dimensions={0} | all-to-all | bytes 1179648 | tf_op jit(solution)/shard_map/all_to_all | solution.py:333
  73.9 0.0 copy-done.1
  73.9 0.0 copy-start
  73.9 1.4 %inverse_x.1 = bf16[8,96,384]{2,1,0:T(8,128)(2,1)S(1)} custom-call(bf16[4,288,256]{2,1,0:T(8,128)(2,1)S(1)} %all_to_all.28.values_ref, bf16[8,1024,256]{2,1,0:T(8,128)(2,1)S(1)} %copy-done.1), custom_call_target="tpu_custom_call" | custom-call | flops 1208000000 | bytes 5400000 | tf_op jit(solution)/shard_map/inverse_x/pallas_call | solution.py:265
  75.3 17.4 %all_to_all.29 = bf16[8,96,384]{2,1,0:T(8,128)(2,1)S(1)} all-to-all(bf16[8,96,384]{2,1,0:T(8,128)(2,1)S(1)} %inverse_x.1), channel_id=1, replica_groups=mesh['z_lo'=8,'y'=4,'gx_pair'=2,'gx_in'=2,'z_hi'=2,'core'=2] {'core','gx..., dimensions={0} | all-to-all | bytes 1179648 | tf_op jit(solution)/shard_map/all_to_all | solution.py:333
  92.7 0.0 copy-done
  92.7 0.3 inverse_z_far.2
  93.0 3.7 %collective-permute-start.1 = (bf16[192,384]{1,0:T(8,128)(2,1)S(1)}, bf16[192,384]{1,0:T(8,128)(2,1)S(1)}, u32[]{:S(2)}, u32[]{:S(2)}) collective-permute-start(bf16[192,384]{1,0:T(8,128)(2,1)S(1)} %inverse_z_far.2), channel_id=1, source_target_pairs={{0,256},{1,259},{64,320},{65,323},{128,384},{129,387},{192,448},{1... | collective-permute-start | bytes 442376 | tf_op jit(solution)/shard_map/ppermute | solution.py:349
  96.8 0.3 inverse_z_far.3
  97.1 3.0 %collective-permute-start.4 = (bf16[192,384]{1,0:T(8,128)(2,1)S(1)}, bf16[192,384]{1,0:T(8,128)(2,1)S(1)}, u32[]{:S(2)}, u32[]{:S(2)}) collective-permute-start(bf16[192,384]{1,0:T(8,128)(2,1)S(1)} %inverse_z_far.3), channel_id=1, source_target_pairs={{0,256},{1,259},{64,320},{65,323},{128,384},{129,387},{192,448},{1... | collective-permute-start | bytes 442376 | tf_op jit(solution)/shard_map/ppermute | solution.py:349
  100.1 0.5 inverse_z_near.1
  100.6 2.8 %collective-permute-start.3 = (bf16[192,384]{1,0:T(8,128)(2,1)S(1)}, bf16[192,384]{1,0:T(8,128)(2,1)S(1)}, u32[]{:S(2)}, u32[]{:S(2)}) collective-permute-start(bf16[192,384]{1,0:T(8,128)(2,1)S(1)} %get-tuple-element.12), channel_id=1, source_target_pairs={{0,1},{1,0},{2,3},{3,2},{4,5},{5,4},{6,7},{7,6},{8,9},{9,8},{10,11... | collective-permute-start | bytes 442376 | tf_op jit(solution)/shard_map/ppermute | solution.py:337
  103.4 1.9 %collective-permute-done.1 = bf16[192,384]{1,0:T(8,128)(2,1)S(1)} collective-permute-done((bf16[192,384]{1,0:T(8,128)(2,1)S(1)}, bf16[192,384]{1,0:T(8,128)(2,1)S(1)}, u32[]{:S(2)}, u32[]{:S(2)}) %collective-permute-start.1) | collective-permute-done | bytes 147488 | tf_op jit(solution)/shard_map/ppermute | solution.py:349
  105.3 4.7 %collective-permute-start.2 = (bf16[192,384]{1,0:T(8,128)(2,1)S(1)}, bf16[192,384]{1,0:T(8,128)(2,1)S(1)}, u32[]{:S(2)}, u32[]{:S(2)}) collective-permute-start(bf16[192,384]{1,0:T(8,128)(2,1)S(1)} %collective-permute-done.1), channel_id=1, source_target_pairs={{0,256},{1,259},{64,320},{65,323},{128,384},{129,387},{192,448},{1... | collective-permute-start | bytes 442376 | tf_op jit(solution)/shard_map/ppermute | solution.py:349
  110.0 1.4 %collective-permute-done.4 = bf16[192,384]{1,0:T(8,128)(2,1)S(1)} collective-permute-done((bf16[192,384]{1,0:T(8,128)(2,1)S(1)}, bf16[192,384]{1,0:T(8,128)(2,1)S(1)}, u32[]{:S(2)}, u32[]{:S(2)}) %collective-permute-start.4) | collective-permute-done | bytes 147488 | tf_op jit(solution)/shard_map/ppermute | solution.py:349
  111.5 4.0 %collective-permute-start.5 = (bf16[192,384]{1,0:T(8,128)(2,1)S(1)}, bf16[192,384]{1,0:T(8,128)(2,1)S(1)}, u32[]{:S(2)}, u32[]{:S(2)}) collective-permute-start(bf16[192,384]{1,0:T(8,128)(2,1)S(1)} %collective-permute-done.4), channel_id=1, source_target_pairs={{0,257},{1,258},{64,321},{65,322},{128,385},{129,386},{192,449},{1... | collective-permute-start | bytes 442376 | tf_op jit(solution)/shard_map/ppermute | solution.py:349
  115.5 0.0 collective-permute-done.3.near_ref
  115.5 4.3 %collective-permute-done.2.far_own_ref = bf16[192,384]{1,0:T(8,128)(2,1)S(1)} collective-permute-done((bf16[192,384]{1,0:T(8,128)(2,1)S(1)}, bf16[192,384]{1,0:T(8,128)(2,1)S(1)}, u32[]{:S(2)}, u32[]{:S(2)}) %collective-permute-start.2) | collective-permute-done | bytes 147488 | tf_op jit(solution)/shard_map/ppermute | solution.py:349
  119.8 10.6 %collective-permute-done.5.far_near_ref = bf16[192,384]{1,0:T(8,128)(2,1)S(1)} collective-permute-done((bf16[192,384]{1,0:T(8,128)(2,1)S(1)}, bf16[192,384]{1,0:T(8,128)(2,1)S(1)}, u32[]{:S(2)}, u32[]{:S(2)}) %collective-permute-start.5) | collective-permute-done | bytes 147488 | tf_op jit(solution)/shard_map/ppermute | solution.py:349
  130.3 0.8 finish.1
Async XLA Ops:
  0.0 51.1 %copy-start.2 = (bf16[8,256,512]{2,1,0:T(8,128)(2,1)S(1)}, bf16[8,256,512]{2,1,0:T(8,128)(2,1)}, u32[]{:S(2)}) copy-start(bf16[8,256,512]{2,1,0:T(8,128)(2,1)} %constant.17.clone.table_ref) | copy-start | bytes 6291460
  28.9 7.3 %collective-permute-start = (bf16[16,40,128]{2,1,0:T(8,128)(2,1)S(1)}, bf16[16,40,128]{2,1,0:T(8,128)(2,1)S(1)}, u32[]{:S(2)}, u32[]{:S(2)}) collective-permute-start(bf16[16,40,128]{2,1,0:T(8,128)(2,1)S(1)} %all_to_all.25.rows_ref), channel_id=1, source_target_pairs={{0,1},{1,0},{2,3},{3,2},{4,5},{5,4},{6,7},{7,6},{8,9},{9,8},{10,11... | collective-permute-start | bytes 491528 | tf_op jit(solution)/shard_map/ppermute | solution.py:337
  51.1 12.2 %copy-start.3 = (bf16[2,3,3,1,192,256]{5,4,3,2,1,0:T(8,128)(2,1)S(1)}, bf16[2,3,3,1,192,256]{5,4,3,2,1,0:T(8,128)(2,1)}, u32[]{:S(2)}) copy-start(bf16[2,3,3,1,192,256]{5,4,3,2,1,0:T(8,128)(2,1)} %kernel_ref.1) | copy-start | bytes 5308420
  51.6 22.3 %copy-start.1 = (bf16[8,1024,256]{2,1,0:T(8,128)(2,1)S(1)}, bf16[8,1024,256]{2,1,0:T(8,128)(2,1)}, u32[]{:S(2)}) copy-start(bf16[8,1024,256]{2,1,0:T(8,128)(2,1)} %constant.18.clone.table_ref) | copy-start | bytes 12582916
  73.9 18.8 %copy-start = (bf16[4,192,768]{2,1,0:T(8,128)(2,1)S(1)}, bf16[4,192,768]{2,1,0:T(8,128)(2,1)}, u32[]{:S(2)}) copy-start(bf16[4,192,768]{2,1,0:T(8,128)(2,1)} %constant.19.clone.table_ref) | copy-start | bytes 3538948
  93.0 12.3 %collective-permute-start.1 = (bf16[192,384]{1,0:T(8,128)(2,1)S(1)}, bf16[192,384]{1,0:T(8,128)(2,1)S(1)}, u32[]{:S(2)}, u32[]{:S(2)}) collective-permute-start(bf16[192,384]{1,0:T(8,128)(2,1)S(1)} %inverse_z_far.2), channel_id=1, source_target_pairs={{0,256},{1,259},{64,320},{65,323},{128,384},{129,387},{192,448},{1... | collective-permute-start | bytes 442376 | tf_op jit(solution)/shard_map/ppermute | solution.py:349
  97.1 14.4 %collective-permute-start.4 = (bf16[192,384]{1,0:T(8,128)(2,1)S(1)}, bf16[192,384]{1,0:T(8,128)(2,1)S(1)}, u32[]{:S(2)}, u32[]{:S(2)}) collective-permute-start(bf16[192,384]{1,0:T(8,128)(2,1)S(1)} %inverse_z_far.3), channel_id=1, source_target_pairs={{0,256},{1,259},{64,320},{65,323},{128,384},{129,387},{192,448},{1... | collective-permute-start | bytes 442376 | tf_op jit(solution)/shard_map/ppermute | solution.py:349
  100.6 14.9 %collective-permute-start.3 = (bf16[192,384]{1,0:T(8,128)(2,1)S(1)}, bf16[192,384]{1,0:T(8,128)(2,1)S(1)}, u32[]{:S(2)}, u32[]{:S(2)}) collective-permute-start(bf16[192,384]{1,0:T(8,128)(2,1)S(1)} %get-tuple-element.12), channel_id=1, source_target_pairs={{0,1},{1,0},{2,3},{3,2},{4,5},{5,4},{6,7},{7,6},{8,9},{9,8},{10,11... | collective-permute-start | bytes 442376 | tf_op jit(solution)/shard_map/ppermute | solution.py:337
  105.3 14.4 %collective-permute-start.2 = (bf16[192,384]{1,0:T(8,128)(2,1)S(1)}, bf16[192,384]{1,0:T(8,128)(2,1)S(1)}, u32[]{:S(2)}, u32[]{:S(2)}) collective-permute-start(bf16[192,384]{1,0:T(8,128)(2,1)S(1)} %collective-permute-done.1), channel_id=1, source_target_pairs={{0,256},{1,259},{64,320},{65,323},{128,384},{129,387},{192,448},{1... | collective-permute-start | bytes 442376 | tf_op jit(solution)/shard_map/ppermute | solution.py:349
  111.5 18.9 %collective-permute-start.5 = (bf16[192,384]{1,0:T(8,128)(2,1)S(1)}, bf16[192,384]{1,0:T(8,128)(2,1)S(1)}, u32[]{:S(2)}, u32[]{:S(2)}) collective-permute-start(bf16[192,384]{1,0:T(8,128)(2,1)S(1)} %collective-permute-done.4), channel_id=1, source_target_pairs={{0,257},{1,258},{64,321},{65,322},{128,385},{129,386},{192,449},{1... | collective-permute-start | bytes 442376 | tf_op jit(solution)/shard_map/ppermute | solution.py:349

commit v6 on v5

--- a/solution.py
+++ b/solution.py
@@ -112,7 +112,7 @@
     result = None
     for high in range(2):
         position = high * 2 + (core if step == 0 else 1 - core)
-        blocks = [rows_ref[high * 8 + low].astype(jnp.float32) for low in range(8)]
+        blocks = [rows_ref[low * 2 + high].astype(jnp.float32) for low in range(8)]
         main = jnp.concatenate([block[c * 8 : c * 8 + 8] for block in blocks], axis=0)
         start = 24 + (c // 2) * 8
         tail = jnp.concatenate([block[start : start + 8] for block in blocks], axis=0)
@@ -354,7 +354,7 @@
     gz = (lax.axis_index("z_hi") * 2 + core).reshape(1).astype(jnp.int32)
 
     rows, z_table = pack_call(wall, jnp.asarray(forward_z_table()))
-    rows = exchange(rows, ("z_hi", "z_lo"))
+    rows = exchange(rows, ("z_lo", "z_hi"))
     other = swap_cores(rows)
     z_spectra = forward_z_call(gz, other, z_table, forward_z_call(gz, rows, z_table, None))
     z_spectra = exchange(z_spectra, ("gx_pair", "gx_in", "y"))

time: 132 us -> 129 us (0.977)
  starting transfers between devices: 24.6 us -> 17.5 us
  blocking collectives: 80.7 us -> 82.6 us
  waiting for transfers between devices: 18.6 us -> 20.1 us
    ppermute x4, starting transfers between devices: 15.4 us -> 9.69 us  [move_z(): return lax.ppermute(values, ('z_lo', 'z_hi', 'core'), perm)]
    all_to_all x5, blocking collectives: 80.7 us -> 82.6 us  [exchange(): return lax.all_to_all(values, axis, split_axis=0, concat_axis=0, tiled=True)]
    ppermute x4, waiting for transfers between devices: 18.2 us -> 19.6 us  [move_z(): return lax.ppermute(values, ('z_lo', 'z_hi', 'core'), perm)]
where the time goes in v6:
time: 129 us; the launch traced here: 127 us
  blocking collectives  82.6 us (64%)
  waiting for transfers between devices  20.1 us (16%)
  starting transfers between devices  17.5 us (14%)
  Pallas kernels  7.1 us (6%)
    all_to_all x5, blocking collectives, exchange(): return lax.all_to_all(values, axis, split_axis=0, concat_axis=0, tiled=True)  82.6 us
    ppermute x4, waiting for transfers between devices, move_z(): return lax.ppermute(values, ('z_lo', 'z_hi', 'core'), perm)  19.6 us
    ppermute x4, starting transfers between devices, move_z(): return lax.ppermute(values, ('z_lo', 'z_hi', 'core'), perm)  9.69 us
    ppermute x2, starting transfers between devices, swap_cores(): return lax.ppermute(values, 'core', [(0, 1), (1, 0)])  7.81 us
  transfers between devices with their start and end apart: 6, of which 5 were waited for; matrix products, arithmetic and copies ran while one was open for 0% of the time, Pallas kernels for 1%

profile of v6, /device:TPU:1, one launch (start us, length us, event | category | flops | bytes accessed | tf_op | source)
XLA Modules:
  0.0 127.4 jit_solution(4111398100059474630)
XLA Ops:
  0.0 0.0 copy-start.2
  0.0 1.1 pack.1
  1.2 29.7 %all_to_all.25.rows_ref = bf16[16,40,128]{2,1,0:T(8,128)(2,1)S(1)} all-to-all(bf16[16,40,128]{2,1,0:T(8,128)(2,1)S(1)} %get-tuple-element.9), channel_id=1, replica_groups=mesh['z_lo'=8,'y'=4,'gx_pair'=2,'gx_in'=2,'z_hi'=2,'core'=2] {'z_lo','z_..., dimensions={0} | all-to-all | bytes 327680 | tf_op jit(solution)/shard_map/all_to_all | solution.py:333
  30.8 5.3 %collective-permute-start = (bf16[16,40,128]{2,1,0:T(8,128)(2,1)S(1)}, bf16[16,40,128]{2,1,0:T(8,128)(2,1)S(1)}, u32[]{:S(2)}, u32[]{:S(2)}) collective-permute-start(bf16[16,40,128]{2,1,0:T(8,128)(2,1)S(1)} %all_to_all.25.rows_ref), channel_id=1, source_target_pairs={{0,1},{1,0},{2,3},{3,2},{4,5},{5,4},{6,7},{7,6},{8,9},{9,8},{10,11... | collective-permute-start | bytes 491528 | tf_op jit(solution)/shard_map/ppermute | solution.py:337
  36.2 0.6 forward_z_own.1.own_ref
  36.7 0.4 collective-permute-done.rows_ref
  37.2 0.6 forward_z.1
  37.7 14.3 %all_to_all.26.values_ref = bf16[16,72,128]{2,1,0:T(8,128)(2,1)S(1)} all-to-all(bf16[16,72,128]{2,1,0:T(8,128)(2,1)S(1)} %forward_z.1), channel_id=1, replica_groups=mesh['z_lo'=8,'y'=4,'gx_pair'=2,'gx_in'=2,'z_hi'=2,'core'=2] {'gx_pair',..., dimensions={0} | all-to-all | bytes 589824 | tf_op jit(solution)/shard_map/all_to_all | solution.py:333
  52.0 0.0 copy-done.2
  52.0 0.0 copy-start.3
  52.0 0.5 forward_x.1
  52.6 0.0 copy-start.1
  52.6 11.6 %all_to_all.27 = bf16[8,72,512]{2,1,0:T(8,128)(2,1)S(1)} all-to-all(bf16[8,72,512]{2,1,0:T(8,128)(2,1)S(1)} %forward_x.1), channel_id=1, replica_groups=mesh['z_lo'=8,'y'=4,'gx_pair'=2,'gx_in'=2,'z_hi'=2,'core'=2] {'gx_in','y'}, dimensions={0} | all-to-all | bytes 1179648 | tf_op jit(solution)/shard_map/all_to_all | solution.py:333
  64.2 0.0 copy-done.3
  64.2 1.0 modes.1
  65.2 9.7 %all_to_all.28.values_ref = bf16[4,288,256]{2,1,0:T(8,128)(2,1)S(1)} all-to-all(bf16[4,288,256]{2,1,0:T(8,128)(2,1)S(1)} %modes.1), channel_id=1, replica_groups=mesh['z_lo'=8,'y'=4,'gx_pair'=2,'gx_in'=2,'z_hi'=2,'core'=2] {'gx_pair',..., dimensions={0} | all-to-all | bytes 1179648 | tf_op jit(solution)/shard_map/all_to_all | solution.py:333
  74.8 0.0 copy-done.1
  74.8 0.0 copy-start
  74.8 1.4 %inverse_x.1 = bf16[8,96,384]{2,1,0:T(8,128)(2,1)S(1)} custom-call(bf16[4,288,256]{2,1,0:T(8,128)(2,1)S(1)} %all_to_all.28.values_ref, bf16[8,1024,256]{2,1,0:T(8,128)(2,1)S(1)} %copy-done.1), custom_call_target="tpu_custom_call" | custom-call | flops 1208000000 | bytes 5400000 | tf_op jit(solution)/shard_map/inverse_x/pallas_call | solution.py:265
  76.3 17.4 %all_to_all.29 = bf16[8,96,384]{2,1,0:T(8,128)(2,1)S(1)} all-to-all(bf16[8,96,384]{2,1,0:T(8,128)(2,1)S(1)} %inverse_x.1), channel_id=1, replica_groups=mesh['z_lo'=8,'y'=4,'gx_pair'=2,'gx_in'=2,'z_hi'=2,'core'=2] {'core','gx..., dimensions={0} | all-to-all | bytes 1179648 | tf_op jit(solution)/shard_map/all_to_all | solution.py:333
  93.6 0.0 copy-done
  93.6 0.3 inverse_z_far.2
  94.0 3.4 %collective-permute-start.1 = (bf16[192,384]{1,0:T(8,128)(2,1)S(1)}, bf16[192,384]{1,0:T(8,128)(2,1)S(1)}, u32[]{:S(2)}, u32[]{:S(2)}) collective-permute-start(bf16[192,384]{1,0:T(8,128)(2,1)S(1)} %inverse_z_far.2), channel_id=1, source_target_pairs={{0,256},{1,259},{64,320},{65,323},{128,384},{129,387},{192,448},{1... | collective-permute-start | bytes 442376 | tf_op jit(solution)/shard_map/ppermute | solution.py:349
  97.3 0.3 inverse_z_far.3
  97.7 1.9 %collective-permute-start.4 = (bf16[192,384]{1,0:T(8,128)(2,1)S(1)}, bf16[192,384]{1,0:T(8,128)(2,1)S(1)}, u32[]{:S(2)}, u32[]{:S(2)}) collective-permute-start(bf16[192,384]{1,0:T(8,128)(2,1)S(1)} %inverse_z_far.3), channel_id=1, source_target_pairs={{0,256},{1,259},{64,320},{65,323},{128,384},{129,387},{192,448},{1... | collective-permute-start | bytes 442376 | tf_op jit(solution)/shard_map/ppermute | solution.py:349
  99.6 0.5 inverse_z_near.1
  100.1 2.5 %collective-permute-start.3 = (bf16[192,384]{1,0:T(8,128)(2,1)S(1)}, bf16[192,384]{1,0:T(8,128)(2,1)S(1)}, u32[]{:S(2)}, u32[]{:S(2)}) collective-permute-start(bf16[192,384]{1,0:T(8,128)(2,1)S(1)} %get-tuple-element.12), channel_id=1, source_target_pairs={{0,1},{1,0},{2,3},{3,2},{4,5},{5,4},{6,7},{7,6},{8,9},{9,8},{10,11... | collective-permute-start | bytes 442376 | tf_op jit(solution)/shard_map/ppermute | solution.py:337
  102.5 9.9 %collective-permute-done.1 = bf16[192,384]{1,0:T(8,128)(2,1)S(1)} collective-permute-done((bf16[192,384]{1,0:T(8,128)(2,1)S(1)}, bf16[192,384]{1,0:T(8,128)(2,1)S(1)}, u32[]{:S(2)}, u32[]{:S(2)}) %collective-permute-start.1) | collective-permute-done | bytes 147488 | tf_op jit(solution)/shard_map/ppermute | solution.py:349
  112.5 1.9 %collective-permute-start.2 = (bf16[192,384]{1,0:T(8,128)(2,1)S(1)}, bf16[192,384]{1,0:T(8,128)(2,1)S(1)}, u32[]{:S(2)}, u32[]{:S(2)}) collective-permute-start(bf16[192,384]{1,0:T(8,128)(2,1)S(1)} %collective-permute-done.1), channel_id=1, source_target_pairs={{0,256},{1,259},{64,320},{65,323},{128,384},{129,387},{192,448},{1... | collective-permute-start | bytes 442376 | tf_op jit(solution)/shard_map/ppermute | solution.py:349
  114.4 0.3 collective-permute-done.4
  114.6 2.5 %collective-permute-start.5 = (bf16[192,384]{1,0:T(8,128)(2,1)S(1)}, bf16[192,384]{1,0:T(8,128)(2,1)S(1)}, u32[]{:S(2)}, u32[]{:S(2)}) collective-permute-start(bf16[192,384]{1,0:T(8,128)(2,1)S(1)} %collective-permute-done.4), channel_id=1, source_target_pairs={{0,257},{1,258},{64,321},{65,322},{128,385},{129,386},{192,449},{1... | collective-permute-start | bytes 442376 | tf_op jit(solution)/shard_map/ppermute | solution.py:349
  117.2 0.0 collective-permute-done.3.near_ref
  117.2 5.4 %collective-permute-done.2.far_own_ref = bf16[192,384]{1,0:T(8,128)(2,1)S(1)} collective-permute-done((bf16[192,384]{1,0:T(8,128)(2,1)S(1)}, bf16[192,384]{1,0:T(8,128)(2,1)S(1)}, u32[]{:S(2)}, u32[]{:S(2)}) %collective-permute-start.2) | collective-permute-done | bytes 147488 | tf_op jit(solution)/shard_map/ppermute | solution.py:349
  122.6 4.0 %collective-permute-done.5.far_near_ref = bf16[192,384]{1,0:T(8,128)(2,1)S(1)} collective-permute-done((bf16[192,384]{1,0:T(8,128)(2,1)S(1)}, bf16[192,384]{1,0:T(8,128)(2,1)S(1)}, u32[]{:S(2)}, u32[]{:S(2)}) %collective-permute-start.5) | collective-permute-done | bytes 147488 | tf_op jit(solution)/shard_map/ppermute | solution.py:349
  126.6 0.8 finish.1
Async XLA Ops:
  0.0 52.0 %copy-start.2 = (bf16[8,256,512]{2,1,0:T(8,128)(2,1)S(1)}, bf16[8,256,512]{2,1,0:T(8,128)(2,1)}, u32[]{:S(2)}) copy-start(bf16[8,256,512]{2,1,0:T(8,128)(2,1)} %constant.17.clone.table_ref) | copy-start | bytes 6291460
  30.8 6.3 %collective-permute-start = (bf16[16,40,128]{2,1,0:T(8,128)(2,1)S(1)}, bf16[16,40,128]{2,1,0:T(8,128)(2,1)S(1)}, u32[]{:S(2)}, u32[]{:S(2)}) collective-permute-start(bf16[16,40,128]{2,1,0:T(8,128)(2,1)S(1)} %all_to_all.25.rows_ref), channel_id=1, source_target_pairs={{0,1},{1,0},{2,3},{3,2},{4,5},{5,4},{6,7},{7,6},{8,9},{9,8},{10,11... | collective-permute-start | bytes 491528 | tf_op jit(solution)/shard_map/ppermute | solution.py:337
  52.0 12.2 %copy-start.3 = (bf16[2,3,3,1,192,256]{5,4,3,2,1,0:T(8,128)(2,1)S(1)}, bf16[2,3,3,1,192,256]{5,4,3,2,1,0:T(8,128)(2,1)}, u32[]{:S(2)}) copy-start(bf16[2,3,3,1,192,256]{5,4,3,2,1,0:T(8,128)(2,1)} %kernel_ref.1) | copy-start | bytes 5308420
  52.6 22.3 %copy-start.1 = (bf16[8,1024,256]{2,1,0:T(8,128)(2,1)S(1)}, bf16[8,1024,256]{2,1,0:T(8,128)(2,1)}, u32[]{:S(2)}) copy-start(bf16[8,1024,256]{2,1,0:T(8,128)(2,1)} %constant.18.clone.table_ref) | copy-start | bytes 12582916
  74.8 18.8 %copy-start = (bf16[4,192,768]{2,1,0:T(8,128)(2,1)S(1)}, bf16[4,192,768]{2,1,0:T(8,128)(2,1)}, u32[]{:S(2)}) copy-start(bf16[4,192,768]{2,1,0:T(8,128)(2,1)} %constant.19.clone.table_ref) | copy-start | bytes 3538948
  94.0 18.5 %collective-permute-start.1 = (bf16[192,384]{1,0:T(8,128)(2,1)S(1)}, bf16[192,384]{1,0:T(8,128)(2,1)S(1)}, u32[]{:S(2)}, u32[]{:S(2)}) collective-permute-start(bf16[192,384]{1,0:T(8,128)(2,1)S(1)} %inverse_z_far.2), channel_id=1, source_target_pairs={{0,256},{1,259},{64,320},{65,323},{128,384},{129,387},{192,448},{1... | collective-permute-start | bytes 442376 | tf_op jit(solution)/shard_map/ppermute | solution.py:349
  97.7 17.0 %collective-permute-start.4 = (bf16[192,384]{1,0:T(8,128)(2,1)S(1)}, bf16[192,384]{1,0:T(8,128)(2,1)S(1)}, u32[]{:S(2)}, u32[]{:S(2)}) collective-permute-start(bf16[192,384]{1,0:T(8,128)(2,1)S(1)} %inverse_z_far.3), channel_id=1, source_target_pairs={{0,256},{1,259},{64,320},{65,323},{128,384},{129,387},{192,448},{1... | collective-permute-start | bytes 442376 | tf_op jit(solution)/shard_map/ppermute | solution.py:349
  100.1 17.1 %collective-permute-start.3 = (bf16[192,384]{1,0:T(8,128)(2,1)S(1)}, bf16[192,384]{1,0:T(8,128)(2,1)S(1)}, u32[]{:S(2)}, u32[]{:S(2)}) collective-permute-start(bf16[192,384]{1,0:T(8,128)(2,1)S(1)} %get-tuple-element.12), channel_id=1, source_target_pairs={{0,1},{1,0},{2,3},{3,2},{4,5},{5,4},{6,7},{7,6},{8,9},{9,8},{10,11... | collective-permute-start | bytes 442376 | tf_op jit(solution)/shard_map/ppermute | solution.py:337
  112.5 10.1 %collective-permute-start.2 = (bf16[192,384]{1,0:T(8,128)(2,1)S(1)}, bf16[192,384]{1,0:T(8,128)(2,1)S(1)}, u32[]{:S(2)}, u32[]{:S(2)}) collective-permute-start(bf16[192,384]{1,0:T(8,128)(2,1)S(1)} %collective-permute-done.1), channel_id=1, source_target_pairs={{0,256},{1,259},{64,320},{65,323},{128,384},{129,387},{192,448},{1... | collective-permute-start | bytes 442376 | tf_op jit(solution)/shard_map/ppermute | solution.py:349
  114.6 12.0 %collective-permute-start.5 = (bf16[192,384]{1,0:T(8,128)(2,1)S(1)}, bf16[192,384]{1,0:T(8,128)(2,1)S(1)}, u32[]{:S(2)}, u32[]{:S(2)}) collective-permute-start(bf16[192,384]{1,0:T(8,128)(2,1)S(1)} %collective-permute-done.4), channel_id=1, source_target_pairs={{0,257},{1,258},{64,321},{65,322},{128,385},{129,386},{192,449},{1... | collective-permute-start | bytes 442376 | tf_op jit(solution)/shard_map/ppermute | solution.py:349

commit v7 on v6

--- a/solution.py
+++ b/solution.py
@@ -301,7 +301,7 @@
     )(me, values, table)
 
 
-def finish_body(core_ref, own_ref, far_own_ref, near_ref, far_near_ref, out_ref):
+def finish_body(core_ref, near_ref, far_near_ref, own_ref, far_own_ref, out_ref):
     own = own_ref[...].astype(jnp.float32) + far_own_ref[...].astype(jnp.float32)
     near = near_ref[...].astype(jnp.float32) + far_near_ref[...].astype(jnp.float32)
     first = core_ref[0] == 0
@@ -312,7 +312,7 @@
         out_ref[o, 0, :, 128:256] = right[:, o * 128 : (o + 1) * 128]
 
 
-def finish_call(core, own, far_own, near, far_near):
+def finish_call(core, near, far_near, own, far_own):
     block = pl.BlockSpec((NQ, 384), lambda j, s: (0, 0))
     return pl.pallas_call(
         finish_body,
@@ -326,7 +326,7 @@
         compiler_params=pltpu.CompilerParams(vmem_limit_bytes=VMEM),
         cost_estimate=pl.CostEstimate(flops=150000, bytes_accessed=900000, transcendentals=0),
         name="finish",
-    )(core, own, far_own, near, far_near)
+    )(core, near, far_near, own, far_own)
 
 
 def exchange(values, axis):
@@ -364,13 +364,13 @@
     planes = exchange(inverse_x_call(modes, jnp.asarray(inverse_x_table())), ("core", "gx_pair", "gx_in"))
     planes = planes.reshape(NZ, 384)
     z_table = jnp.asarray(inverse_z_table())
+    (to_far_near,) = inverse_z_call(gz, planes, z_table, (3,))
     (to_far,) = inverse_z_call(gz, planes, z_table, (2,))
-    (to_far_near,) = inverse_z_call(gz, planes, z_table, (3,))
     own, to_near = inverse_z_call(gz, planes, z_table, (0, 1))
+    far_near = move_z(move_z(to_far_near, 4, 0), 4, 1)
     far_own = move_z(move_z(to_far, 4, 0), 4, 0)
-    far_near = move_z(move_z(to_far_near, 4, 0), 4, 1)
     near = swap_cores(to_near)
-    return finish_call(core.reshape(1).astype(jnp.int32), own, far_own, near, far_near)
+    return finish_call(core.reshape(1).astype(jnp.int32), near, far_near, own, far_own)
 
 
 def solution(mesh):

time: 129 us -> 130 us (level)
  starting transfers between devices: 17.5 us -> 18.9 us
    ppermute x4, starting transfers between devices: 9.69 us -> 11.1 us  [move_z(): return lax.ppermute(values, ('z_lo', 'z_hi', 'core'), perm)]
  transfers between devices with their start and end apart: 6 -> 6, of which waited for: 5 -> 4; matrix products, arithmetic and copies ran while one was open for 0% -> 0% of each run, Pallas kernels for 1% -> 1%
where the time goes in v7:
time: 130 us; the launch traced here: 129 us
  blocking collectives  82.6 us (64%)
  waiting for transfers between devices  19.7 us (15%)
  starting transfers between devices  18.9 us (15%)
  Pallas kernels  7.1 us (5%)
    all_to_all x5, blocking collectives, exchange(): return lax.all_to_all(values, axis, split_axis=0, concat_axis=0, tiled=True)  82.6 us
    ppermute x4, waiting for transfers between devices, move_z(): return lax.ppermute(values, ('z_lo', 'z_hi', 'core'), perm)  19.3 us
    ppermute x4, starting transfers between devices, move_z(): return lax.ppermute(values, ('z_lo', 'z_hi', 'core'), perm)  11.1 us
    ppermute x2, starting transfers between devices, swap_cores(): return lax.ppermute(values, 'core', [(0, 1), (1, 0)])  7.81 us
  transfers between devices with their start and end apart: 6, of which 4 were waited for; matrix products, arithmetic and copies ran while one was open for 0% of the time, Pallas kernels for 1%

profile of v7, /device:TPU:1, one launch (start us, length us, event | category | flops | bytes accessed | tf_op | source)
XLA Modules:
  0.0 128.5 jit_solution(3468349424529549449)
XLA Ops:
  0.0 0.0 copy-start.2
  0.0 1.1 pack.1
  1.2 29.7 %all_to_all.25.rows_ref = bf16[16,40,128]{2,1,0:T(8,128)(2,1)S(1)} all-to-all(bf16[16,40,128]{2,1,0:T(8,128)(2,1)S(1)} %get-tuple-element.9), channel_id=1, replica_groups=mesh['z_lo'=8,'y'=4,'gx_pair'=2,'gx_in'=2,'z_hi'=2,'core'=2] {'z_lo','z_..., dimensions={0} | all-to-all | bytes 327680 | tf_op jit(solution)/shard_map/all_to_all | solution.py:333
  30.8 5.3 %collective-permute-start = (bf16[16,40,128]{2,1,0:T(8,128)(2,1)S(1)}, bf16[16,40,128]{2,1,0:T(8,128)(2,1)S(1)}, u32[]{:S(2)}, u32[]{:S(2)}) collective-permute-start(bf16[16,40,128]{2,1,0:T(8,128)(2,1)S(1)} %all_to_all.25.rows_ref), channel_id=1, source_target_pairs={{0,1},{1,0},{2,3},{3,2},{4,5},{5,4},{6,7},{7,6},{8,9},{9,8},{10,11... | collective-permute-start | bytes 491528 | tf_op jit(solution)/shard_map/ppermute | solution.py:337
  36.2 0.6 forward_z_own.1.own_ref
  36.7 0.4 collective-permute-done.rows_ref
  37.2 0.6 forward_z.1
  37.7 14.3 %all_to_all.26.values_ref = bf16[16,72,128]{2,1,0:T(8,128)(2,1)S(1)} all-to-all(bf16[16,72,128]{2,1,0:T(8,128)(2,1)S(1)} %forward_z.1), channel_id=1, replica_groups=mesh['z_lo'=8,'y'=4,'gx_pair'=2,'gx_in'=2,'z_hi'=2,'core'=2] {'gx_pair',..., dimensions={0} | all-to-all | bytes 589824 | tf_op jit(solution)/shard_map/all_to_all | solution.py:333
  52.0 0.0 copy-done.2
  52.0 0.0 copy-start.3
  52.0 0.5 forward_x.1
  52.6 0.0 copy-start.1
  52.6 11.6 %all_to_all.27 = bf16[8,72,512]{2,1,0:T(8,128)(2,1)S(1)} all-to-all(bf16[8,72,512]{2,1,0:T(8,128)(2,1)S(1)} %forward_x.1), channel_id=1, replica_groups=mesh['z_lo'=8,'y'=4,'gx_pair'=2,'gx_in'=2,'z_hi'=2,'core'=2] {'gx_in','y'}, dimensions={0} | all-to-all | bytes 1179648 | tf_op jit(solution)/shard_map/all_to_all | solution.py:333
  64.2 0.0 copy-done.3
  64.2 1.0 modes.1
  65.2 9.7 %all_to_all.28.values_ref = bf16[4,288,256]{2,1,0:T(8,128)(2,1)S(1)} all-to-all(bf16[4,288,256]{2,1,0:T(8,128)(2,1)S(1)} %modes.1), channel_id=1, replica_groups=mesh['z_lo'=8,'y'=4,'gx_pair'=2,'gx_in'=2,'z_hi'=2,'core'=2] {'gx_pair',..., dimensions={0} | all-to-all | bytes 1179648 | tf_op jit(solution)/shard_map/all_to_all | solution.py:333
  74.8 0.0 copy-done.1
  74.8 0.0 copy-start
  74.8 1.4 %inverse_x.1 = bf16[8,96,384]{2,1,0:T(8,128)(2,1)S(1)} custom-call(bf16[4,288,256]{2,1,0:T(8,128)(2,1)S(1)} %all_to_all.28.values_ref, bf16[8,1024,256]{2,1,0:T(8,128)(2,1)S(1)} %copy-done.1), custom_call_target="tpu_custom_call" | custom-call | flops 1208000000 | bytes 5400000 | tf_op jit(solution)/shard_map/inverse_x/pallas_call | solution.py:265
  76.3 17.4 %all_to_all.29 = bf16[8,96,384]{2,1,0:T(8,128)(2,1)S(1)} all-to-all(bf16[8,96,384]{2,1,0:T(8,128)(2,1)S(1)} %inverse_x.1), channel_id=1, replica_groups=mesh['z_lo'=8,'y'=4,'gx_pair'=2,'gx_in'=2,'z_hi'=2,'core'=2] {'core','gx..., dimensions={0} | all-to-all | bytes 1179648 | tf_op jit(solution)/shard_map/all_to_all | solution.py:333
  93.6 0.0 copy-done
  93.6 0.3 inverse_z_far.2
  94.0 3.4 %collective-permute-start.2 = (bf16[192,384]{1,0:T(8,128)(2,1)S(1)}, bf16[192,384]{1,0:T(8,128)(2,1)S(1)}, u32[]{:S(2)}, u32[]{:S(2)}) collective-permute-start(bf16[192,384]{1,0:T(8,128)(2,1)S(1)} %inverse_z_far.2), channel_id=1, source_target_pairs={{0,256},{1,259},{64,320},{65,323},{128,384},{129,387},{192,448},{1... | collective-permute-start | bytes 442376 | tf_op jit(solution)/shard_map/ppermute | solution.py:349
  97.3 0.3 inverse_z_far.3
  97.7 1.9 %collective-permute-start.4 = (bf16[192,384]{1,0:T(8,128)(2,1)S(1)}, bf16[192,384]{1,0:T(8,128)(2,1)S(1)}, u32[]{:S(2)}, u32[]{:S(2)}) collective-permute-start(bf16[192,384]{1,0:T(8,128)(2,1)S(1)} %inverse_z_far.3), channel_id=1, source_target_pairs={{0,256},{1,259},{64,320},{65,323},{128,384},{129,387},{192,448},{1... | collective-permute-start | bytes 442376 | tf_op jit(solution)/shard_map/ppermute | solution.py:349
  99.6 0.5 inverse_z_near.1
  100.1 2.5 %collective-permute-start.1 = (bf16[192,384]{1,0:T(8,128)(2,1)S(1)}, bf16[192,384]{1,0:T(8,128)(2,1)S(1)}, u32[]{:S(2)}, u32[]{:S(2)}) collective-permute-start(bf16[192,384]{1,0:T(8,128)(2,1)S(1)} %get-tuple-element.11), channel_id=1, source_target_pairs={{0,1},{1,0},{2,3},{3,2},{4,5},{5,4},{6,7},{7,6},{8,9},{9,8},{10,11... | collective-permute-start | bytes 442376 | tf_op jit(solution)/shard_map/ppermute | solution.py:337
  102.5 9.9 %collective-permute-done.2 = bf16[192,384]{1,0:T(8,128)(2,1)S(1)} collective-permute-done((bf16[192,384]{1,0:T(8,128)(2,1)S(1)}, bf16[192,384]{1,0:T(8,128)(2,1)S(1)}, u32[]{:S(2)}, u32[]{:S(2)}) %collective-permute-start.2) | collective-permute-done | bytes 147488 | tf_op jit(solution)/shard_map/ppermute | solution.py:349
  112.4 2.5 %collective-permute-start.3 = (bf16[192,384]{1,0:T(8,128)(2,1)S(1)}, bf16[192,384]{1,0:T(8,128)(2,1)S(1)}, u32[]{:S(2)}, u32[]{:S(2)}) collective-permute-start(bf16[192,384]{1,0:T(8,128)(2,1)S(1)} %collective-permute-done.2), channel_id=1, source_target_pairs={{0,257},{1,258},{64,321},{65,322},{128,385},{129,386},{192,449},{1... | collective-permute-start | bytes 442376 | tf_op jit(solution)/shard_map/ppermute | solution.py:349
  114.9 0.0 collective-permute-done.4
  114.9 3.3 %collective-permute-start.5 = (bf16[192,384]{1,0:T(8,128)(2,1)S(1)}, bf16[192,384]{1,0:T(8,128)(2,1)S(1)}, u32[]{:S(2)}, u32[]{:S(2)}) collective-permute-start(bf16[192,384]{1,0:T(8,128)(2,1)S(1)} %collective-permute-done.4), channel_id=1, source_target_pairs={{0,256},{1,259},{64,320},{65,323},{128,384},{129,387},{192,448},{1... | collective-permute-start | bytes 442376 | tf_op jit(solution)/shard_map/ppermute | solution.py:349
  118.3 0.0 collective-permute-done.1.near_ref
  118.3 6.3 %collective-permute-done.3.far_near_ref = bf16[192,384]{1,0:T(8,128)(2,1)S(1)} collective-permute-done((bf16[192,384]{1,0:T(8,128)(2,1)S(1)}, bf16[192,384]{1,0:T(8,128)(2,1)S(1)}, u32[]{:S(2)}, u32[]{:S(2)}) %collective-permute-start.3) | collective-permute-done | bytes 147488 | tf_op jit(solution)/shard_map/ppermute | solution.py:349
  124.6 3.1 %collective-permute-done.5.far_own_ref = bf16[192,384]{1,0:T(8,128)(2,1)S(1)} collective-permute-done((bf16[192,384]{1,0:T(8,128)(2,1)S(1)}, bf16[192,384]{1,0:T(8,128)(2,1)S(1)}, u32[]{:S(2)}, u32[]{:S(2)}) %collective-permute-start.5) | collective-permute-done | bytes 147488 | tf_op jit(solution)/shard_map/ppermute | solution.py:349
  127.7 0.8 finish.1
Async XLA Ops:
  0.0 52.0 %copy-start.2 = (bf16[8,256,512]{2,1,0:T(8,128)(2,1)S(1)}, bf16[8,256,512]{2,1,0:T(8,128)(2,1)}, u32[]{:S(2)}) copy-start(bf16[8,256,512]{2,1,0:T(8,128)(2,1)} %constant.17.clone.table_ref) | copy-start | bytes 6291460
  30.8 6.3 %collective-permute-start = (bf16[16,40,128]{2,1,0:T(8,128)(2,1)S(1)}, bf16[16,40,128]{2,1,0:T(8,128)(2,1)S(1)}, u32[]{:S(2)}, u32[]{:S(2)}) collective-permute-start(bf16[16,40,128]{2,1,0:T(8,128)(2,1)S(1)} %all_to_all.25.rows_ref), channel_id=1, source_target_pairs={{0,1},{1,0},{2,3},{3,2},{4,5},{5,4},{6,7},{7,6},{8,9},{9,8},{10,11... | collective-permute-start | bytes 491528 | tf_op jit(solution)/shard_map/ppermute | solution.py:337
  52.0 12.2 %copy-start.3 = (bf16[2,3,3,1,192,256]{5,4,3,2,1,0:T(8,128)(2,1)S(1)}, bf16[2,3,3,1,192,256]{5,4,3,2,1,0:T(8,128)(2,1)}, u32[]{:S(2)}) copy-start(bf16[2,3,3,1,192,256]{5,4,3,2,1,0:T(8,128)(2,1)} %kernel_ref.1) | copy-start | bytes 5308420
  52.6 22.3 %copy-start.1 = (bf16[8,1024,256]{2,1,0:T(8,128)(2,1)S(1)}, bf16[8,1024,256]{2,1,0:T(8,128)(2,1)}, u32[]{:S(2)}) copy-start(bf16[8,1024,256]{2,1,0:T(8,128)(2,1)} %constant.18.clone.table_ref) | copy-start | bytes 12582916
  74.8 18.8 %copy-start = (bf16[4,192,768]{2,1,0:T(8,128)(2,1)S(1)}, bf16[4,192,768]{2,1,0:T(8,128)(2,1)}, u32[]{:S(2)}) copy-start(bf16[4,192,768]{2,1,0:T(8,128)(2,1)} %constant.19.clone.table_ref) | copy-start | bytes 3538948
  94.0 18.5 %collective-permute-start.2 = (bf16[192,384]{1,0:T(8,128)(2,1)S(1)}, bf16[192,384]{1,0:T(8,128)(2,1)S(1)}, u32[]{:S(2)}, u32[]{:S(2)}) collective-permute-start(bf16[192,384]{1,0:T(8,128)(2,1)S(1)} %inverse_z_far.2), channel_id=1, source_target_pairs={{0,256},{1,259},{64,320},{65,323},{128,384},{129,387},{192,448},{1... | collective-permute-start | bytes 442376 | tf_op jit(solution)/shard_map/ppermute | solution.py:349
  97.7 17.3 %collective-permute-start.4 = (bf16[192,384]{1,0:T(8,128)(2,1)S(1)}, bf16[192,384]{1,0:T(8,128)(2,1)S(1)}, u32[]{:S(2)}, u32[]{:S(2)}) collective-permute-start(bf16[192,384]{1,0:T(8,128)(2,1)S(1)} %inverse_z_far.3), channel_id=1, source_target_pairs={{0,256},{1,259},{64,320},{65,323},{128,384},{129,387},{192,448},{1... | collective-permute-start | bytes 442376 | tf_op jit(solution)/shard_map/ppermute | solution.py:349
  100.1 18.2 %collective-permute-start.1 = (bf16[192,384]{1,0:T(8,128)(2,1)S(1)}, bf16[192,384]{1,0:T(8,128)(2,1)S(1)}, u32[]{:S(2)}, u32[]{:S(2)}) collective-permute-start(bf16[192,384]{1,0:T(8,128)(2,1)S(1)} %get-tuple-element.11), channel_id=1, source_target_pairs={{0,1},{1,0},{2,3},{3,2},{4,5},{5,4},{6,7},{7,6},{8,9},{9,8},{10,11... | collective-permute-start | bytes 442376 | tf_op jit(solution)/shard_map/ppermute | solution.py:337
  112.4 12.2 %collective-permute-start.3 = (bf16[192,384]{1,0:T(8,128)(2,1)S(1)}, bf16[192,384]{1,0:T(8,128)(2,1)S(1)}, u32[]{:S(2)}, u32[]{:S(2)}) collective-permute-start(bf16[192,384]{1,0:T(8,128)(2,1)S(1)} %collective-permute-done.2), channel_id=1, source_target_pairs={{0,257},{1,258},{64,321},{65,322},{128,385},{129,386},{192,449},{1... | collective-permute-start | bytes 442376 | tf_op jit(solution)/shard_map/ppermute | solution.py:349
  114.9 12.8 %collective-permute-start.5 = (bf16[192,384]{1,0:T(8,128)(2,1)S(1)}, bf16[192,384]{1,0:T(8,128)(2,1)S(1)}, u32[]{:S(2)}, u32[]{:S(2)}) collective-permute-start(bf16[192,384]{1,0:T(8,128)(2,1)S(1)} %collective-permute-done.4), channel_id=1, source_target_pairs={{0,256},{1,259},{64,320},{65,323},{128,384},{129,387},{192,448},{1... | collective-permute-start | bytes 442376 | tf_op jit(solution)/shard_map/ppermute | solution.py:349

commit v8 on v6

--- a/solution.py
+++ b/solution.py
@@ -276,13 +276,21 @@
     values = values_ref[...]
     odd = (lax.broadcasted_iota(jnp.int32, (NQ, 384), 0) * (me // 2)) % 2
     scale = jnp.where(odd == 1, -1.0, 1.0) * (1.0 / math.sqrt(NZ))
-    for k, out_ref in zip(steps, out_refs):
+    for i, k in enumerate(steps):
         total = jnp.dot(table_ref[me ^ k], values, preferred_element_type=jnp.float32)
-        out_ref[...] = (total * scale).astype(out_ref.dtype)
-
-
-def inverse_z_call(me, values, table, steps):
-    block = pl.BlockSpec((NQ, 384), lambda j, s: (0, 0))
+        total = (total * scale).astype(jnp.bfloat16)
+        if len(out_refs) == len(steps):
+            out_refs[i][...] = total
+        else:
+            out_refs[0][i] = total
+
+
+def inverse_z_call(me, values, table, steps, stacked=False):
+    if stacked:
+        shapes = [(len(steps), NQ, 384)]
+    else:
+        shapes = [(NQ, 384)] * len(steps)
+    blocks = [pl.BlockSpec(shape, lambda j, s, n=len(shape): (0,) * n) for shape in shapes]
     return pl.pallas_call(
         functools.partial(inverse_z_body, steps),
         grid_spec=pltpu.PrefetchScalarGridSpec(
@@ -292,9 +300,9 @@
                 pl.BlockSpec((NZ, 384), lambda j, s: (0, 0)),
                 pl.BlockSpec((4, NQ, NZ), lambda j, s: (0, 0, 0)),
             ],
-            out_specs=[block] * len(steps),
+            out_specs=blocks,
         ),
-        out_shape=[jax.ShapeDtypeStruct((NQ, 384), jnp.bfloat16) for _ in steps],
+        out_shape=[jax.ShapeDtypeStruct(shape, jnp.bfloat16) for shape in shapes],
         compiler_params=pltpu.CompilerParams(vmem_limit_bytes=VMEM),
         cost_estimate=pl.CostEstimate(flops=227000000, bytes_accessed=2000000, transcendentals=0),
         name="inverse_z_far" if steps[0] else "inverse_z_near",
@@ -364,11 +372,11 @@
     planes = exchange(inverse_x_call(modes, jnp.asarray(inverse_x_table())), ("core", "gx_pair", "gx_in"))
     planes = planes.reshape(NZ, 384)
     z_table = jnp.asarray(inverse_z_table())
-    (to_far,) = inverse_z_call(gz, planes, z_table, (2,))
-    (to_far_near,) = inverse_z_call(gz, planes, z_table, (3,))
+    (to_far,) = inverse_z_call(gz, planes, z_table, (2, 3), True)
     own, to_near = inverse_z_call(gz, planes, z_table, (0, 1))
-    far_own = move_z(move_z(to_far, 4, 0), 4, 0)
-    far_near = move_z(move_z(to_far_near, 4, 0), 4, 1)
+    half = move_z(to_far, 4, 0)
+    far_own = move_z(half[0], 4, 0)
+    far_near = move_z(half[1], 4, 1)
     near = swap_cores(to_near)
     return finish_call(core.reshape(1).astype(jnp.int32), own, far_own, near, far_near)
 

time: 129 us -> 134 us (1.039); the launches traced: 127 us -> 134 us
  waiting for transfers between devices: 20.1 us -> 26 us
    ppermute x4 -> x3, waiting for transfers between devices: 19.6 us -> 25.5 us  [move_z(): return lax.ppermute(values, ('z_lo', 'z_hi', 'core'), perm)]
    ppermute x4 -> x3, starting transfers between devices: 9.69 us -> 11 us  [move_z(): return lax.ppermute(values, ('z_lo', 'z_hi', 'core'), perm)]
  transfers between devices with their start and end apart: 6 -> 5, of which waited for: 5 -> 4; matrix products, arithmetic and copies ran while one was open for 0% -> 0% of each run, Pallas kernels for 1% -> 1%
where the time goes in v8:
time: 134 us
  blocking collectives  82.6 us (62%)
  waiting for transfers between devices  26 us (19%)
  starting transfers between devices  18.2 us (14%)
  Pallas kernels  6.94 us (5%)
    all_to_all x5, blocking collectives, exchange(): return lax.all_to_all(values, axis, split_axis=0, concat_axis=0, tiled=True)  82.6 us
    ppermute x3, waiting for transfers between devices, move_z(): return lax.ppermute(values, ('z_lo', 'z_hi', 'core'), perm)  25.5 us
    ppermute x3, starting transfers between devices, move_z(): return lax.ppermute(values, ('z_lo', 'z_hi', 'core'), perm)  11 us
    ppermute x2, starting transfers between devices, swap_cores(): return lax.ppermute(values, 'core', [(0, 1), (1, 0)])  7.26 us
  transfers between devices with their start and end apart: 5, of which 4 were waited for; matrix products, arithmetic and copies ran while one was open for 0% of the time, Pallas kernels for 1%

profile of v8, /device:TPU:1, one launch (start us, length us, event | category | flops | bytes accessed | tf_op | source)
XLA Modules:
  0.0 133.9 jit_solution(1736600042545036869)
XLA Ops:
  0.0 0.0 copy-start.2
  0.0 1.1 pack.1
  1.2 29.7 %all_to_all.25.rows_ref = bf16[16,40,128]{2,1,0:T(8,128)(2,1)S(1)} all-to-all(bf16[16,40,128]{2,1,0:T(8,128)(2,1)S(1)} %get-tuple-element.9), channel_id=1, replica_groups=mesh['z_lo'=8,'y'=4,'gx_pair'=2,'gx_in'=2,'z_hi'=2,'core'=2] {'z_lo','z_..., dimensions={0} | all-to-all | bytes 327680 | tf_op jit(solution)/shard_map/all_to_all | solution.py:341
  30.8 5.3 %collective-permute-start = (bf16[16,40,128]{2,1,0:T(8,128)(2,1)S(1)}, bf16[16,40,128]{2,1,0:T(8,128)(2,1)S(1)}, u32[]{:S(2)}, u32[]{:S(2)}) collective-permute-start(bf16[16,40,128]{2,1,0:T(8,128)(2,1)S(1)} %all_to_all.25.rows_ref), channel_id=1, source_target_pairs={{0,1},{1,0},{2,3},{3,2},{4,5},{5,4},{6,7},{7,6},{8,9},{9,8},{10,11... | collective-permute-start | bytes 491528 | tf_op jit(solution)/shard_map/ppermute | solution.py:345
  36.2 0.6 forward_z_own.1.own_ref
  36.7 0.4 collective-permute-done.rows_ref
  37.2 0.6 forward_z.1
  37.7 14.3 %all_to_all.26.values_ref = bf16[16,72,128]{2,1,0:T(8,128)(2,1)S(1)} all-to-all(bf16[16,72,128]{2,1,0:T(8,128)(2,1)S(1)} %forward_z.1), channel_id=1, replica_groups=mesh['z_lo'=8,'y'=4,'gx_pair'=2,'gx_in'=2,'z_hi'=2,'core'=2] {'gx_pair',..., dimensions={0} | all-to-all | bytes 589824 | tf_op jit(solution)/shard_map/all_to_all | solution.py:341
  52.0 0.0 copy-done.2
  52.0 0.0 copy-start.3
  52.0 0.5 forward_x.1
  52.6 0.0 copy-start.1
  52.6 11.6 %all_to_all.27 = bf16[8,72,512]{2,1,0:T(8,128)(2,1)S(1)} all-to-all(bf16[8,72,512]{2,1,0:T(8,128)(2,1)S(1)} %forward_x.1), channel_id=1, replica_groups=mesh['z_lo'=8,'y'=4,'gx_pair'=2,'gx_in'=2,'z_hi'=2,'core'=2] {'gx_in','y'}, dimensions={0} | all-to-all | bytes 1179648 | tf_op jit(solution)/shard_map/all_to_all | solution.py:341
  64.2 0.0 copy-done.3
  64.2 1.0 modes.1
  65.2 9.7 %all_to_all.28.values_ref = bf16[4,288,256]{2,1,0:T(8,128)(2,1)S(1)} all-to-all(bf16[4,288,256]{2,1,0:T(8,128)(2,1)S(1)} %modes.1), channel_id=1, replica_groups=mesh['z_lo'=8,'y'=4,'gx_pair'=2,'gx_in'=2,'z_hi'=2,'core'=2] {'gx_pair',..., dimensions={0} | all-to-all | bytes 1179648 | tf_op jit(solution)/shard_map/all_to_all | solution.py:341
  74.8 0.0 copy-done.1
  74.8 0.0 copy-start
  74.8 1.4 %inverse_x.1 = bf16[8,96,384]{2,1,0:T(8,128)(2,1)S(1)} custom-call(bf16[4,288,256]{2,1,0:T(8,128)(2,1)S(1)} %all_to_all.28.values_ref, bf16[8,1024,256]{2,1,0:T(8,128)(2,1)S(1)} %copy-done.1), custom_call_target="tpu_custom_call" | custom-call | flops 1208000000 | bytes 5400000 | tf_op jit(solution)/shard_map/inverse_x/pallas_call | solution.py:265
  76.3 17.4 %all_to_all.29 = bf16[8,96,384]{2,1,0:T(8,128)(2,1)S(1)} all-to-all(bf16[8,96,384]{2,1,0:T(8,128)(2,1)S(1)} %inverse_x.1), channel_id=1, replica_groups=mesh['z_lo'=8,'y'=4,'gx_pair'=2,'gx_in'=2,'z_hi'=2,'core'=2] {'core','gx..., dimensions={0} | all-to-all | bytes 1179648 | tf_op jit(solution)/shard_map/all_to_all | solution.py:341
  93.6 0.0 copy-done
  93.6 0.5 inverse_z_far.1
  94.1 3.4 %collective-permute-start.1 = (bf16[2,192,384]{2,1,0:T(8,128)(2,1)S(1)}, bf16[2,192,384]{2,1,0:T(8,128)(2,1)S(1)}, u32[]{:S(2)}, u32[]{:S(2)}) collective-permute-start(bf16[2,192,384]{2,1,0:T(8,128)(2,1)S(1)} %inverse_z_far.1), channel_id=1, source_target_pairs={{0,256},{1,259},{64,320},{65,323},{128,384},{129,387},{192,448},{1... | collective-permute-start | bytes 884744 | tf_op jit(solution)/shard_map/ppermute | solution.py:357
  97.5 0.5 inverse_z_near.1
  98.0 1.9 %collective-permute-start.3 = (bf16[192,384]{1,0:T(8,128)(2,1)S(1)}, bf16[192,384]{1,0:T(8,128)(2,1)S(1)}, u32[]{:S(2)}, u32[]{:S(2)}) collective-permute-start(bf16[192,384]{1,0:T(8,128)(2,1)S(1)} %get-tuple-element.12), channel_id=1, source_target_pairs={{0,1},{1,0},{2,3},{3,2},{4,5},{5,4},{6,7},{7,6},{8,9},{9,8},{10,11... | collective-permute-start | bytes 442376 | tf_op jit(solution)/shard_map/ppermute | solution.py:345
  99.9 14.2 %collective-permute-done.1 = bf16[2,192,384]{2,1,0:T(8,128)(2,1)S(1)} collective-permute-done((bf16[2,192,384]{2,1,0:T(8,128)(2,1)S(1)}, bf16[2,192,384]{2,1,0:T(8,128)(2,1)S(1)}, u32[]{:S(2)}, u32[]{:S(2)}) %collective-permute-start.1) | collective-permute-done | bytes 294944 | tf_op jit(solution)/shard_map/ppermute | solution.py:357
  114.1 5.7 %collective-permute-start.4 = (bf16[192,384]{1,0:T(8,128)(2,1)S(1)}, bf16[192,384]{1,0:T(8,128)(2,1)S(1)}, u32[]{:S(2)}, u32[]{:S(2)}) collective-permute-start(bf16[192,384]{1,0:T(8,128)(2,1)S(1)} %get-tuple-element.13), channel_id=1, source_target_pairs={{0,257},{1,258},{64,321},{65,322},{128,385},{129,386},{192,449},{1... | collective-permute-start | bytes 442376 | tf_op jit(solution)/shard_map/ppermute | solution.py:357
  119.8 1.9 %collective-permute-start.2 = (bf16[192,384]{1,0:T(8,128)(2,1)S(1)}, bf16[192,384]{1,0:T(8,128)(2,1)S(1)}, u32[]{:S(2)}, u32[]{:S(2)}) collective-permute-start(bf16[192,384]{1,0:T(8,128)(2,1)S(1)} %get-tuple-element.14), channel_id=1, source_target_pairs={{0,256},{1,259},{64,320},{65,323},{128,384},{129,387},{192,448},{1... | collective-permute-start | bytes 442376 | tf_op jit(solution)/shard_map/ppermute | solution.py:357
  121.7 0.0 collective-permute-done.3.near_ref
  121.8 5.5 %collective-permute-done.4.far_near_ref = bf16[192,384]{1,0:T(8,128)(2,1)S(1)} collective-permute-done((bf16[192,384]{1,0:T(8,128)(2,1)S(1)}, bf16[192,384]{1,0:T(8,128)(2,1)S(1)}, u32[]{:S(2)}, u32[]{:S(2)}) %collective-permute-start.4) | collective-permute-done | bytes 147488 | tf_op jit(solution)/shard_map/ppermute | solution.py:357
  127.2 5.9 %collective-permute-done.2.far_own_ref = bf16[192,384]{1,0:T(8,128)(2,1)S(1)} collective-permute-done((bf16[192,384]{1,0:T(8,128)(2,1)S(1)}, bf16[192,384]{1,0:T(8,128)(2,1)S(1)}, u32[]{:S(2)}, u32[]{:S(2)}) %collective-permute-start.2) | collective-permute-done | bytes 147488 | tf_op jit(solution)/shard_map/ppermute | solution.py:357
  133.1 0.8 finish.1
  (1 shorter events, 0.0 us)
Async XLA Ops:
  0.0 52.0 %copy-start.2 = (bf16[8,256,512]{2,1,0:T(8,128)(2,1)S(1)}, bf16[8,256,512]{2,1,0:T(8,128)(2,1)}, u32[]{:S(2)}) copy-start(bf16[8,256,512]{2,1,0:T(8,128)(2,1)} %constant.17.clone.table_ref) | copy-start | bytes 6291460
  30.8 6.3 %collective-permute-start = (bf16[16,40,128]{2,1,0:T(8,128)(2,1)S(1)}, bf16[16,40,128]{2,1,0:T(8,128)(2,1)S(1)}, u32[]{:S(2)}, u32[]{:S(2)}) collective-permute-start(bf16[16,40,128]{2,1,0:T(8,128)(2,1)S(1)} %all_to_all.25.rows_ref), channel_id=1, source_target_pairs={{0,1},{1,0},{2,3},{3,2},{4,5},{5,4},{6,7},{7,6},{8,9},{9,8},{10,11... | collective-permute-start | bytes 491528 | tf_op jit(solution)/shard_map/ppermute | solution.py:345
  52.0 12.2 %copy-start.3 = (bf16[2,3,3,1,192,256]{5,4,3,2,1,0:T(8,128)(2,1)S(1)}, bf16[2,3,3,1,192,256]{5,4,3,2,1,0:T(8,128)(2,1)}, u32[]{:S(2)}) copy-start(bf16[2,3,3,1,192,256]{5,4,3,2,1,0:T(8,128)(2,1)} %kernel_ref.1) | copy-start | bytes 5308420
  52.6 22.3 %copy-start.1 = (bf16[8,1024,256]{2,1,0:T(8,128)(2,1)S(1)}, bf16[8,1024,256]{2,1,0:T(8,128)(2,1)}, u32[]{:S(2)}) copy-start(bf16[8,1024,256]{2,1,0:T(8,128)(2,1)} %constant.18.clone.table_ref) | copy-start | bytes 12582916
  74.8 18.8 %copy-start = (bf16[4,192,768]{2,1,0:T(8,128)(2,1)S(1)}, bf16[4,192,768]{2,1,0:T(8,128)(2,1)}, u32[]{:S(2)}) copy-start(bf16[4,192,768]{2,1,0:T(8,128)(2,1)} %constant.19.clone.table_ref) | copy-start | bytes 3538948
  94.1 20.0 %collective-permute-start.1 = (bf16[2,192,384]{2,1,0:T(8,128)(2,1)S(1)}, bf16[2,192,384]{2,1,0:T(8,128)(2,1)S(1)}, u32[]{:S(2)}, u32[]{:S(2)}) collective-permute-start(bf16[2,192,384]{2,1,0:T(8,128)(2,1)S(1)} %inverse_z_far.1), channel_id=1, source_target_pairs={{0,256},{1,259},{64,320},{65,323},{128,384},{129,387},{192,448},{1... | collective-permute-start | bytes 884744 | tf_op jit(solution)/shard_map/ppermute | solution.py:357
  98.0 23.8 %collective-permute-start.3 = (bf16[192,384]{1,0:T(8,128)(2,1)S(1)}, bf16[192,384]{1,0:T(8,128)(2,1)S(1)}, u32[]{:S(2)}, u32[]{:S(2)}) collective-permute-start(bf16[192,384]{1,0:T(8,128)(2,1)S(1)} %get-tuple-element.12), channel_id=1, source_target_pairs={{0,1},{1,0},{2,3},{3,2},{4,5},{5,4},{6,7},{7,6},{8,9},{9,8},{10,11... | collective-permute-start | bytes 442376 | tf_op jit(solution)/shard_map/ppermute | solution.py:345
  114.1 13.1 %collective-permute-start.4 = (bf16[192,384]{1,0:T(8,128)(2,1)S(1)}, bf16[192,384]{1,0:T(8,128)(2,1)S(1)}, u32[]{:S(2)}, u32[]{:S(2)}) collective-permute-start(bf16[192,384]{1,0:T(8,128)(2,1)S(1)} %get-tuple-element.13), channel_id=1, source_target_pairs={{0,257},{1,258},{64,321},{65,322},{128,385},{129,386},{192,449},{1... | collective-permute-start | bytes 442376 | tf_op jit(solution)/shard_map/ppermute | solution.py:357
  119.8 13.3 %collective-permute-start.2 = (bf16[192,384]{1,0:T(8,128)(2,1)S(1)}, bf16[192,384]{1,0:T(8,128)(2,1)S(1)}, u32[]{:S(2)}, u32[]{:S(2)}) collective-permute-start(bf16[192,384]{1,0:T(8,128)(2,1)S(1)} %get-tuple-element.14), channel_id=1, source_target_pairs={{0,256},{1,259},{64,320},{65,323},{128,384},{129,387},{192,448},{1... | collective-permute-start | bytes 442376 | tf_op jit(solution)/shard_map/ppermute | solution.py:357

commit v9 on v6

--- a/solution.py
+++ b/solution.py
@@ -103,11 +103,13 @@
     return values * keep + pltpu.roll(values, 64, axis=1) * swap
 
 
-def partial_z(me, rows_ref, table_ref, step, c):
+def partial_z(me_ref, rows_ref, table_ref, step, c):
+    me = me_ref[0]
+    wanted = pl.ds(pl.multiple_of(me_ref[1] * 96, 96), 96)
     turn = (me * lax.broadcasted_iota(jnp.int32, (64, 256), 1)) % 4
     to_real = jnp.where(turn == 0, 1.0, jnp.where(turn == 2, -1.0, 0.0))
     to_imag = jnp.where(turn == 3, 1.0, jnp.where(turn == 1, -1.0, 0.0))
-    row = lax.broadcasted_iota(jnp.int32, (NQ, 128), 0)
+    row = lax.broadcasted_iota(jnp.int32, (96, 128), 0)
     core = me % 2
     result = None
     for high in range(2):
@@ -123,10 +125,10 @@
         by_cos = jnp.concatenate([real, imag], axis=0).astype(jnp.bfloat16)
         by_sin = jnp.concatenate([imag, -real], axis=0).astype(jnp.bfloat16)
         lanes = slice(128, 384) if c == 1 else slice(0, 256)
-        total = jnp.zeros((NQ, 128), jnp.float32)
+        total = jnp.zeros((96, 128), jnp.float32)
         for part, values in enumerate((by_cos, by_sin)):
             total = total + lax.dot_general(
-                table_ref[part, :, lanes],
+                table_ref[part, wanted, lanes],
                 values,
                 (((1,), (1,)), ((), ())),
                 preferred_element_type=jnp.float32,
@@ -138,21 +140,21 @@
 
 def forward_z_own_body(me_ref, rows_ref, table_ref, out_ref):
     for c in range(3):
-        out_ref[c] = partial_z(me_ref[0], rows_ref, table_ref, 0, c)
+        out_ref[c] = partial_z(me_ref, rows_ref, table_ref, 0, c)
 
 
 def forward_z_body(me_ref, rows_ref, table_ref, own_ref, out_ref):
-    lane = lax.broadcasted_iota(jnp.int32, (NQ, 128), 1)
+    lane = lax.broadcasted_iota(jnp.int32, (96, 128), 1)
     totals = []
     for c in range(3):
-        total = own_ref[c] + partial_z(me_ref[0], rows_ref, table_ref, 1, c)
+        total = own_ref[c] + partial_z(me_ref, rows_ref, table_ref, 1, c)
         totals.append(total * (1.0 / math.sqrt(NZ)))
     for pair in range(2):
         if pair:
             totals = [jnp.where(lane % 2 == 1, -total, total) for total in totals]
         for y in range(4):
             for half in range(2):
-                start = y * 48 + half * 24
+                start = (y % 2) * 48 + half * 24
                 pieces = [total[start : start + 24] for total in totals]
                 block = jnp.concatenate(pieces, axis=0).astype(jnp.bfloat16)
                 out_ref[pair * 8 + half * 4 + y] = block
@@ -161,7 +163,7 @@
 def forward_z_call(me, rows, table, own):
     rows_spec = pl.BlockSpec((16, 40, 128), lambda j, s: (0, 0, 0))
     table_spec = pl.BlockSpec((2, NQ, 384), lambda j, s: (0, 0, 0))
-    own_spec = pl.BlockSpec((3, NQ, 128), lambda j, s: (0, 0, 0))
+    own_spec = pl.BlockSpec((3, 96, 128), lambda j, s: (0, 0, 0))
     out_spec = pl.BlockSpec((16, 72, 128), lambda j, s: (0, 0, 0))
     first = own is None
     return pl.pallas_call(
@@ -172,11 +174,11 @@
             in_specs=[rows_spec, table_spec] + ([] if first else [own_spec]),
             out_specs=own_spec if first else out_spec,
         ),
-        out_shape=jax.ShapeDtypeStruct((3, NQ, 128), jnp.float32)
+        out_shape=jax.ShapeDtypeStruct((3, 96, 128), jnp.float32)
         if first
         else jax.ShapeDtypeStruct((16, 72, 128), jnp.bfloat16),
         compiler_params=pltpu.CompilerParams(vmem_limit_bytes=VMEM),
-        cost_estimate=pl.CostEstimate(flops=151000000, bytes_accessed=1700000, transcendentals=0),
+        cost_estimate=pl.CostEstimate(flops=76000000, bytes_accessed=1200000, transcendentals=0),
         name="forward_z_own" if first else "forward_z",
     )(me, rows, table, *([] if first else [own]))
 
@@ -193,8 +195,8 @@
     total = total * (1.0 / 32.0)
     for half in range(2):
         block = total[half * 72 : half * 72 + 72].astype(jnp.bfloat16)
-        for y in range(4):
-            out_ref[half * 4 + y] = block
+        for i in range(4):
+            out_ref[i * 2 + half] = block
 
 
 def forward_x_call(values, table):
@@ -208,7 +210,7 @@
 
 
 def modes_body(kernel_ref, spec_ref, out_ref):
-    halves = [spec_ref[half, 0].astype(jnp.float32) for half in range(2)]
+    halves = [spec_ref[half].astype(jnp.float32) for half in range(2)]
     spec = []
     for c in range(3):
         pieces = [half[c * 24 : c * 24 + 24] for half in halves]
@@ -235,7 +237,7 @@
         grid=(4,),
         in_specs=[
             pl.BlockSpec((2, 3, 3, 1, 48, NP), lambda j: (0, 0, 0, 0, j, 0)),
-            pl.BlockSpec((2, 1, 72, 512), lambda j: (0, j, 0, 0)),
+            pl.BlockSpec((2, 72, 512), lambda j: (j, 0, 0)),
         ],
         out_specs=pl.BlockSpec((1, 288, NP), lambda j: (j, 0, 0)),
         out_shape=jax.ShapeDtypeStruct((4, 288, NP), jnp.bfloat16),
@@ -346,7 +348,7 @@
         for core in range(2):
             target = (z + (step if core == 0 else -step)) % 16
             perm.append((position(z, core), position(target, core ^ flip)))
-    return lax.ppermute(values, ("z_lo", "z_hi", "core"), perm)
+    return lax.ppermute(values, ("z_a", "z_b", "z_hi", "core"), perm)
 
 
 def per_device(wall, kernel):
@@ -354,13 +356,18 @@
     gz = (lax.axis_index("z_hi") * 2 + core).reshape(1).astype(jnp.int32)
 
     rows, z_table = pack_call(wall, jnp.asarray(forward_z_table()))
-    rows = exchange(rows, ("z_lo", "z_hi"))
+    rows = exchange(rows, ("z_a", "z_b", "z_hi"))
     other = swap_cores(rows)
-    z_spectra = forward_z_call(gz, other, z_table, forward_z_call(gz, rows, z_table, None))
-    z_spectra = exchange(z_spectra, ("gx_pair", "gx_in", "y"))
-    spec = exchange(forward_x_call(z_spectra, jnp.asarray(forward_x_table())), ("gx_in", "y"))
-
-    modes = exchange(modes_call(kernel, spec.reshape(2, 4, 72, 512)), ("gx_pair", "gx_in"))
+    place = jnp.concatenate([gz, lax.axis_index("z_b").reshape(1).astype(jnp.int32)])
+    z_spectra = forward_z_call(
+        place, other, z_table, forward_z_call(place, rows, z_table, None)
+    )
+    z_spectra = exchange(z_spectra, ("gx_pair", "gx_in", "y_pair", "y_in"))
+    spec = exchange(
+        forward_x_call(z_spectra, jnp.asarray(forward_x_table())), ("z_b", "y_in", "gx_in")
+    )
+
+    modes = exchange(modes_call(kernel, spec), ("gx_pair", "gx_in"))
     planes = exchange(inverse_x_call(modes, jnp.asarray(inverse_x_table())), ("core", "gx_pair", "gx_in"))
     planes = planes.reshape(NZ, 384)
     z_table = jnp.asarray(inverse_z_table())
@@ -374,18 +381,13 @@
 
 
 def solution(mesh):
-    fine = Mesh(
-        mesh.devices.reshape(8, 4, 2, 2, 2, 2),
-        ("z_lo", "y", "gx_pair", "gx_in", "z_hi", "core"),
-    )
-    gx, gz = ("gx_pair", "gx_in"), ("z_hi", "core")
+    names = ("z_a", "z_b", "y_pair", "y_in", "gx_pair", "gx_in", "z_hi", "core")
+    fine = Mesh(mesh.devices.reshape(4, 2, 2, 2, 2, 2, 2, 2), names)
+    gy, gx, gz = names[:4], names[4:6], names[6:]
     return jax.shard_map(
         per_device,
         mesh=fine,
-        in_specs=(
-            P(None, ("z_lo", "y") + gx, gz),
-            P(None, None, None, ("z_lo", "y"), gz, gx),
-        ),
-        out_specs=P(None, ("z_lo", "y"), gz, gx),
+        in_specs=(P(None, gy + gx, gz), P(None, None, None, gy, gz, gx)),
+        out_specs=P(None, gy, gz, gx),
         check_vma=False,
     )

time: 129 us -> 131 us (1.016)
  starting transfers between devices: 17.5 us -> 21.5 us
  waiting for transfers between devices: 20.1 us -> 16.9 us
    ppermute x4, starting transfers between devices: 9.69 us -> 13.7 us  [move_z(): return lax.ppermute(values, ('z_a', 'z_b', 'z_hi', 'core'), perm)]
    ppermute x4, waiting for transfers between devices: 19.6 us -> 16.9 us  [move_z(): return lax.ppermute(values, ('z_a', 'z_b', 'z_hi', 'core'), perm)]
  transfers between devices with their start and end apart: 6 -> 6, of which waited for: 5 -> 4; matrix products, arithmetic and copies ran while one was open for 0% -> 0% of each run, Pallas kernels for 1% -> 1%
where the time goes in v9:
time: 131 us; the launch traced here: 130 us
  blocking collectives  83.2 us (64%)
  starting transfers between devices  21.5 us (16%)
  waiting for transfers between devices  16.9 us (13%)
  Pallas kernels  7.94 us (6%)
    all_to_all x5, blocking collectives, exchange(): return lax.all_to_all(values, axis, split_axis=0, concat_axis=0, tiled=True)  83.2 us
    ppermute x4, waiting for transfers between devices, move_z(): return lax.ppermute(values, ('z_a', 'z_b', 'z_hi', 'core'), perm)  16.9 us
    ppermute x4, starting transfers between devices, move_z(): return lax.ppermute(values, ('z_a', 'z_b', 'z_hi', 'core'), perm)  13.7 us
    ppermute x2, starting transfers between devices, swap_cores(): return lax.ppermute(values, 'core', [(0, 1), (1, 0)])  7.82 us
  transfers between devices with their start and end apart: 6, of which 4 were waited for; matrix products, arithmetic and copies ran while one was open for 0% of the time, Pallas kernels for 1%

profile of v9, /device:TPU:1, one launch (start us, length us, event | category | flops | bytes accessed | tf_op | source)
XLA Modules:
  0.0 129.8 jit_solution(8489522248809175612)
XLA Ops:
  0.0 0.0 copy-start.2
  0.0 1.1 pack.1
  1.2 29.7 %all_to_all.25.rows_ref = bf16[16,40,128]{2,1,0:T(8,128)(2,1)S(1)} all-to-all(bf16[16,40,128]{2,1,0:T(8,128)(2,1)S(1)} %get-tuple-element.9), channel_id=1, replica_groups=mesh['z_a'=4,'z_b'=2,'y_pair'=2,'y_in'=2,'gx_pair'=2,'gx_in'=2,'z_hi'=2,..., dimensions={0} | all-to-all | bytes 327680 | tf_op jit(solution)/shard_map/all_to_all | solution.py:335
  30.8 5.3 %collective-permute-start = (bf16[16,40,128]{2,1,0:T(8,128)(2,1)S(1)}, bf16[16,40,128]{2,1,0:T(8,128)(2,1)S(1)}, u32[]{:S(2)}, u32[]{:S(2)}) collective-permute-start(bf16[16,40,128]{2,1,0:T(8,128)(2,1)S(1)} %all_to_all.25.rows_ref), channel_id=1, source_target_pairs={{0,1},{1,0},{2,3},{3,2},{4,5},{5,4},{6,7},{7,6},{8,9},{9,8},{10,11... | collective-permute-start | bytes 491528 | tf_op jit(solution)/shard_map/ppermute | solution.py:339
  36.2 0.1 pad_add_fusion.me_ref
  36.2 1.0 forward_z_own.1.own_ref
  37.3 0.0 collective-permute-done.rows_ref
  37.3 1.0 forward_z.1
  38.3 14.5 %all_to_all.26.values_ref = bf16[16,72,128]{2,1,0:T(8,128)(2,1)S(1)} all-to-all(bf16[16,72,128]{2,1,0:T(8,128)(2,1)S(1)} %forward_z.1), channel_id=1, replica_groups=mesh['z_a'=4,'z_b'=2,'y_pair'=2,'y_in'=2,'gx_pair'=2,'gx_in'=2,'z_hi'=2,..., dimensions={0} | all-to-all | bytes 589824 | tf_op jit(solution)/shard_map/all_to_all | solution.py:335
  52.8 0.0 copy-done.2
  52.8 0.0 copy-start.3
  52.8 0.5 forward_x.1
  53.3 0.0 copy-start.1
  53.3 10.9 %all_to_all.27.spec_ref = bf16[8,72,512]{2,1,0:T(8,128)(2,1)S(1)} all-to-all(bf16[8,72,512]{2,1,0:T(8,128)(2,1)S(1)} %forward_x.1), channel_id=1, replica_groups=mesh['z_a'=4,'z_b'=2,'y_pair'=2,'y_in'=2,'gx_pair'=2,'gx_in'=2,'z_hi'=2,..., dimensions={0} | all-to-all | bytes 1179648 | tf_op jit(solution)/shard_map/all_to_all | solution.py:335
  64.2 0.0 copy-done.3
  64.2 0.9 modes.1
  65.1 11.3 %all_to_all.28.values_ref = bf16[4,288,256]{2,1,0:T(8,128)(2,1)S(1)} all-to-all(bf16[4,288,256]{2,1,0:T(8,128)(2,1)S(1)} %modes.1), channel_id=1, replica_groups=mesh['z_a'=4,'z_b'=2,'y_pair'=2,'y_in'=2,'gx_pair'=2,'gx_in'=2,'z_hi'=2,..., dimensions={0} | all-to-all | bytes 1179648 | tf_op jit(solution)/shard_map/all_to_all | solution.py:335
  76.4 0.0 copy-done.1
  76.4 0.0 copy-start
  76.4 1.4 %inverse_x.1 = bf16[8,96,384]{2,1,0:T(8,128)(2,1)S(1)} custom-call(bf16[4,288,256]{2,1,0:T(8,128)(2,1)S(1)} %all_to_all.28.values_ref, bf16[8,1024,256]{2,1,0:T(8,128)(2,1)S(1)} %copy-done.1), custom_call_target="tpu_custom_call" | custom-call | flops 1208000000 | bytes 5400000 | tf_op jit(solution)/shard_map/inverse_x/pallas_call | solution.py:267
  77.8 16.9 %all_to_all.29 = bf16[8,96,384]{2,1,0:T(8,128)(2,1)S(1)} all-to-all(bf16[8,96,384]{2,1,0:T(8,128)(2,1)S(1)} %inverse_x.1), channel_id=1, replica_groups=mesh['z_a'=4,'z_b'=2,'y_pair'=2,'y_in'=2,'gx_pair'=2,'gx_in'=2,'z_hi'=2,..., dimensions={0} | all-to-all | bytes 1179648 | tf_op jit(solution)/shard_map/all_to_all | solution.py:335
  94.7 0.0 copy-done
  94.7 0.3 inverse_z_far.2
  95.0 3.0 %collective-permute-start.1 = (bf16[192,384]{1,0:T(8,128)(2,1)S(1)}, bf16[192,384]{1,0:T(8,128)(2,1)S(1)}, u32[]{:S(2)}, u32[]{:S(2)}) collective-permute-start(bf16[192,384]{1,0:T(8,128)(2,1)S(1)} %inverse_z_far.2), channel_id=1, source_target_pairs={{0,256},{1,259},{64,320},{65,323},{128,384},{129,387},{192,448},{1... | collective-permute-start | bytes 442376 | tf_op jit(solution)/shard_map/ppermute | solution.py:351
  98.0 0.3 inverse_z_far.3
  98.3 1.9 %collective-permute-start.4 = (bf16[192,384]{1,0:T(8,128)(2,1)S(1)}, bf16[192,384]{1,0:T(8,128)(2,1)S(1)}, u32[]{:S(2)}, u32[]{:S(2)}) collective-permute-start(bf16[192,384]{1,0:T(8,128)(2,1)S(1)} %inverse_z_far.3), channel_id=1, source_target_pairs={{0,256},{1,259},{64,320},{65,323},{128,384},{129,387},{192,448},{1... | collective-permute-start | bytes 442376 | tf_op jit(solution)/shard_map/ppermute | solution.py:351
  100.3 0.5 inverse_z_near.1
  100.8 2.5 %collective-permute-start.3 = (bf16[192,384]{1,0:T(8,128)(2,1)S(1)}, bf16[192,384]{1,0:T(8,128)(2,1)S(1)}, u32[]{:S(2)}, u32[]{:S(2)}) collective-permute-start(bf16[192,384]{1,0:T(8,128)(2,1)S(1)} %get-tuple-element.12), channel_id=1, source_target_pairs={{0,1},{1,0},{2,3},{3,2},{4,5},{5,4},{6,7},{7,6},{8,9},{9,8},{10,11... | collective-permute-start | bytes 442376 | tf_op jit(solution)/shard_map/ppermute | solution.py:339
  103.2 8.0 %collective-permute-done.1 = bf16[192,384]{1,0:T(8,128)(2,1)S(1)} collective-permute-done((bf16[192,384]{1,0:T(8,128)(2,1)S(1)}, bf16[192,384]{1,0:T(8,128)(2,1)S(1)}, u32[]{:S(2)}, u32[]{:S(2)}) %collective-permute-start.1) | collective-permute-done | bytes 147488 | tf_op jit(solution)/shard_map/ppermute | solution.py:351
  111.3 6.3 %collective-permute-start.2 = (bf16[192,384]{1,0:T(8,128)(2,1)S(1)}, bf16[192,384]{1,0:T(8,128)(2,1)S(1)}, u32[]{:S(2)}, u32[]{:S(2)}) collective-permute-start(bf16[192,384]{1,0:T(8,128)(2,1)S(1)} %collective-permute-done.1), channel_id=1, source_target_pairs={{0,256},{1,259},{64,320},{65,323},{128,384},{129,387},{192,448},{1... | collective-permute-start | bytes 442376 | tf_op jit(solution)/shard_map/ppermute | solution.py:351
  117.6 0.2 collective-permute-done.4
  117.8 2.5 %collective-permute-start.5 = (bf16[192,384]{1,0:T(8,128)(2,1)S(1)}, bf16[192,384]{1,0:T(8,128)(2,1)S(1)}, u32[]{:S(2)}, u32[]{:S(2)}) collective-permute-start(bf16[192,384]{1,0:T(8,128)(2,1)S(1)} %collective-permute-done.4), channel_id=1, source_target_pairs={{0,257},{1,258},{64,321},{65,322},{128,385},{129,386},{192,449},{1... | collective-permute-start | bytes 442376 | tf_op jit(solution)/shard_map/ppermute | solution.py:351
  120.2 0.0 collective-permute-done.3.near_ref
  120.3 2.8 %collective-permute-done.2.far_own_ref = bf16[192,384]{1,0:T(8,128)(2,1)S(1)} collective-permute-done((bf16[192,384]{1,0:T(8,128)(2,1)S(1)}, bf16[192,384]{1,0:T(8,128)(2,1)S(1)}, u32[]{:S(2)}, u32[]{:S(2)}) %collective-permute-start.2) | collective-permute-done | bytes 147488 | tf_op jit(solution)/shard_map/ppermute | solution.py:351
  123.0 5.9 %collective-permute-done.5.far_near_ref = bf16[192,384]{1,0:T(8,128)(2,1)S(1)} collective-permute-done((bf16[192,384]{1,0:T(8,128)(2,1)S(1)}, bf16[192,384]{1,0:T(8,128)(2,1)S(1)}, u32[]{:S(2)}, u32[]{:S(2)}) %collective-permute-start.5) | collective-permute-done | bytes 147488 | tf_op jit(solution)/shard_map/ppermute | solution.py:351
  128.9 0.8 finish.1
Async XLA Ops:
  0.0 52.8 %copy-start.2 = (bf16[8,256,512]{2,1,0:T(8,128)(2,1)S(1)}, bf16[8,256,512]{2,1,0:T(8,128)(2,1)}, u32[]{:S(2)}) copy-start(bf16[8,256,512]{2,1,0:T(8,128)(2,1)} %constant.21.clone.table_ref) | copy-start | bytes 6291460
  30.8 6.4 %collective-permute-start = (bf16[16,40,128]{2,1,0:T(8,128)(2,1)S(1)}, bf16[16,40,128]{2,1,0:T(8,128)(2,1)S(1)}, u32[]{:S(2)}, u32[]{:S(2)}) collective-permute-start(bf16[16,40,128]{2,1,0:T(8,128)(2,1)S(1)} %all_to_all.25.rows_ref), channel_id=1, source_target_pairs={{0,1},{1,0},{2,3},{3,2},{4,5},{5,4},{6,7},{7,6},{8,9},{9,8},{10,11... | collective-permute-start | bytes 491528 | tf_op jit(solution)/shard_map/ppermute | solution.py:339
  52.8 11.4 %copy-start.3 = (bf16[2,3,3,1,192,256]{5,4,3,2,1,0:T(8,128)(2,1)S(1)}, bf16[2,3,3,1,192,256]{5,4,3,2,1,0:T(8,128)(2,1)}, u32[]{:S(2)}) copy-start(bf16[2,3,3,1,192,256]{5,4,3,2,1,0:T(8,128)(2,1)} %kernel_ref.1) | copy-start | bytes 5308420
  53.3 23.1 %copy-start.1 = (bf16[8,1024,256]{2,1,0:T(8,128)(2,1)S(1)}, bf16[8,1024,256]{2,1,0:T(8,128)(2,1)}, u32[]{:S(2)}) copy-start(bf16[8,1024,256]{2,1,0:T(8,128)(2,1)} %constant.22.clone.table_ref) | copy-start | bytes 12582916
  76.4 18.3 %copy-start = (bf16[4,192,768]{2,1,0:T(8,128)(2,1)S(1)}, bf16[4,192,768]{2,1,0:T(8,128)(2,1)}, u32[]{:S(2)}) copy-start(bf16[4,192,768]{2,1,0:T(8,128)(2,1)} %constant.23.clone.table_ref) | copy-start | bytes 3538948
  95.0 16.2 %collective-permute-start.1 = (bf16[192,384]{1,0:T(8,128)(2,1)S(1)}, bf16[192,384]{1,0:T(8,128)(2,1)S(1)}, u32[]{:S(2)}, u32[]{:S(2)}) collective-permute-start(bf16[192,384]{1,0:T(8,128)(2,1)S(1)} %inverse_z_far.2), channel_id=1, source_target_pairs={{0,256},{1,259},{64,320},{65,323},{128,384},{129,387},{192,448},{1... | collective-permute-start | bytes 442376 | tf_op jit(solution)/shard_map/ppermute | solution.py:351
  98.3 19.4 %collective-permute-start.4 = (bf16[192,384]{1,0:T(8,128)(2,1)S(1)}, bf16[192,384]{1,0:T(8,128)(2,1)S(1)}, u32[]{:S(2)}, u32[]{:S(2)}) collective-permute-start(bf16[192,384]{1,0:T(8,128)(2,1)S(1)} %inverse_z_far.3), channel_id=1, source_target_pairs={{0,256},{1,259},{64,320},{65,323},{128,384},{129,387},{192,448},{1... | collective-permute-start | bytes 442376 | tf_op jit(solution)/shard_map/ppermute | solution.py:351
  100.8 19.5 %collective-permute-start.3 = (bf16[192,384]{1,0:T(8,128)(2,1)S(1)}, bf16[192,384]{1,0:T(8,128)(2,1)S(1)}, u32[]{:S(2)}, u32[]{:S(2)}) collective-permute-start(bf16[192,384]{1,0:T(8,128)(2,1)S(1)} %get-tuple-element.12), channel_id=1, source_target_pairs={{0,1},{1,0},{2,3},{3,2},{4,5},{5,4},{6,7},{7,6},{8,9},{9,8},{10,11... | collective-permute-start | bytes 442376 | tf_op jit(solution)/shard_map/ppermute | solution.py:339
  111.3 11.7 %collective-permute-start.2 = (bf16[192,384]{1,0:T(8,128)(2,1)S(1)}, bf16[192,384]{1,0:T(8,128)(2,1)S(1)}, u32[]{:S(2)}, u32[]{:S(2)}) collective-permute-start(bf16[192,384]{1,0:T(8,128)(2,1)S(1)} %collective-permute-done.1), channel_id=1, source_target_pairs={{0,256},{1,259},{64,320},{65,323},{128,384},{129,387},{192,448},{1... | collective-permute-start | bytes 442376 | tf_op jit(solution)/shard_map/ppermute | solution.py:351
  117.8 11.2 %collective-permute-start.5 = (bf16[192,384]{1,0:T(8,128)(2,1)S(1)}, bf16[192,384]{1,0:T(8,128)(2,1)S(1)}, u32[]{:S(2)}, u32[]{:S(2)}) collective-permute-start(bf16[192,384]{1,0:T(8,128)(2,1)S(1)} %collective-permute-done.4), channel_id=1, source_target_pairs={{0,257},{1,258},{64,321},{65,322},{128,385},{129,386},{192,449},{1... | collective-permute-start | bytes 442376 | tf_op jit(solution)/shard_map/ppermute | solution.py:351

commit v10 on v9

--- a/solution.py
+++ b/solution.py
@@ -27,7 +27,8 @@
     both = np.stack([np.cos(theta), np.sin(theta)])
     main, tail = both[..., :128], both[..., 128:]
     zero = np.zeros_like(tail)
-    return np.concatenate([tail, zero, main, zero, tail], axis=-1).astype(jnp.bfloat16)
+    both = np.concatenate([tail, zero, main, zero, tail], axis=-1)
+    return np.transpose(both.reshape(2, 2, 96, 384), (1, 0, 2, 3)).astype(jnp.bfloat16)
 
 
 def forward_x_table():
@@ -84,7 +85,7 @@
         scratch_shapes=[pltpu.VMEM((3, 8, NQ), jnp.bfloat16), pltpu.SemaphoreType.DMA((2,))],
         out_shape=[
             jax.ShapeDtypeStruct((16, 40, 128), jnp.bfloat16),
-            jax.ShapeDtypeStruct((2, NQ, 384), jnp.bfloat16),
+            jax.ShapeDtypeStruct((2, 2, 96, 384), jnp.bfloat16),
         ],
         compiler_params=pltpu.CompilerParams(vmem_limit_bytes=VMEM),
         cost_estimate=pl.CostEstimate(flops=10000, bytes_accessed=180000, transcendentals=0),
@@ -105,7 +106,7 @@
 
 def partial_z(me_ref, rows_ref, table_ref, step, c):
     me = me_ref[0]
-    wanted = pl.ds(pl.multiple_of(me_ref[1] * 96, 96), 96)
+    wanted = me_ref[1]
     turn = (me * lax.broadcasted_iota(jnp.int32, (64, 256), 1)) % 4
     to_real = jnp.where(turn == 0, 1.0, jnp.where(turn == 2, -1.0, 0.0))
     to_imag = jnp.where(turn == 3, 1.0, jnp.where(turn == 1, -1.0, 0.0))
@@ -128,7 +129,7 @@
         total = jnp.zeros((96, 128), jnp.float32)
         for part, values in enumerate((by_cos, by_sin)):
             total = total + lax.dot_general(
-                table_ref[part, wanted, lanes],
+                table_ref[wanted, part, :, lanes],
                 values,
                 (((1,), (1,)), ((), ())),
                 preferred_element_type=jnp.float32,
@@ -162,7 +163,7 @@
 
 def forward_z_call(me, rows, table, own):
     rows_spec = pl.BlockSpec((16, 40, 128), lambda j, s: (0, 0, 0))
-    table_spec = pl.BlockSpec((2, NQ, 384), lambda j, s: (0, 0, 0))
+    table_spec = pl.BlockSpec((2, 2, 96, 384), lambda j, s: (0, 0, 0, 0))
     own_spec = pl.BlockSpec((3, 96, 128), lambda j, s: (0, 0, 0))
     out_spec = pl.BlockSpec((16, 72, 128), lambda j, s: (0, 0, 0))
     first = own is None

time: 131 us -> 131 us (level)
  no operation moved by 1% of the time
where the time goes in v10:
time: 131 us; the launch traced here: 129 us
  blocking collectives  83.2 us (64%)
  starting transfers between devices  21.2 us (16%)
  waiting for transfers between devices  16.9 us (13%)
  Pallas kernels  7.94 us (6%)
    all_to_all x5, blocking collectives, exchange(): return lax.all_to_all(values, axis, split_axis=0, concat_axis=0, tiled=True)  83.2 us
    ppermute x4, waiting for transfers between devices, move_z(): return lax.ppermute(values, ('z_a', 'z_b', 'z_hi', 'core'), perm)  16.9 us
    ppermute x4, starting transfers between devices, move_z(): return lax.ppermute(values, ('z_a', 'z_b', 'z_hi', 'core'), perm)  13.4 us
    ppermute x2, starting transfers between devices, swap_cores(): return lax.ppermute(values, 'core', [(0, 1), (1, 0)])  7.82 us
  transfers between devices with their start and end apart: 6, of which 4 were waited for; matrix products, arithmetic and copies ran while one was open for 0% of the time, Pallas kernels for 1%

profile of v10, /device:TPU:1, one launch (start us, length us, event | category | flops | bytes accessed | tf_op | source)
XLA Modules:
  0.0 129.5 jit_solution(12947508271741344996)
XLA Ops:
  0.0 0.0 copy-start.2
  0.0 1.1 pack.1
  1.2 29.7 %all_to_all.25.rows_ref = bf16[16,40,128]{2,1,0:T(8,128)(2,1)S(1)} all-to-all(bf16[16,40,128]{2,1,0:T(8,128)(2,1)S(1)} %get-tuple-element.9), channel_id=1, replica_groups=mesh['z_a'=4,'z_b'=2,'y_pair'=2,'y_in'=2,'gx_pair'=2,'gx_in'=2,'z_hi'=2,..., dimensions={0} | all-to-all | bytes 327680 | tf_op jit(solution)/shard_map/all_to_all | solution.py:336
  30.8 5.3 %collective-permute-start = (bf16[16,40,128]{2,1,0:T(8,128)(2,1)S(1)}, bf16[16,40,128]{2,1,0:T(8,128)(2,1)S(1)}, u32[]{:S(2)}, u32[]{:S(2)}) collective-permute-start(bf16[16,40,128]{2,1,0:T(8,128)(2,1)S(1)} %all_to_all.25.rows_ref), channel_id=1, source_target_pairs={{0,1},{1,0},{2,3},{3,2},{4,5},{5,4},{6,7},{7,6},{8,9},{9,8},{10,11... | collective-permute-start | bytes 491528 | tf_op jit(solution)/shard_map/ppermute | solution.py:340
  36.2 0.1 pad_add_fusion.me_ref
  36.2 1.0 forward_z_own.1.own_ref
  37.3 0.0 collective-permute-done.rows_ref
  37.3 1.0 forward_z.1
  38.3 14.5 %all_to_all.26.values_ref = bf16[16,72,128]{2,1,0:T(8,128)(2,1)S(1)} all-to-all(bf16[16,72,128]{2,1,0:T(8,128)(2,1)S(1)} %forward_z.1), channel_id=1, replica_groups=mesh['z_a'=4,'z_b'=2,'y_pair'=2,'y_in'=2,'gx_pair'=2,'gx_in'=2,'z_hi'=2,..., dimensions={0} | all-to-all | bytes 589824 | tf_op jit(solution)/shard_map/all_to_all | solution.py:336
  52.8 0.0 copy-done.2
  52.8 0.0 copy-start.3
  52.8 0.5 forward_x.1
  53.3 0.0 copy-start.1
  53.3 10.9 %all_to_all.27.spec_ref = bf16[8,72,512]{2,1,0:T(8,128)(2,1)S(1)} all-to-all(bf16[8,72,512]{2,1,0:T(8,128)(2,1)S(1)} %forward_x.1), channel_id=1, replica_groups=mesh['z_a'=4,'z_b'=2,'y_pair'=2,'y_in'=2,'gx_pair'=2,'gx_in'=2,'z_hi'=2,..., dimensions={0} | all-to-all | bytes 1179648 | tf_op jit(solution)/shard_map/all_to_all | solution.py:336
  64.2 0.0 copy-done.3
  64.2 0.9 modes.1
  65.1 11.2 %all_to_all.28.values_ref = bf16[4,288,256]{2,1,0:T(8,128)(2,1)S(1)} all-to-all(bf16[4,288,256]{2,1,0:T(8,128)(2,1)S(1)} %modes.1), channel_id=1, replica_groups=mesh['z_a'=4,'z_b'=2,'y_pair'=2,'y_in'=2,'gx_pair'=2,'gx_in'=2,'z_hi'=2,..., dimensions={0} | all-to-all | bytes 1179648 | tf_op jit(solution)/shard_map/all_to_all | solution.py:336
  76.4 0.0 copy-done.1
  76.4 0.0 copy-start
  76.4 1.4 %inverse_x.1 = bf16[8,96,384]{2,1,0:T(8,128)(2,1)S(1)} custom-call(bf16[4,288,256]{2,1,0:T(8,128)(2,1)S(1)} %all_to_all.28.values_ref, bf16[8,1024,256]{2,1,0:T(8,128)(2,1)S(1)} %copy-done.1), custom_call_target="tpu_custom_call" | custom-call | flops 1208000000 | bytes 5400000 | tf_op jit(solution)/shard_map/inverse_x/pallas_call | solution.py:268
  77.8 16.9 %all_to_all.29 = bf16[8,96,384]{2,1,0:T(8,128)(2,1)S(1)} all-to-all(bf16[8,96,384]{2,1,0:T(8,128)(2,1)S(1)} %inverse_x.1), channel_id=1, replica_groups=mesh['z_a'=4,'z_b'=2,'y_pair'=2,'y_in'=2,'gx_pair'=2,'gx_in'=2,'z_hi'=2,..., dimensions={0} | all-to-all | bytes 1179648 | tf_op jit(solution)/shard_map/all_to_all | solution.py:336
  94.7 0.0 copy-done
  94.7 0.3 inverse_z_far.2
  95.0 3.0 %collective-permute-start.1 = (bf16[192,384]{1,0:T(8,128)(2,1)S(1)}, bf16[192,384]{1,0:T(8,128)(2,1)S(1)}, u32[]{:S(2)}, u32[]{:S(2)}) collective-permute-start(bf16[192,384]{1,0:T(8,128)(2,1)S(1)} %inverse_z_far.2), channel_id=1, source_target_pairs={{0,256},{1,259},{64,320},{65,323},{128,384},{129,387},{192,448},{1... | collective-permute-start | bytes 442376 | tf_op jit(solution)/shard_map/ppermute | solution.py:352
  98.0 0.3 inverse_z_far.3
  98.4 1.9 %collective-permute-start.4 = (bf16[192,384]{1,0:T(8,128)(2,1)S(1)}, bf16[192,384]{1,0:T(8,128)(2,1)S(1)}, u32[]{:S(2)}, u32[]{:S(2)}) collective-permute-start(bf16[192,384]{1,0:T(8,128)(2,1)S(1)} %inverse_z_far.3), channel_id=1, source_target_pairs={{0,256},{1,259},{64,320},{65,323},{128,384},{129,387},{192,448},{1... | collective-permute-start | bytes 442376 | tf_op jit(solution)/shard_map/ppermute | solution.py:352
  100.3 0.5 inverse_z_near.1
  100.8 2.5 %collective-permute-start.3 = (bf16[192,384]{1,0:T(8,128)(2,1)S(1)}, bf16[192,384]{1,0:T(8,128)(2,1)S(1)}, u32[]{:S(2)}, u32[]{:S(2)}) collective-permute-start(bf16[192,384]{1,0:T(8,128)(2,1)S(1)} %get-tuple-element.12), channel_id=1, source_target_pairs={{0,1},{1,0},{2,3},{3,2},{4,5},{5,4},{6,7},{7,6},{8,9},{9,8},{10,11... | collective-permute-start | bytes 442376 | tf_op jit(solution)/shard_map/ppermute | solution.py:340
  103.2 7.6 %collective-permute-done.1 = bf16[192,384]{1,0:T(8,128)(2,1)S(1)} collective-permute-done((bf16[192,384]{1,0:T(8,128)(2,1)S(1)}, bf16[192,384]{1,0:T(8,128)(2,1)S(1)}, u32[]{:S(2)}, u32[]{:S(2)}) %collective-permute-start.1) | collective-permute-done | bytes 147488 | tf_op jit(solution)/shard_map/ppermute | solution.py:352
  110.9 6.0 %collective-permute-start.2 = (bf16[192,384]{1,0:T(8,128)(2,1)S(1)}, bf16[192,384]{1,0:T(8,128)(2,1)S(1)}, u32[]{:S(2)}, u32[]{:S(2)}) collective-permute-start(bf16[192,384]{1,0:T(8,128)(2,1)S(1)} %collective-permute-done.1), channel_id=1, source_target_pairs={{0,256},{1,259},{64,320},{65,323},{128,384},{129,387},{192,448},{1... | collective-permute-start | bytes 442376 | tf_op jit(solution)/shard_map/ppermute | solution.py:352
  116.8 0.9 collective-permute-done.4
  117.8 2.5 %collective-permute-start.5 = (bf16[192,384]{1,0:T(8,128)(2,1)S(1)}, bf16[192,384]{1,0:T(8,128)(2,1)S(1)}, u32[]{:S(2)}, u32[]{:S(2)}) collective-permute-start(bf16[192,384]{1,0:T(8,128)(2,1)S(1)} %collective-permute-done.4), channel_id=1, source_target_pairs={{0,257},{1,258},{64,321},{65,322},{128,385},{129,386},{192,449},{1... | collective-permute-start | bytes 442376 | tf_op jit(solution)/shard_map/ppermute | solution.py:352
  120.3 0.0 collective-permute-done.3.near_ref
  120.3 2.7 %collective-permute-done.2.far_own_ref = bf16[192,384]{1,0:T(8,128)(2,1)S(1)} collective-permute-done((bf16[192,384]{1,0:T(8,128)(2,1)S(1)}, bf16[192,384]{1,0:T(8,128)(2,1)S(1)}, u32[]{:S(2)}, u32[]{:S(2)}) %collective-permute-start.2) | collective-permute-done | bytes 147488 | tf_op jit(solution)/shard_map/ppermute | solution.py:352
  123.0 5.6 %collective-permute-done.5.far_near_ref = bf16[192,384]{1,0:T(8,128)(2,1)S(1)} collective-permute-done((bf16[192,384]{1,0:T(8,128)(2,1)S(1)}, bf16[192,384]{1,0:T(8,128)(2,1)S(1)}, u32[]{:S(2)}, u32[]{:S(2)}) %collective-permute-start.5) | collective-permute-done | bytes 147488 | tf_op jit(solution)/shard_map/ppermute | solution.py:352
  128.6 0.8 finish.1
Async XLA Ops:
  0.0 52.8 %copy-start.2 = (bf16[8,256,512]{2,1,0:T(8,128)(2,1)S(1)}, bf16[8,256,512]{2,1,0:T(8,128)(2,1)}, u32[]{:S(2)}) copy-start(bf16[8,256,512]{2,1,0:T(8,128)(2,1)} %constant.21.clone.table_ref) | copy-start | bytes 6291460
  30.8 6.4 %collective-permute-start = (bf16[16,40,128]{2,1,0:T(8,128)(2,1)S(1)}, bf16[16,40,128]{2,1,0:T(8,128)(2,1)S(1)}, u32[]{:S(2)}, u32[]{:S(2)}) collective-permute-start(bf16[16,40,128]{2,1,0:T(8,128)(2,1)S(1)} %all_to_all.25.rows_ref), channel_id=1, source_target_pairs={{0,1},{1,0},{2,3},{3,2},{4,5},{5,4},{6,7},{7,6},{8,9},{9,8},{10,11... | collective-permute-start | bytes 491528 | tf_op jit(solution)/shard_map/ppermute | solution.py:340
  52.8 11.4 %copy-start.3 = (bf16[2,3,3,1,192,256]{5,4,3,2,1,0:T(8,128)(2,1)S(1)}, bf16[2,3,3,1,192,256]{5,4,3,2,1,0:T(8,128)(2,1)}, u32[]{:S(2)}) copy-start(bf16[2,3,3,1,192,256]{5,4,3,2,1,0:T(8,128)(2,1)} %kernel_ref.1) | copy-start | bytes 5308420
  53.3 23.1 %copy-start.1 = (bf16[8,1024,256]{2,1,0:T(8,128)(2,1)S(1)}, bf16[8,1024,256]{2,1,0:T(8,128)(2,1)}, u32[]{:S(2)}) copy-start(bf16[8,1024,256]{2,1,0:T(8,128)(2,1)} %constant.22.clone.table_ref) | copy-start | bytes 12582916
  76.4 18.3 %copy-start = (bf16[4,192,768]{2,1,0:T(8,128)(2,1)S(1)}, bf16[4,192,768]{2,1,0:T(8,128)(2,1)}, u32[]{:S(2)}) copy-start(bf16[4,192,768]{2,1,0:T(8,128)(2,1)} %constant.23.clone.table_ref) | copy-start | bytes 3538948
  95.0 15.8 %collective-permute-start.1 = (bf16[192,384]{1,0:T(8,128)(2,1)S(1)}, bf16[192,384]{1,0:T(8,128)(2,1)S(1)}, u32[]{:S(2)}, u32[]{:S(2)}) collective-permute-start(bf16[192,384]{1,0:T(8,128)(2,1)S(1)} %inverse_z_far.2), channel_id=1, source_target_pairs={{0,256},{1,259},{64,320},{65,323},{128,384},{129,387},{192,448},{1... | collective-permute-start | bytes 442376 | tf_op jit(solution)/shard_map/ppermute | solution.py:352
  98.4 19.4 %collective-permute-start.4 = (bf16[192,384]{1,0:T(8,128)(2,1)S(1)}, bf16[192,384]{1,0:T(8,128)(2,1)S(1)}, u32[]{:S(2)}, u32[]{:S(2)}) collective-permute-start(bf16[192,384]{1,0:T(8,128)(2,1)S(1)} %inverse_z_far.3), channel_id=1, source_target_pairs={{0,256},{1,259},{64,320},{65,323},{128,384},{129,387},{192,448},{1... | collective-permute-start | bytes 442376 | tf_op jit(solution)/shard_map/ppermute | solution.py:352
  100.8 19.5 %collective-permute-start.3 = (bf16[192,384]{1,0:T(8,128)(2,1)S(1)}, bf16[192,384]{1,0:T(8,128)(2,1)S(1)}, u32[]{:S(2)}, u32[]{:S(2)}) collective-permute-start(bf16[192,384]{1,0:T(8,128)(2,1)S(1)} %get-tuple-element.12), channel_id=1, source_target_pairs={{0,1},{1,0},{2,3},{3,2},{4,5},{5,4},{6,7},{7,6},{8,9},{9,8},{10,11... | collective-permute-start | bytes 442376 | tf_op jit(solution)/shard_map/ppermute | solution.py:340
  110.9 12.2 %collective-permute-start.2 = (bf16[192,384]{1,0:T(8,128)(2,1)S(1)}, bf16[192,384]{1,0:T(8,128)(2,1)S(1)}, u32[]{:S(2)}, u32[]{:S(2)}) collective-permute-start(bf16[192,384]{1,0:T(8,128)(2,1)S(1)} %collective-permute-done.1), channel_id=1, source_target_pairs={{0,256},{1,259},{64,320},{65,323},{128,384},{129,387},{192,448},{1... | collective-permute-start | bytes 442376 | tf_op jit(solution)/shard_map/ppermute | solution.py:352
  117.8 10.9 %collective-permute-start.5 = (bf16[192,384]{1,0:T(8,128)(2,1)S(1)}, bf16[192,384]{1,0:T(8,128)(2,1)S(1)}, u32[]{:S(2)}, u32[]{:S(2)}) collective-permute-start(bf16[192,384]{1,0:T(8,128)(2,1)S(1)} %collective-permute-done.4), channel_id=1, source_target_pairs={{0,257},{1,258},{64,321},{65,322},{128,385},{129,386},{192,449},{1... | collective-permute-start | bytes 442376 | tf_op jit(solution)/shard_map/ppermute | solution.py:352

commit v11 on v6

--- a/solution.py
+++ b/solution.py
@@ -52,7 +52,7 @@
 def inverse_z_table():
     q = (
         192 * np.arange(2)[:, None, None]
-        + 48 * np.arange(4)[None, :, None]
+        + 48 * np.array([0, 2, 1, 3])[None, :, None]
         + np.arange(48)[None, None, :]
     ).reshape(-1)
     theta = angle(np.arange(NZ), q, NZ).reshape(NZ, 8, 48)
@@ -237,7 +237,7 @@
             pl.BlockSpec((2, 3, 3, 1, 48, NP), lambda j: (0, 0, 0, 0, j, 0)),
             pl.BlockSpec((2, 1, 72, 512), lambda j: (0, j, 0, 0)),
         ],
-        out_specs=pl.BlockSpec((1, 288, NP), lambda j: (j, 0, 0)),
+        out_specs=pl.BlockSpec((1, 288, NP), lambda j: ((j % 2) * 2 + j // 2, 0, 0)),
         out_shape=jax.ShapeDtypeStruct((4, 288, NP), jnp.bfloat16),
         compiler_params=pltpu.CompilerParams(vmem_limit_bytes=VMEM),
         cost_estimate=pl.CostEstimate(flops=3600000, bytes_accessed=2950000, transcendentals=0),
@@ -246,16 +246,18 @@
 
 
 def inverse_x_body(values_ref, table_ref, out_ref):
-    values = jnp.concatenate([values_ref[s] for s in range(4)], axis=1)
+    values = jnp.concatenate([values_ref[s] for s in (0, 2, 1, 3)], axis=1)
 
     def block(j, carry):
         total = jnp.dot(values, table_ref[j], preferred_element_type=jnp.float32)
         total = total * (1.0 / 32.0)
         real = (total[:144, :128] - total[144:, 128:]).astype(jnp.bfloat16)
         imag = (total[:144, 128:] + total[144:, :128]).astype(jnp.bfloat16)
+        gx = j // 2
+        place = (j % 2) * 4 + (gx % 2) * 2 + gx // 2
         for o in range(3):
-            out_ref[(j % 2) * 4 + j // 2, 0:48, o * 128 : (o + 1) * 128] = real[o * 48 : (o + 1) * 48]
-            out_ref[(j % 2) * 4 + j // 2, 48:96, o * 128 : (o + 1) * 128] = imag[o * 48 : (o + 1) * 48]
+            out_ref[place, 0:48, o * 128 : (o + 1) * 128] = real[o * 48 : (o + 1) * 48]
+            out_ref[place, 48:96, o * 128 : (o + 1) * 128] = imag[o * 48 : (o + 1) * 48]
         return carry
 
     lax.fori_loop(0, 8, block, 0, unroll=True)
@@ -360,8 +362,8 @@
     z_spectra = exchange(z_spectra, ("gx_pair", "gx_in", "y"))
     spec = exchange(forward_x_call(z_spectra, jnp.asarray(forward_x_table())), ("gx_in", "y"))
 
-    modes = exchange(modes_call(kernel, spec.reshape(2, 4, 72, 512)), ("gx_pair", "gx_in"))
-    planes = exchange(inverse_x_call(modes, jnp.asarray(inverse_x_table())), ("core", "gx_pair", "gx_in"))
+    modes = exchange(modes_call(kernel, spec.reshape(2, 4, 72, 512)), ("gx_in", "gx_pair"))
+    planes = exchange(inverse_x_call(modes, jnp.asarray(inverse_x_table())), ("core", "gx_in", "gx_pair"))
     planes = planes.reshape(NZ, 384)
     z_table = jnp.asarray(inverse_z_table())
     (to_far,) = inverse_z_call(gz, planes, z_table, (2,))

time: 129 us -> 129 us (level)
  no operation moved by 1% of the time
where the time goes in v11:
time: 129 us; the launch traced here: 127 us
  blocking collectives  82.5 us (64%)
  waiting for transfers between devices  20.1 us (16%)
  starting transfers between devices  17.5 us (14%)
  Pallas kernels  7.1 us (6%)
    all_to_all x5, blocking collectives, exchange(): return lax.all_to_all(values, axis, split_axis=0, concat_axis=0, tiled=True)  82.5 us
    ppermute x4, waiting for transfers between devices, move_z(): return lax.ppermute(values, ('z_lo', 'z_hi', 'core'), perm)  19.6 us
    ppermute x4, starting transfers between devices, move_z(): return lax.ppermute(values, ('z_lo', 'z_hi', 'core'), perm)  9.68 us
    ppermute x2, starting transfers between devices, swap_cores(): return lax.ppermute(values, 'core', [(0, 1), (1, 0)])  7.82 us
  transfers between devices with their start and end apart: 6, of which 5 were waited for; matrix products, arithmetic and copies ran while one was open for 0% of the time, Pallas kernels for 1%

profile of v11, /device:TPU:1, one launch (start us, length us, event | category | flops | bytes accessed | tf_op | source)
XLA Modules:
  0.0 127.3 jit_solution(9979882701545111930)
XLA Ops:
  0.0 0.0 copy-start.2
  0.0 1.1 pack.1
  1.2 29.7 %all_to_all.25.rows_ref = bf16[16,40,128]{2,1,0:T(8,128)(2,1)S(1)} all-to-all(bf16[16,40,128]{2,1,0:T(8,128)(2,1)S(1)} %get-tuple-element.9), channel_id=1, replica_groups=mesh['z_lo'=8,'y'=4,'gx_pair'=2,'gx_in'=2,'z_hi'=2,'core'=2] {'z_lo','z_..., dimensions={0} | all-to-all | bytes 327680 | tf_op jit(solution)/shard_map/all_to_all | solution.py:335
  30.8 5.3 %collective-permute-start = (bf16[16,40,128]{2,1,0:T(8,128)(2,1)S(1)}, bf16[16,40,128]{2,1,0:T(8,128)(2,1)S(1)}, u32[]{:S(2)}, u32[]{:S(2)}) collective-permute-start(bf16[16,40,128]{2,1,0:T(8,128)(2,1)S(1)} %all_to_all.25.rows_ref), channel_id=1, source_target_pairs={{0,1},{1,0},{2,3},{3,2},{4,5},{5,4},{6,7},{7,6},{8,9},{9,8},{10,11... | collective-permute-start | bytes 491528 | tf_op jit(solution)/shard_map/ppermute | solution.py:339
  36.2 0.6 forward_z_own.1.own_ref
  36.7 0.4 collective-permute-done.rows_ref
  37.2 0.6 forward_z.1
  37.7 14.3 %all_to_all.26.values_ref = bf16[16,72,128]{2,1,0:T(8,128)(2,1)S(1)} all-to-all(bf16[16,72,128]{2,1,0:T(8,128)(2,1)S(1)} %forward_z.1), channel_id=1, replica_groups=mesh['z_lo'=8,'y'=4,'gx_pair'=2,'gx_in'=2,'z_hi'=2,'core'=2] {'gx_pair',..., dimensions={0} | all-to-all | bytes 589824 | tf_op jit(solution)/shard_map/all_to_all | solution.py:335
  52.0 0.0 copy-done.2
  52.0 0.0 copy-start.3
  52.0 0.5 forward_x.1
  52.6 0.0 copy-start.1
  52.6 11.6 %all_to_all.27 = bf16[8,72,512]{2,1,0:T(8,128)(2,1)S(1)} all-to-all(bf16[8,72,512]{2,1,0:T(8,128)(2,1)S(1)} %forward_x.1), channel_id=1, replica_groups=mesh['z_lo'=8,'y'=4,'gx_pair'=2,'gx_in'=2,'z_hi'=2,'core'=2] {'gx_in','y'}, dimensions={0} | all-to-all | bytes 1179648 | tf_op jit(solution)/shard_map/all_to_all | solution.py:335
  64.2 0.0 copy-done.3
  64.2 1.0 modes.1
  65.2 9.5 %all_to_all.28.values_ref = bf16[4,288,256]{2,1,0:T(8,128)(2,1)S(1)} all-to-all(bf16[4,288,256]{2,1,0:T(8,128)(2,1)S(1)} %modes.1), channel_id=1, replica_groups=mesh['z_lo'=8,'y'=4,'gx_pair'=2,'gx_in'=2,'z_hi'=2,'core'=2] {'gx_in','g..., dimensions={0} | all-to-all | bytes 1179648 | tf_op jit(solution)/shard_map/all_to_all | solution.py:335
  74.7 0.0 copy-done.1
  74.7 0.0 copy-start
  74.7 1.4 %inverse_x.1 = bf16[8,96,384]{2,1,0:T(8,128)(2,1)S(1)} custom-call(bf16[4,288,256]{2,1,0:T(8,128)(2,1)S(1)} %all_to_all.28.values_ref, bf16[8,1024,256]{2,1,0:T(8,128)(2,1)S(1)} %copy-done.1), custom_call_target="tpu_custom_call" | custom-call | flops 1208000000 | bytes 5400000 | tf_op jit(solution)/shard_map/inverse_x/pallas_call | solution.py:267
  76.1 17.4 %all_to_all.29 = bf16[8,96,384]{2,1,0:T(8,128)(2,1)S(1)} all-to-all(bf16[8,96,384]{2,1,0:T(8,128)(2,1)S(1)} %inverse_x.1), channel_id=1, replica_groups=mesh['z_lo'=8,'y'=4,'gx_pair'=2,'gx_in'=2,'z_hi'=2,'core'=2] {'core','gx..., dimensions={0} | all-to-all | bytes 1179648 | tf_op jit(solution)/shard_map/all_to_all | solution.py:335
  93.5 0.0 copy-done
  93.5 0.3 inverse_z_far.2
  93.8 3.4 %collective-permute-start.1 = (bf16[192,384]{1,0:T(8,128)(2,1)S(1)}, bf16[192,384]{1,0:T(8,128)(2,1)S(1)}, u32[]{:S(2)}, u32[]{:S(2)}) collective-permute-start(bf16[192,384]{1,0:T(8,128)(2,1)S(1)} %inverse_z_far.2), channel_id=1, source_target_pairs={{0,256},{1,259},{64,320},{65,323},{128,384},{129,387},{192,448},{1... | collective-permute-start | bytes 442376 | tf_op jit(solution)/shard_map/ppermute | solution.py:351
  97.2 0.3 inverse_z_far.3
  97.5 1.9 %collective-permute-start.4 = (bf16[192,384]{1,0:T(8,128)(2,1)S(1)}, bf16[192,384]{1,0:T(8,128)(2,1)S(1)}, u32[]{:S(2)}, u32[]{:S(2)}) collective-permute-start(bf16[192,384]{1,0:T(8,128)(2,1)S(1)} %inverse_z_far.3), channel_id=1, source_target_pairs={{0,256},{1,259},{64,320},{65,323},{128,384},{129,387},{192,448},{1... | collective-permute-start | bytes 442376 | tf_op jit(solution)/shard_map/ppermute | solution.py:351
  99.4 0.5 inverse_z_near.1
  99.9 2.5 %collective-permute-start.3 = (bf16[192,384]{1,0:T(8,128)(2,1)S(1)}, bf16[192,384]{1,0:T(8,128)(2,1)S(1)}, u32[]{:S(2)}, u32[]{:S(2)}) collective-permute-start(bf16[192,384]{1,0:T(8,128)(2,1)S(1)} %get-tuple-element.12), channel_id=1, source_target_pairs={{0,1},{1,0},{2,3},{3,2},{4,5},{5,4},{6,7},{7,6},{8,9},{9,8},{10,11... | collective-permute-start | bytes 442376 | tf_op jit(solution)/shard_map/ppermute | solution.py:339
  102.4 9.9 %collective-permute-done.1 = bf16[192,384]{1,0:T(8,128)(2,1)S(1)} collective-permute-done((bf16[192,384]{1,0:T(8,128)(2,1)S(1)}, bf16[192,384]{1,0:T(8,128)(2,1)S(1)}, u32[]{:S(2)}, u32[]{:S(2)}) %collective-permute-start.1) | collective-permute-done | bytes 147488 | tf_op jit(solution)/shard_map/ppermute | solution.py:351
  112.3 1.9 %collective-permute-start.2 = (bf16[192,384]{1,0:T(8,128)(2,1)S(1)}, bf16[192,384]{1,0:T(8,128)(2,1)S(1)}, u32[]{:S(2)}, u32[]{:S(2)}) collective-permute-start(bf16[192,384]{1,0:T(8,128)(2,1)S(1)} %collective-permute-done.1), channel_id=1, source_target_pairs={{0,256},{1,259},{64,320},{65,323},{128,384},{129,387},{192,448},{1... | collective-permute-start | bytes 442376 | tf_op jit(solution)/shard_map/ppermute | solution.py:351
  114.2 0.3 collective-permute-done.4
  114.5 2.5 %collective-permute-start.5 = (bf16[192,384]{1,0:T(8,128)(2,1)S(1)}, bf16[192,384]{1,0:T(8,128)(2,1)S(1)}, u32[]{:S(2)}, u32[]{:S(2)}) collective-permute-start(bf16[192,384]{1,0:T(8,128)(2,1)S(1)} %collective-permute-done.4), channel_id=1, source_target_pairs={{0,257},{1,258},{64,321},{65,322},{128,385},{129,386},{192,449},{1... | collective-permute-start | bytes 442376 | tf_op jit(solution)/shard_map/ppermute | solution.py:351
  117.0 0.0 collective-permute-done.3.near_ref
  117.0 5.4 %collective-permute-done.2.far_own_ref = bf16[192,384]{1,0:T(8,128)(2,1)S(1)} collective-permute-done((bf16[192,384]{1,0:T(8,128)(2,1)S(1)}, bf16[192,384]{1,0:T(8,128)(2,1)S(1)}, u32[]{:S(2)}, u32[]{:S(2)}) %collective-permute-start.2) | collective-permute-done | bytes 147488 | tf_op jit(solution)/shard_map/ppermute | solution.py:351
  122.4 4.0 %collective-permute-done.5.far_near_ref = bf16[192,384]{1,0:T(8,128)(2,1)S(1)} collective-permute-done((bf16[192,384]{1,0:T(8,128)(2,1)S(1)}, bf16[192,384]{1,0:T(8,128)(2,1)S(1)}, u32[]{:S(2)}, u32[]{:S(2)}) %collective-permute-start.5) | collective-permute-done | bytes 147488 | tf_op jit(solution)/shard_map/ppermute | solution.py:351
  126.5 0.8 finish.1
Async XLA Ops:
  0.0 52.0 %copy-start.2 = (bf16[8,256,512]{2,1,0:T(8,128)(2,1)S(1)}, bf16[8,256,512]{2,1,0:T(8,128)(2,1)}, u32[]{:S(2)}) copy-start(bf16[8,256,512]{2,1,0:T(8,128)(2,1)} %constant.17.clone.table_ref) | copy-start | bytes 6291460
  30.8 6.3 %collective-permute-start = (bf16[16,40,128]{2,1,0:T(8,128)(2,1)S(1)}, bf16[16,40,128]{2,1,0:T(8,128)(2,1)S(1)}, u32[]{:S(2)}, u32[]{:S(2)}) collective-permute-start(bf16[16,40,128]{2,1,0:T(8,128)(2,1)S(1)} %all_to_all.25.rows_ref), channel_id=1, source_target_pairs={{0,1},{1,0},{2,3},{3,2},{4,5},{5,4},{6,7},{7,6},{8,9},{9,8},{10,11... | collective-permute-start | bytes 491528 | tf_op jit(solution)/shard_map/ppermute | solution.py:339
  52.0 12.2 %copy-start.3 = (bf16[2,3,3,1,192,256]{5,4,3,2,1,0:T(8,128)(2,1)S(1)}, bf16[2,3,3,1,192,256]{5,4,3,2,1,0:T(8,128)(2,1)}, u32[]{:S(2)}) copy-start(bf16[2,3,3,1,192,256]{5,4,3,2,1,0:T(8,128)(2,1)} %kernel_ref.1) | copy-start | bytes 5308420
  52.6 22.1 %copy-start.1 = (bf16[8,1024,256]{2,1,0:T(8,128)(2,1)S(1)}, bf16[8,1024,256]{2,1,0:T(8,128)(2,1)}, u32[]{:S(2)}) copy-start(bf16[8,1024,256]{2,1,0:T(8,128)(2,1)} %constant.18.clone.table_ref) | copy-start | bytes 12582916
  74.7 18.8 %copy-start = (bf16[4,192,768]{2,1,0:T(8,128)(2,1)S(1)}, bf16[4,192,768]{2,1,0:T(8,128)(2,1)}, u32[]{:S(2)}) copy-start(bf16[4,192,768]{2,1,0:T(8,128)(2,1)} %constant.19.clone.table_ref) | copy-start | bytes 3538948
  93.8 18.5 %collective-permute-start.1 = (bf16[192,384]{1,0:T(8,128)(2,1)S(1)}, bf16[192,384]{1,0:T(8,128)(2,1)S(1)}, u32[]{:S(2)}, u32[]{:S(2)}) collective-permute-start(bf16[192,384]{1,0:T(8,128)(2,1)S(1)} %inverse_z_far.2), channel_id=1, source_target_pairs={{0,256},{1,259},{64,320},{65,323},{128,384},{129,387},{192,448},{1... | collective-permute-start | bytes 442376 | tf_op jit(solution)/shard_map/ppermute | solution.py:351
  97.5 17.0 %collective-permute-start.4 = (bf16[192,384]{1,0:T(8,128)(2,1)S(1)}, bf16[192,384]{1,0:T(8,128)(2,1)S(1)}, u32[]{:S(2)}, u32[]{:S(2)}) collective-permute-start(bf16[192,384]{1,0:T(8,128)(2,1)S(1)} %inverse_z_far.3), channel_id=1, source_target_pairs={{0,256},{1,259},{64,320},{65,323},{128,384},{129,387},{192,448},{1... | collective-permute-start | bytes 442376 | tf_op jit(solution)/shard_map/ppermute | solution.py:351
  99.9 17.1 %collective-permute-start.3 = (bf16[192,384]{1,0:T(8,128)(2,1)S(1)}, bf16[192,384]{1,0:T(8,128)(2,1)S(1)}, u32[]{:S(2)}, u32[]{:S(2)}) collective-permute-start(bf16[192,384]{1,0:T(8,128)(2,1)S(1)} %get-tuple-element.12), channel_id=1, source_target_pairs={{0,1},{1,0},{2,3},{3,2},{4,5},{5,4},{6,7},{7,6},{8,9},{9,8},{10,11... | collective-permute-start | bytes 442376 | tf_op jit(solution)/shard_map/ppermute | solution.py:339
  112.3 10.1 %collective-permute-start.2 = (bf16[192,384]{1,0:T(8,128)(2,1)S(1)}, bf16[192,384]{1,0:T(8,128)(2,1)S(1)}, u32[]{:S(2)}, u32[]{:S(2)}) collective-permute-start(bf16[192,384]{1,0:T(8,128)(2,1)S(1)} %collective-permute-done.1), channel_id=1, source_target_pairs={{0,256},{1,259},{64,320},{65,323},{128,384},{129,387},{192,448},{1... | collective-permute-start | bytes 442376 | tf_op jit(solution)/shard_map/ppermute | solution.py:351
  114.5 12.0 %collective-permute-start.5 = (bf16[192,384]{1,0:T(8,128)(2,1)S(1)}, bf16[192,384]{1,0:T(8,128)(2,1)S(1)}, u32[]{:S(2)}, u32[]{:S(2)}) collective-permute-start(bf16[192,384]{1,0:T(8,128)(2,1)S(1)} %collective-permute-done.4), channel_id=1, source_target_pairs={{0,257},{1,258},{64,321},{65,322},{128,385},{129,386},{192,449},{1... | collective-permute-start | bytes 442376 | tf_op jit(solution)/shard_map/ppermute | solution.py:351

commit v12 on v11

--- a/solution.py
+++ b/solution.py
@@ -346,7 +346,7 @@
     perm = []
     for z in range(16):
         for core in range(2):
-            target = (z + (step if core == 0 else -step)) % 16
+            target = (z + (step if core == 1 else -step)) % 16
             perm.append((position(z, core), position(target, core ^ flip)))
     return lax.ppermute(values, ("z_lo", "z_hi", "core"), perm)
 

time: 129 us -> 130 us (level)
  starting transfers between devices: 17.5 us -> 26.8 us
  waiting for transfers between devices: 20.1 us -> 12.6 us
    ppermute x4, starting transfers between devices: 9.68 us -> 18.5 us  [move_z(): return lax.ppermute(values, ('z_lo', 'z_hi', 'core'), perm)]
    ppermute x4, waiting for transfers between devices: 19.6 us -> 12.1 us  [move_z(): return lax.ppermute(values, ('z_lo', 'z_hi', 'core'), perm)]
  transfers between devices with their start and end apart: 6 -> 6, of which waited for: 5 -> 4; matrix products, arithmetic and copies ran while one was open for 0% -> 0% of each run, Pallas kernels for 1% -> 1%
where the time goes in v12:
time: 130 us; the launch traced here: 129 us
  blocking collectives  82.5 us (63%)
  starting transfers between devices  26.8 us (21%)
  waiting for transfers between devices  12.6 us (10%)
  Pallas kernels  7.09 us (5%)
    all_to_all x5, blocking collectives, exchange(): return lax.all_to_all(values, axis, split_axis=0, concat_axis=0, tiled=True)  82.5 us
    ppermute x4, starting transfers between devices, move_z(): return lax.ppermute(values, ('z_lo', 'z_hi', 'core'), perm)  18.5 us
    ppermute x4, waiting for transfers between devices, move_z(): return lax.ppermute(values, ('z_lo', 'z_hi', 'core'), perm)  12.1 us
    ppermute x2, starting transfers between devices, swap_cores(): return lax.ppermute(values, 'core', [(0, 1), (1, 0)])  8.3 us
  transfers between devices with their start and end apart: 6, of which 4 were waited for; matrix products, arithmetic and copies ran while one was open for 0% of the time, Pallas kernels for 1%

profile of v12, /device:TPU:1, one launch (start us, length us, event | category | flops | bytes accessed | tf_op | source)
XLA Modules:
  0.0 129.1 jit_solution(6686923888164580116)
XLA Ops:
  0.0 0.0 copy-start.2
  0.0 1.1 pack.1
  1.2 29.7 %all_to_all.25.rows_ref = bf16[16,40,128]{2,1,0:T(8,128)(2,1)S(1)} all-to-all(bf16[16,40,128]{2,1,0:T(8,128)(2,1)S(1)} %get-tuple-element.9), channel_id=1, replica_groups=mesh['z_lo'=8,'y'=4,'gx_pair'=2,'gx_in'=2,'z_hi'=2,'core'=2] {'z_lo','z_..., dimensions={0} | all-to-all | bytes 327680 | tf_op jit(solution)/shard_map/all_to_all | solution.py:335
  30.8 5.3 %collective-permute-start = (bf16[16,40,128]{2,1,0:T(8,128)(2,1)S(1)}, bf16[16,40,128]{2,1,0:T(8,128)(2,1)S(1)}, u32[]{:S(2)}, u32[]{:S(2)}) collective-permute-start(bf16[16,40,128]{2,1,0:T(8,128)(2,1)S(1)} %all_to_all.25.rows_ref), channel_id=1, source_target_pairs={{0,1},{1,0},{2,3},{3,2},{4,5},{5,4},{6,7},{7,6},{8,9},{9,8},{10,11... | collective-permute-start | bytes 491528 | tf_op jit(solution)/shard_map/ppermute | solution.py:339
  36.2 0.6 forward_z_own.1.own_ref
  36.7 0.4 collective-permute-done.rows_ref
  37.2 0.6 forward_z.1
  37.7 14.3 %all_to_all.26.values_ref = bf16[16,72,128]{2,1,0:T(8,128)(2,1)S(1)} all-to-all(bf16[16,72,128]{2,1,0:T(8,128)(2,1)S(1)} %forward_z.1), channel_id=1, replica_groups=mesh['z_lo'=8,'y'=4,'gx_pair'=2,'gx_in'=2,'z_hi'=2,'core'=2] {'gx_pair',..., dimensions={0} | all-to-all | bytes 589824 | tf_op jit(solution)/shard_map/all_to_all | solution.py:335
  52.0 0.0 copy-done.2
  52.0 0.0 copy-start.3
  52.0 0.5 forward_x.1
  52.6 0.0 copy-start.1
  52.6 11.6 %all_to_all.27 = bf16[8,72,512]{2,1,0:T(8,128)(2,1)S(1)} all-to-all(bf16[8,72,512]{2,1,0:T(8,128)(2,1)S(1)} %forward_x.1), channel_id=1, replica_groups=mesh['z_lo'=8,'y'=4,'gx_pair'=2,'gx_in'=2,'z_hi'=2,'core'=2] {'gx_in','y'}, dimensions={0} | all-to-all | bytes 1179648 | tf_op jit(solution)/shard_map/all_to_all | solution.py:335
  64.2 0.0 copy-done.3
  64.2 1.0 modes.1
  65.2 9.5 %all_to_all.28.values_ref = bf16[4,288,256]{2,1,0:T(8,128)(2,1)S(1)} all-to-all(bf16[4,288,256]{2,1,0:T(8,128)(2,1)S(1)} %modes.1), channel_id=1, replica_groups=mesh['z_lo'=8,'y'=4,'gx_pair'=2,'gx_in'=2,'z_hi'=2,'core'=2] {'gx_in','g..., dimensions={0} | all-to-all | bytes 1179648 | tf_op jit(solution)/shard_map/all_to_all | solution.py:335
  74.7 0.0 copy-done.1
  74.7 0.0 copy-start
  74.7 1.4 %inverse_x.1 = bf16[8,96,384]{2,1,0:T(8,128)(2,1)S(1)} custom-call(bf16[4,288,256]{2,1,0:T(8,128)(2,1)S(1)} %all_to_all.28.values_ref, bf16[8,1024,256]{2,1,0:T(8,128)(2,1)S(1)} %copy-done.1), custom_call_target="tpu_custom_call" | custom-call | flops 1208000000 | bytes 5400000 | tf_op jit(solution)/shard_map/inverse_x/pallas_call | solution.py:267
  76.1 17.4 %all_to_all.29 = bf16[8,96,384]{2,1,0:T(8,128)(2,1)S(1)} all-to-all(bf16[8,96,384]{2,1,0:T(8,128)(2,1)S(1)} %inverse_x.1), channel_id=1, replica_groups=mesh['z_lo'=8,'y'=4,'gx_pair'=2,'gx_in'=2,'z_hi'=2,'core'=2] {'core','gx..., dimensions={0} | all-to-all | bytes 1179648 | tf_op jit(solution)/shard_map/all_to_all | solution.py:335
  93.5 0.0 copy-done
  93.5 0.3 inverse_z_far.2
  93.8 1.9 %collective-permute-start.1 = (bf16[192,384]{1,0:T(8,128)(2,1)S(1)}, bf16[192,384]{1,0:T(8,128)(2,1)S(1)}, u32[]{:S(2)}, u32[]{:S(2)}) collective-permute-start(bf16[192,384]{1,0:T(8,128)(2,1)S(1)} %inverse_z_far.2), channel_id=1, source_target_pairs={{0,258},{1,257},{64,322},{65,321},{128,386},{129,385},{192,450},{1... | collective-permute-start | bytes 442376 | tf_op jit(solution)/shard_map/ppermute | solution.py:351
  95.8 0.3 inverse_z_far.3
  96.1 3.0 %collective-permute-start.4 = (bf16[192,384]{1,0:T(8,128)(2,1)S(1)}, bf16[192,384]{1,0:T(8,128)(2,1)S(1)}, u32[]{:S(2)}, u32[]{:S(2)}) collective-permute-start(bf16[192,384]{1,0:T(8,128)(2,1)S(1)} %inverse_z_far.3), channel_id=1, source_target_pairs={{0,258},{1,257},{64,322},{65,321},{128,386},{129,385},{192,450},{1... | collective-permute-start | bytes 442376 | tf_op jit(solution)/shard_map/ppermute | solution.py:351
  99.1 0.5 inverse_z_near.1
  99.5 3.0 %collective-permute-start.3 = (bf16[192,384]{1,0:T(8,128)(2,1)S(1)}, bf16[192,384]{1,0:T(8,128)(2,1)S(1)}, u32[]{:S(2)}, u32[]{:S(2)}) collective-permute-start(bf16[192,384]{1,0:T(8,128)(2,1)S(1)} %get-tuple-element.12), channel_id=1, source_target_pairs={{0,1},{1,0},{2,3},{3,2},{4,5},{5,4},{6,7},{7,6},{8,9},{9,8},{10,11... | collective-permute-start | bytes 442376 | tf_op jit(solution)/shard_map/ppermute | solution.py:339
  102.5 3.8 %collective-permute-done.1 = bf16[192,384]{1,0:T(8,128)(2,1)S(1)} collective-permute-done((bf16[192,384]{1,0:T(8,128)(2,1)S(1)}, bf16[192,384]{1,0:T(8,128)(2,1)S(1)}, u32[]{:S(2)}, u32[]{:S(2)}) %collective-permute-start.1) | collective-permute-done | bytes 147488 | tf_op jit(solution)/shard_map/ppermute | solution.py:351
  106.3 3.7 %collective-permute-start.2 = (bf16[192,384]{1,0:T(8,128)(2,1)S(1)}, bf16[192,384]{1,0:T(8,128)(2,1)S(1)}, u32[]{:S(2)}, u32[]{:S(2)}) collective-permute-start(bf16[192,384]{1,0:T(8,128)(2,1)S(1)} %collective-permute-done.1), channel_id=1, source_target_pairs={{0,258},{1,257},{64,322},{65,321},{128,386},{129,385},{192,450},{1... | collective-permute-start | bytes 442376 | tf_op jit(solution)/shard_map/ppermute | solution.py:351
  110.1 1.2 collective-permute-done.4
  111.3 9.9 %collective-permute-start.5 = (bf16[192,384]{1,0:T(8,128)(2,1)S(1)}, bf16[192,384]{1,0:T(8,128)(2,1)S(1)}, u32[]{:S(2)}, u32[]{:S(2)}) collective-permute-start(bf16[192,384]{1,0:T(8,128)(2,1)S(1)} %collective-permute-done.4), channel_id=1, source_target_pairs={{0,259},{1,256},{64,323},{65,320},{128,387},{129,384},{192,451},{1... | collective-permute-start | bytes 442376 | tf_op jit(solution)/shard_map/ppermute | solution.py:351
  121.2 0.0 collective-permute-done.3.near_ref
  121.2 0.0 collective-permute-done.2.far_own_ref
  121.2 7.1 %collective-permute-done.5.far_near_ref = bf16[192,384]{1,0:T(8,128)(2,1)S(1)} collective-permute-done((bf16[192,384]{1,0:T(8,128)(2,1)S(1)}, bf16[192,384]{1,0:T(8,128)(2,1)S(1)}, u32[]{:S(2)}, u32[]{:S(2)}) %collective-permute-start.5) | collective-permute-done | bytes 147488 | tf_op jit(solution)/shard_map/ppermute | solution.py:351
  128.3 0.8 finish.1
Async XLA Ops:
  0.0 52.0 %copy-start.2 = (bf16[8,256,512]{2,1,0:T(8,128)(2,1)S(1)}, bf16[8,256,512]{2,1,0:T(8,128)(2,1)}, u32[]{:S(2)}) copy-start(bf16[8,256,512]{2,1,0:T(8,128)(2,1)} %constant.17.clone.table_ref) | copy-start | bytes 6291460
  30.8 6.3 %collective-permute-start = (bf16[16,40,128]{2,1,0:T(8,128)(2,1)S(1)}, bf16[16,40,128]{2,1,0:T(8,128)(2,1)S(1)}, u32[]{:S(2)}, u32[]{:S(2)}) collective-permute-start(bf16[16,40,128]{2,1,0:T(8,128)(2,1)S(1)} %all_to_all.25.rows_ref), channel_id=1, source_target_pairs={{0,1},{1,0},{2,3},{3,2},{4,5},{5,4},{6,7},{7,6},{8,9},{9,8},{10,11... | collective-permute-start | bytes 491528 | tf_op jit(solution)/shard_map/ppermute | solution.py:339
  52.0 12.2 %copy-start.3 = (bf16[2,3,3,1,192,256]{5,4,3,2,1,0:T(8,128)(2,1)S(1)}, bf16[2,3,3,1,192,256]{5,4,3,2,1,0:T(8,128)(2,1)}, u32[]{:S(2)}) copy-start(bf16[2,3,3,1,192,256]{5,4,3,2,1,0:T(8,128)(2,1)} %kernel_ref.1) | copy-start | bytes 5308420
  52.6 22.1 %copy-start.1 = (bf16[8,1024,256]{2,1,0:T(8,128)(2,1)S(1)}, bf16[8,1024,256]{2,1,0:T(8,128)(2,1)}, u32[]{:S(2)}) copy-start(bf16[8,1024,256]{2,1,0:T(8,128)(2,1)} %constant.18.clone.table_ref) | copy-start | bytes 12582916
  74.7 18.8 %copy-start = (bf16[4,192,768]{2,1,0:T(8,128)(2,1)S(1)}, bf16[4,192,768]{2,1,0:T(8,128)(2,1)}, u32[]{:S(2)}) copy-start(bf16[4,192,768]{2,1,0:T(8,128)(2,1)} %constant.19.clone.table_ref) | copy-start | bytes 3538948
  93.8 12.5 %collective-permute-start.1 = (bf16[192,384]{1,0:T(8,128)(2,1)S(1)}, bf16[192,384]{1,0:T(8,128)(2,1)S(1)}, u32[]{:S(2)}, u32[]{:S(2)}) collective-permute-start(bf16[192,384]{1,0:T(8,128)(2,1)S(1)} %inverse_z_far.2), channel_id=1, source_target_pairs={{0,258},{1,257},{64,322},{65,321},{128,386},{129,385},{192,450},{1... | collective-permute-start | bytes 442376 | tf_op jit(solution)/shard_map/ppermute | solution.py:351
  96.1 15.2 %collective-permute-start.4 = (bf16[192,384]{1,0:T(8,128)(2,1)S(1)}, bf16[192,384]{1,0:T(8,128)(2,1)S(1)}, u32[]{:S(2)}, u32[]{:S(2)}) collective-permute-start(bf16[192,384]{1,0:T(8,128)(2,1)S(1)} %inverse_z_far.3), channel_id=1, source_target_pairs={{0,258},{1,257},{64,322},{65,321},{128,386},{129,385},{192,450},{1... | collective-permute-start | bytes 442376 | tf_op jit(solution)/shard_map/ppermute | solution.py:351
  99.5 21.6 %collective-permute-start.3 = (bf16[192,384]{1,0:T(8,128)(2,1)S(1)}, bf16[192,384]{1,0:T(8,128)(2,1)S(1)}, u32[]{:S(2)}, u32[]{:S(2)}) collective-permute-start(bf16[192,384]{1,0:T(8,128)(2,1)S(1)} %get-tuple-element.12), channel_id=1, source_target_pairs={{0,1},{1,0},{2,3},{3,2},{4,5},{5,4},{6,7},{7,6},{8,9},{9,8},{10,11... | collective-permute-start | bytes 442376 | tf_op jit(solution)/shard_map/ppermute | solution.py:339
  106.3 14.8 %collective-permute-start.2 = (bf16[192,384]{1,0:T(8,128)(2,1)S(1)}, bf16[192,384]{1,0:T(8,128)(2,1)S(1)}, u32[]{:S(2)}, u32[]{:S(2)}) collective-permute-start(bf16[192,384]{1,0:T(8,128)(2,1)S(1)} %collective-permute-done.1), channel_id=1, source_target_pairs={{0,258},{1,257},{64,322},{65,321},{128,386},{129,385},{192,450},{1... | collective-permute-start | bytes 442376 | tf_op jit(solution)/shard_map/ppermute | solution.py:351
  111.3 17.0 %collective-permute-start.5 = (bf16[192,384]{1,0:T(8,128)(2,1)S(1)}, bf16[192,384]{1,0:T(8,128)(2,1)S(1)}, u32[]{:S(2)}, u32[]{:S(2)}) collective-permute-start(bf16[192,384]{1,0:T(8,128)(2,1)S(1)} %collective-permute-done.4), channel_id=1, source_target_pairs={{0,259},{1,256},{64,323},{65,320},{128,387},{129,384},{192,451},{1... | collective-permute-start | bytes 442376 | tf_op jit(solution)/shard_map/ppermute | solution.py:351

commit v13 on v11

--- a/solution.py
+++ b/solution.py
@@ -370,7 +370,7 @@
     (to_far_near,) = inverse_z_call(gz, planes, z_table, (3,))
     own, to_near = inverse_z_call(gz, planes, z_table, (0, 1))
     far_own = move_z(move_z(to_far, 4, 0), 4, 0)
-    far_near = move_z(move_z(to_far_near, 4, 0), 4, 1)
+    far_near = move_z(move_z(to_far_near, -4, 0), -4, 1)
     near = swap_cores(to_near)
     return finish_call(core.reshape(1).astype(jnp.int32), own, far_own, near, far_near)
 

time: 129 us -> 131 us (1.016)
  starting transfers between devices: 17.5 us -> 21.4 us
    ppermute x4, starting transfers between devices: 9.68 us -> 13.1 us  [move_z(): return lax.ppermute(values, ('z_lo', 'z_hi', 'core'), perm)]
  transfers between devices with their start and end apart: 6 -> 6, of which waited for: 5 -> 4; matrix products, arithmetic and copies ran while one was open for 0% -> 0% of each run, Pallas kernels for 1% -> 1%
where the time goes in v13:
time: 131 us
  blocking collectives  82.5 us (63%)
  starting transfers between devices  21.4 us (16%)
  waiting for transfers between devices  19.5 us (15%)
  Pallas kernels  7.1 us (5%)
    all_to_all x5, blocking collectives, exchange(): return lax.all_to_all(values, axis, split_axis=0, concat_axis=0, tiled=True)  82.5 us
    ppermute x4, waiting for transfers between devices, move_z(): return lax.ppermute(values, ('z_lo', 'z_hi', 'core'), perm)  19.1 us
    ppermute x4, starting transfers between devices, move_z(): return lax.ppermute(values, ('z_lo', 'z_hi', 'core'), perm)  13.1 us
    ppermute x2, starting transfers between devices, swap_cores(): return lax.ppermute(values, 'core', [(0, 1), (1, 0)])  8.2 us
  transfers between devices with their start and end apart: 6, of which 4 were waited for; matrix products, arithmetic and copies ran while one was open for 0% of the time, Pallas kernels for 1%

profile of v13, /device:TPU:1, one launch (start us, length us, event | category | flops | bytes accessed | tf_op | source)
XLA Modules:
  0.0 130.6 jit_solution(3025916536251066548)
XLA Ops:
  0.0 0.0 copy-start.2
  0.0 1.1 pack.1
  1.2 29.7 %all_to_all.25.rows_ref = bf16[16,40,128]{2,1,0:T(8,128)(2,1)S(1)} all-to-all(bf16[16,40,128]{2,1,0:T(8,128)(2,1)S(1)} %get-tuple-element.9), channel_id=1, replica_groups=mesh['z_lo'=8,'y'=4,'gx_pair'=2,'gx_in'=2,'z_hi'=2,'core'=2] {'z_lo','z_..., dimensions={0} | all-to-all | bytes 327680 | tf_op jit(solution)/shard_map/all_to_all | solution.py:335
  30.8 5.3 %collective-permute-start = (bf16[16,40,128]{2,1,0:T(8,128)(2,1)S(1)}, bf16[16,40,128]{2,1,0:T(8,128)(2,1)S(1)}, u32[]{:S(2)}, u32[]{:S(2)}) collective-permute-start(bf16[16,40,128]{2,1,0:T(8,128)(2,1)S(1)} %all_to_all.25.rows_ref), channel_id=1, source_target_pairs={{0,1},{1,0},{2,3},{3,2},{4,5},{5,4},{6,7},{7,6},{8,9},{9,8},{10,11... | collective-permute-start | bytes 491528 | tf_op jit(solution)/shard_map/ppermute | solution.py:339
  36.2 0.6 forward_z_own.1.own_ref
  36.7 0.4 collective-permute-done.rows_ref
  37.2 0.6 forward_z.1
  37.7 14.3 %all_to_all.26.values_ref = bf16[16,72,128]{2,1,0:T(8,128)(2,1)S(1)} all-to-all(bf16[16,72,128]{2,1,0:T(8,128)(2,1)S(1)} %forward_z.1), channel_id=1, replica_groups=mesh['z_lo'=8,'y'=4,'gx_pair'=2,'gx_in'=2,'z_hi'=2,'core'=2] {'gx_pair',..., dimensions={0} | all-to-all | bytes 589824 | tf_op jit(solution)/shard_map/all_to_all | solution.py:335
  52.0 0.0 copy-done.2
  52.0 0.0 copy-start.3
  52.0 0.5 forward_x.1
  52.6 0.0 copy-start.1
  52.6 11.6 %all_to_all.27 = bf16[8,72,512]{2,1,0:T(8,128)(2,1)S(1)} all-to-all(bf16[8,72,512]{2,1,0:T(8,128)(2,1)S(1)} %forward_x.1), channel_id=1, replica_groups=mesh['z_lo'=8,'y'=4,'gx_pair'=2,'gx_in'=2,'z_hi'=2,'core'=2] {'gx_in','y'}, dimensions={0} | all-to-all | bytes 1179648 | tf_op jit(solution)/shard_map/all_to_all | solution.py:335
  64.2 0.0 copy-done.3
  64.2 1.0 modes.1
  65.2 9.5 %all_to_all.28.values_ref = bf16[4,288,256]{2,1,0:T(8,128)(2,1)S(1)} all-to-all(bf16[4,288,256]{2,1,0:T(8,128)(2,1)S(1)} %modes.1), channel_id=1, replica_groups=mesh['z_lo'=8,'y'=4,'gx_pair'=2,'gx_in'=2,'z_hi'=2,'core'=2] {'gx_in','g..., dimensions={0} | all-to-all | bytes 1179648 | tf_op jit(solution)/shard_map/all_to_all | solution.py:335
  74.7 0.0 copy-done.1
  74.7 0.0 copy-start
  74.7 1.4 %inverse_x.1 = bf16[8,96,384]{2,1,0:T(8,128)(2,1)S(1)} custom-call(bf16[4,288,256]{2,1,0:T(8,128)(2,1)S(1)} %all_to_all.28.values_ref, bf16[8,1024,256]{2,1,0:T(8,128)(2,1)S(1)} %copy-done.1), custom_call_target="tpu_custom_call" | custom-call | flops 1208000000 | bytes 5400000 | tf_op jit(solution)/shard_map/inverse_x/pallas_call | solution.py:267
  76.1 17.4 %all_to_all.29 = bf16[8,96,384]{2,1,0:T(8,128)(2,1)S(1)} all-to-all(bf16[8,96,384]{2,1,0:T(8,128)(2,1)S(1)} %inverse_x.1), channel_id=1, replica_groups=mesh['z_lo'=8,'y'=4,'gx_pair'=2,'gx_in'=2,'z_hi'=2,'core'=2] {'core','gx..., dimensions={0} | all-to-all | bytes 1179648 | tf_op jit(solution)/shard_map/all_to_all | solution.py:335
  93.5 0.0 copy-done
  93.5 0.3 inverse_z_far.2
  93.8 3.4 %collective-permute-start.1 = (bf16[192,384]{1,0:T(8,128)(2,1)S(1)}, bf16[192,384]{1,0:T(8,128)(2,1)S(1)}, u32[]{:S(2)}, u32[]{:S(2)}) collective-permute-start(bf16[192,384]{1,0:T(8,128)(2,1)S(1)} %inverse_z_far.2), channel_id=1, source_target_pairs={{0,256},{1,259},{64,320},{65,323},{128,384},{129,387},{192,448},{1... | collective-permute-start | bytes 442376 | tf_op jit(solution)/shard_map/ppermute | solution.py:351
  97.2 0.3 inverse_z_far.3
  97.5 5.8 %collective-permute-start.4 = (bf16[192,384]{1,0:T(8,128)(2,1)S(1)}, bf16[192,384]{1,0:T(8,128)(2,1)S(1)}, u32[]{:S(2)}, u32[]{:S(2)}) collective-permute-start(bf16[192,384]{1,0:T(8,128)(2,1)S(1)} %inverse_z_far.3), channel_id=1, source_target_pairs={{0,258},{1,257},{64,322},{65,321},{128,386},{129,385},{192,450},{1... | collective-permute-start | bytes 442376 | tf_op jit(solution)/shard_map/ppermute | solution.py:351
  103.3 0.5 inverse_z_near.1
  103.8 2.9 %collective-permute-start.3 = (bf16[192,384]{1,0:T(8,128)(2,1)S(1)}, bf16[192,384]{1,0:T(8,128)(2,1)S(1)}, u32[]{:S(2)}, u32[]{:S(2)}) collective-permute-start(bf16[192,384]{1,0:T(8,128)(2,1)S(1)} %get-tuple-element.12), channel_id=1, source_target_pairs={{0,1},{1,0},{2,3},{3,2},{4,5},{5,4},{6,7},{7,6},{8,9},{9,8},{10,11... | collective-permute-start | bytes 442376 | tf_op jit(solution)/shard_map/ppermute | solution.py:339
  106.7 6.9 %collective-permute-done.1 = bf16[192,384]{1,0:T(8,128)(2,1)S(1)} collective-permute-done((bf16[192,384]{1,0:T(8,128)(2,1)S(1)}, bf16[192,384]{1,0:T(8,128)(2,1)S(1)}, u32[]{:S(2)}, u32[]{:S(2)}) %collective-permute-start.1) | collective-permute-done | bytes 147488 | tf_op jit(solution)/shard_map/ppermute | solution.py:351
  113.6 1.9 %collective-permute-start.2 = (bf16[192,384]{1,0:T(8,128)(2,1)S(1)}, bf16[192,384]{1,0:T(8,128)(2,1)S(1)}, u32[]{:S(2)}, u32[]{:S(2)}) collective-permute-start(bf16[192,384]{1,0:T(8,128)(2,1)S(1)} %collective-permute-done.1), channel_id=1, source_target_pairs={{0,256},{1,259},{64,320},{65,323},{128,384},{129,387},{192,448},{1... | collective-permute-start | bytes 442376 | tf_op jit(solution)/shard_map/ppermute | solution.py:351
  115.5 0.0 collective-permute-done.4
  115.5 2.1 %collective-permute-start.5 = (bf16[192,384]{1,0:T(8,128)(2,1)S(1)}, bf16[192,384]{1,0:T(8,128)(2,1)S(1)}, u32[]{:S(2)}, u32[]{:S(2)}) collective-permute-start(bf16[192,384]{1,0:T(8,128)(2,1)S(1)} %collective-permute-done.4), channel_id=1, source_target_pairs={{0,259},{1,256},{64,323},{65,320},{128,387},{129,384},{192,451},{1... | collective-permute-start | bytes 442376 | tf_op jit(solution)/shard_map/ppermute | solution.py:351
  117.6 0.0 collective-permute-done.3.near_ref
  117.6 6.1 %collective-permute-done.2.far_own_ref = bf16[192,384]{1,0:T(8,128)(2,1)S(1)} collective-permute-done((bf16[192,384]{1,0:T(8,128)(2,1)S(1)}, bf16[192,384]{1,0:T(8,128)(2,1)S(1)}, u32[]{:S(2)}, u32[]{:S(2)}) %collective-permute-start.2) | collective-permute-done | bytes 147488 | tf_op jit(solution)/shard_map/ppermute | solution.py:351
  123.7 6.1 %collective-permute-done.5.far_near_ref = bf16[192,384]{1,0:T(8,128)(2,1)S(1)} collective-permute-done((bf16[192,384]{1,0:T(8,128)(2,1)S(1)}, bf16[192,384]{1,0:T(8,128)(2,1)S(1)}, u32[]{:S(2)}, u32[]{:S(2)}) %collective-permute-start.5) | collective-permute-done | bytes 147488 | tf_op jit(solution)/shard_map/ppermute | solution.py:351
  129.8 0.8 finish.1
Async XLA Ops:
  0.0 52.0 %copy-start.2 = (bf16[8,256,512]{2,1,0:T(8,128)(2,1)S(1)}, bf16[8,256,512]{2,1,0:T(8,128)(2,1)}, u32[]{:S(2)}) copy-start(bf16[8,256,512]{2,1,0:T(8,128)(2,1)} %constant.17.clone.table_ref) | copy-start | bytes 6291460
  30.8 6.3 %collective-permute-start = (bf16[16,40,128]{2,1,0:T(8,128)(2,1)S(1)}, bf16[16,40,128]{2,1,0:T(8,128)(2,1)S(1)}, u32[]{:S(2)}, u32[]{:S(2)}) collective-permute-start(bf16[16,40,128]{2,1,0:T(8,128)(2,1)S(1)} %all_to_all.25.rows_ref), channel_id=1, source_target_pairs={{0,1},{1,0},{2,3},{3,2},{4,5},{5,4},{6,7},{7,6},{8,9},{9,8},{10,11... | collective-permute-start | bytes 491528 | tf_op jit(solution)/shard_map/ppermute | solution.py:339
  52.0 12.2 %copy-start.3 = (bf16[2,3,3,1,192,256]{5,4,3,2,1,0:T(8,128)(2,1)S(1)}, bf16[2,3,3,1,192,256]{5,4,3,2,1,0:T(8,128)(2,1)}, u32[]{:S(2)}) copy-start(bf16[2,3,3,1,192,256]{5,4,3,2,1,0:T(8,128)(2,1)} %kernel_ref.1) | copy-start | bytes 5308420
  52.6 22.1 %copy-start.1 = (bf16[8,1024,256]{2,1,0:T(8,128)(2,1)S(1)}, bf16[8,1024,256]{2,1,0:T(8,128)(2,1)}, u32[]{:S(2)}) copy-start(bf16[8,1024,256]{2,1,0:T(8,128)(2,1)} %constant.18.clone.table_ref) | copy-start | bytes 12582916
  74.7 18.8 %copy-start = (bf16[4,192,768]{2,1,0:T(8,128)(2,1)S(1)}, bf16[4,192,768]{2,1,0:T(8,128)(2,1)}, u32[]{:S(2)}) copy-start(bf16[4,192,768]{2,1,0:T(8,128)(2,1)} %constant.19.clone.table_ref) | copy-start | bytes 3538948
  93.8 19.8 %collective-permute-start.1 = (bf16[192,384]{1,0:T(8,128)(2,1)S(1)}, bf16[192,384]{1,0:T(8,128)(2,1)S(1)}, u32[]{:S(2)}, u32[]{:S(2)}) collective-permute-start(bf16[192,384]{1,0:T(8,128)(2,1)S(1)} %inverse_z_far.2), channel_id=1, source_target_pairs={{0,256},{1,259},{64,320},{65,323},{128,384},{129,387},{192,448},{1... | collective-permute-start | bytes 442376 | tf_op jit(solution)/shard_map/ppermute | solution.py:351
  97.5 18.0 %collective-permute-start.4 = (bf16[192,384]{1,0:T(8,128)(2,1)S(1)}, bf16[192,384]{1,0:T(8,128)(2,1)S(1)}, u32[]{:S(2)}, u32[]{:S(2)}) collective-permute-start(bf16[192,384]{1,0:T(8,128)(2,1)S(1)} %inverse_z_far.3), channel_id=1, source_target_pairs={{0,258},{1,257},{64,322},{65,321},{128,386},{129,385},{192,450},{1... | collective-permute-start | bytes 442376 | tf_op jit(solution)/shard_map/ppermute | solution.py:351
  103.8 13.8 %collective-permute-start.3 = (bf16[192,384]{1,0:T(8,128)(2,1)S(1)}, bf16[192,384]{1,0:T(8,128)(2,1)S(1)}, u32[]{:S(2)}, u32[]{:S(2)}) collective-permute-start(bf16[192,384]{1,0:T(8,128)(2,1)S(1)} %get-tuple-element.12), channel_id=1, source_target_pairs={{0,1},{1,0},{2,3},{3,2},{4,5},{5,4},{6,7},{7,6},{8,9},{9,8},{10,11... | collective-permute-start | bytes 442376 | tf_op jit(solution)/shard_map/ppermute | solution.py:339
  113.6 10.1 %collective-permute-start.2 = (bf16[192,384]{1,0:T(8,128)(2,1)S(1)}, bf16[192,384]{1,0:T(8,128)(2,1)S(1)}, u32[]{:S(2)}, u32[]{:S(2)}) collective-permute-start(bf16[192,384]{1,0:T(8,128)(2,1)S(1)} %collective-permute-done.1), channel_id=1, source_target_pairs={{0,256},{1,259},{64,320},{65,323},{128,384},{129,387},{192,448},{1... | collective-permute-start | bytes 442376 | tf_op jit(solution)/shard_map/ppermute | solution.py:351
  115.5 14.3 %collective-permute-start.5 = (bf16[192,384]{1,0:T(8,128)(2,1)S(1)}, bf16[192,384]{1,0:T(8,128)(2,1)S(1)}, u32[]{:S(2)}, u32[]{:S(2)}) collective-permute-start(bf16[192,384]{1,0:T(8,128)(2,1)S(1)} %collective-permute-done.4), channel_id=1, source_target_pairs={{0,259},{1,256},{64,323},{65,320},{128,387},{129,384},{192,451},{1... | collective-permute-start | bytes 442376 | tf_op jit(solution)/shard_map/ppermute | solution.py:351
